TPU v7x, 32 devices: a whole 2x2x4 slice. The times are simulated.
32 devices in a mesh: comp: 4 (over y, x), gx: 4 (over z), gy: 2 (over core).
Axes of the slice: x: 2, y: 2, z: 4, core: 2. Of those that a mesh axis runs over, the one named last changes fastest.
Arguments:
- zonal_flow_speed: float32 [64, 64, 256], P('comp', 'gx', 'gy'), may hold values from -5 to 5
- meridional_flow_speed: float32 [64, 64, 256], P('comp', 'gx', 'gy'), may hold values from -5 to 5
- thermal_anomaly: float32 [64, 64, 256], P('comp', 'gx', 'gy'), may hold values from -6 to 6
- brine_anomaly_values: float32 [64, 64, 256], P('comp', 'gx', 'gy'), may hold values from -6 to 6
- marine_indicator: int32 [64, 256], P('gx', 'gy'), may hold values 0 or 1
- seafloor_layer: int32 [64, 256], P('gx', 'gy'), may hold values from 1 to 64
- dissolved_species: float32 [24, 64, 4, 4, 4, 256], P(None, None, 'gx', 'comp', None, 'gy'), may hold values from 0.05 to 2
- topmost_sunshine: float32 [4, 4, 4, 256], P('gx', 'comp', None, 'gy'), may hold values from 0.3 to 3
- attenuation_coefficient: float32 [24], replicated, may hold values from 0.01 to 0.1
- peak_intake_speed: float32 [24], replicated, may hold values from 0.2 to 2
- feedstock_midpoint_constant: float32 [24], replicated, may hold values from 0.05 to 1
- photon_midpoint_constant: float32 [24], replicated, may hold values from 0.05 to 1
- stoichiometry_matrix: float32 [24, 24], replicated, may hold values from -1.25 to 1.25
Outputs:
- east_new: float32 [64, 64, 256], P('comp', 'gx', 'gy')
- north_new: float32 [64, 64, 256], P('comp', 'gx', 'gy')
- warmed_result: float32 [64, 64, 256], P('comp', 'gx', 'gy')
- salt_mixed: float32 [64, 64, 256], P('comp', 'gx', 'gy')
- buoyancy: float32 [64, 64, 256], P('comp', 'gx', 'gy')
- result: float32 [24, 64, 4, 4, 4, 256], P(None, None, 'gx', 'comp', None, 'gy')
All inputs are finite; a program needn't handle non-finite values. No bound on the sum of `marine_indicator` on one device may be relied on, other than what follows from the above.
Results may differ from a plain program's by a relative error of at most 0.00007.
Values sent between devices are 32-bit elements; how exact they have to be, the bound alone decides.
No kernel may reach another device: no remote copies, remote signals or barrier semaphores. Data moves between devices by JAX's collectives and lax.ppermute only.
A program may use at most 128 MiB of HBM per device.

v0:
```python
import functools

import jax
import jax.numpy as jnp
from jax import lax
from jax.experimental import pallas as pl
from jax.experimental.pallas import tpu as pltpu
from jax.sharding import PartitionSpec as P

NSUB = 2
SLOTS = 4 * NSUB
SUB = 8
GROUP = 24
HALF = 64
ENTRIES = 18

DT_FLOW = 0.1
CORIOLIS = 0.3
MIXING = 0.15
COURANT = 0.24
DT_BIO = 0.5
WARMING_FACTOR = 0.5
CLEAR_WATER = 0.5
VMEM_LIMIT = 16 * 1024 * 1024
COVER = pl.CostEstimate(flops=0, bytes_accessed=200_000_000, transcendentals=0)
VMEM_MOST = 62 * 1024 * 1024


def lanes_of(shape):
    return lax.broadcasted_iota(jnp.int32, shape, len(shape) - 1)


def subs_of(shape):
    return lax.broadcasted_iota(jnp.int32, shape, len(shape) - 2)


def turn(x, by, axis):
    by = by % x.shape[axis]
    return x if by == 0 else pltpu.roll(x, by, axis)


def params(limit=VMEM_LIMIT):
    return pltpu.CompilerParams(vmem_limit_bytes=limit)


def whole(shape):
    return pl.BlockSpec(shape, lambda *_: (0,) * len(shape))


def smem():
    return pl.BlockSpec(memory_space=pltpu.SMEM)


def shaped(*shape):
    return jax.ShapeDtypeStruct(shape, jnp.float32)


def halves(x):
    high = x.astype(jnp.bfloat16)
    return high, (x - high.astype(jnp.float32)).astype(jnp.bfloat16)


def sums_above(x):
    sub = subs_of(x.shape)
    running, total = x, x
    by = 1
    while by < x.shape[0]:
        running = running + jnp.where(sub >= by, turn(running, by, 0), 0.0)
        total = total + turn(total, by, 0)
        by *= 2
    return jnp.where(sub >= 1, turn(running, 1, 0), 0.0), total


def cut_kernel(cuts, q_ref, *refs):
    outs, sems = refs[-2 * len(cuts) - 1 : -1], refs[-1]
    rows = q_ref.shape[2]
    copies = [
        pltpu.make_async_copy(
            q_ref.at[:, pl.ds(start, size), r],
            outs[2 * i + r // NSUB].at[:, r % NSUB],
            sems.at[rows * i + r],
        )
        for i, (start, size) in enumerate(cuts)
        for r in range(rows)
    ]
    for copy in copies:
        copy.start()
    for copy in copies:
        copy.wait()


def cut_rows(q, cuts, after):
    tracers, _, rows, _, cols = q.shape
    anywhere = pl.BlockSpec(memory_space=pl.ANY)
    outs = [shaped(tracers, NSUB, size, 1, cols) for _, size in cuts for _ in range(2)]
    outs = pl.pallas_call(
        functools.partial(cut_kernel, cuts),
        in_specs=[anywhere] * (1 + len(after)),
        out_specs=[anywhere] * len(outs),
        out_shape=outs,
        scratch_shapes=[pltpu.SemaphoreType.DMA((rows * len(cuts),))],
        compiler_params=params(),
    )(q, *after)
    return [x.reshape(tracers, NSUB, x.shape[2], cols) for x in outs]


def hold_kernel(*refs):
    pass


def held_until(arrays, after):
    anywhere = pl.BlockSpec(memory_space=pl.ANY)
    return pl.pallas_call(
        hold_kernel,
        in_specs=[anywhere] * (len(arrays) + len(after)),
        out_specs=[anywhere] * len(arrays),
        out_shape=[shaped(*x.shape) for x in arrays],
        input_output_aliases={i: i for i in range(len(arrays))},
        compiler_params=params(),
    )(*arrays, *after)


def both_ends(acc):
    return jnp.where(lanes_of(acc.shape) % SLOTS < SLOTS // 2, acc, turn(acc, SLOTS // 2, 1))


def pack_tracers_kernel(low_ref, high_ref, after_ref, before_ref, packed_ref):
    tracers, _, _, cols = low_ref.shape
    lane = lanes_of((SUB, cols))
    for pair in range(tracers // 2):
        acc = jnp.zeros((SUB, cols), jnp.float32)
        for odd in range(2):
            t = 2 * pair + odd
            rows = [before_ref[t, 1], low_ref[t, 0], low_ref[t, 1], high_ref[t, 0], high_ref[t, 1]]
            for r, x in enumerate(rows + [after_ref[t, 0]]):
                at = HALF * odd + SLOTS * (r + 1)
                acc = jnp.where(lane // SLOTS == at // SLOTS, turn(x, at + NSUB, 1), acc)
        packed_ref[pair] = both_ends(acc)


def pack_tracers(own, rim, after, cost=None):
    tracers, _, levels, cols = own[0].shape
    rows = pl.BlockSpec((tracers, NSUB, SUB, cols), lambda i: (0, 0, i, 0))
    return pl.pallas_call(
        functools.partial(ignoring, len(after), pack_tracers_kernel),
        grid=(levels // SUB,),
        in_specs=[pl.BlockSpec(memory_space=pl.ANY)] * len(after) + [rows] * 4,
        out_specs=pl.BlockSpec((tracers // 2, SUB, cols), lambda i: (0, i, 0)),
        out_shape=shaped(tracers // 2, levels, cols),
        compiler_params=params(),
        cost_estimate=cost,
    )(*after, *own, *rim)


def ignoring(count, kernel, *refs):
    kernel(*refs[count:])


def call_once(kernel, operands, outs, scratch=(), scalars=(), after=(), limit=VMEM_LIMIT):
    return pl.pallas_call(
        functools.partial(ignoring, len(after), kernel),
        grid=(1,),
        in_specs=[pl.BlockSpec(memory_space=pl.ANY)] * len(after)
        + [smem()] * len(scalars)
        + [whole(x.shape) for x in operands],
        out_specs=[whole(x.shape) for x in outs],
        out_shape=outs,
        scratch_shapes=list(scratch),
        compiler_params=params(limit),
    )(*after, *scalars, *operands)


def pack_ocean_kernel(levels, *refs):
    u_ref, v_ref, t_ref, s_ref, sea_ref, floor_ref, packed_ref, edges_ref, row_ref = refs
    edge_low_ref, edge_high_ref = edges_ref.at[0], edges_ref.at[1]
    tile_rows, cols = sea_ref.shape
    lane = lanes_of((levels, cols))
    edge_low_ref[4 * NSUB] = jnp.zeros((levels, cols), jnp.float32)
    edge_high_ref[4 * NSUB] = jnp.zeros((levels, cols), jnp.float32)
    for f, ref in enumerate((u_ref, v_ref, t_ref, s_ref)):
        acc = jnp.zeros((levels, cols), jnp.float32)
        for r in range(tile_rows):
            x = ref[pl.ds(r, levels, stride=tile_rows), :]
            row_ref[f, r] = x
            acc = jnp.where(lane // SLOTS == r, turn(x, SLOTS * r + NSUB, 1), acc)
            if r < NSUB:
                edge_low_ref[NSUB * f + r] = x
            if r >= tile_rows - NSUB:
                edge_high_ref[NSUB * f + r - tile_rows + NSUB] = x
        packed_ref[f] = both_ends(acc)
    depth = jnp.where(sea_ref[...] == 1, floor_ref[...], 0).astype(jnp.float32)
    acc = jnp.zeros((levels, cols), jnp.float32)
    for r in range(tile_rows):
        x = jnp.broadcast_to(depth[r : r + 1], (levels, cols))
        acc = jnp.where(lane // SLOTS == r, turn(x, SLOTS * r + NSUB, 1), acc)
    packed_ref[4] = both_ends(acc)
    edge_low_ref[4 * NSUB, 0:NSUB, :] = depth[0:NSUB]
    edge_high_ref[4 * NSUB, 0:NSUB, :] = depth[tile_rows - NSUB :]


def pack_ocean(flat, sea, levels):
    cols = sea[0].shape[1]
    edges = shaped(2, 4 * NSUB + 1, levels, cols)
    return call_once(
        functools.partial(pack_ocean_kernel, levels),
        [*flat, *sea],
        [shaped(5, levels, cols), edges, shaped(4, sea[0].shape[0], levels, cols)],
        limit=VMEM_MOST,
    )


def with_sides(own, left, right):
    slot = lanes_of(own.shape) % SLOTS
    ends = jnp.where(slot < NSUB, left, right)
    return jnp.where((slot < NSUB) | (slot >= SLOTS - NSUB), ends, own)


def ocean_sides_kernel(own_ref, left_ref, right_ref, edges_ref, up_ref, down_ref, out_ref):
    _, levels, cols = own_ref.shape
    rows = edges_ref.shape[1]
    up_ref[0:rows] = edges_ref[0]
    down_ref[0:rows] = edges_ref[1]
    slot = lanes_of((levels, cols)) % SLOTS
    place = lax.axis_index("gy")
    first, last = place == 0, place == lax.axis_size("gy") - 1
    for f in range(5):
        x = with_sides(own_ref[f], left_ref[f], right_ref[f])
        if f == 4:
            x = jnp.where((slot < NSUB) & first, 0.0, x)
            x = jnp.where((slot >= SLOTS - NSUB) & last, 0.0, x)
        out_ref[f] = x
        up_ref[rows + f] = x
        down_ref[rows + f] = x


def ocean_sides(own, left, right, edges):
    edge = shaped(edges.shape[1] + 5, *edges.shape[2:])
    return call_once(
        ocean_sides_kernel,
        [own, left, right, edges],
        [edge, edge, shaped(*own.shape)],
    )


def ocean_kernel(blocks, levels, *refs):
    own_ref, sea_ref, floor_ref, packed_ref, after_ref, before_ref = refs[:6]
    smix_ref, mixed_ref, send_ref, local_ref, faces_ref, depths_ref, press_ref, total_ref = refs[6:]
    tile_rows, cols = sea_ref.shape
    sub_rows = tile_rows // blocks
    shape = (levels, cols)
    lane = lanes_of(shape)
    first, last = lane == 0, lane == cols - 1
    base = lax.axis_index("comp") * levels
    level = (base + subs_of(shape)).astype(jnp.float32)
    rims = after_ref.shape[0] - 5

    def packed(f):
        after, before = after_ref[rims + f], before_ref[rims + f]
        rim = jnp.where(lane < NSUB * SLOTS, after, jnp.where(lane >= cols - NSUB * SLOTS, before, 0.0))
        return jnp.concatenate([packed_ref[f], rim], axis=1)

    def row_after(x):
        return turn(x, -SLOTS, 1)

    def row_before(x):
        return turn(x, SLOTS, 1)

    up, vp, tp, sp, dp = [packed(f) for f in range(5)]
    wide = jnp.concatenate([level, level], axis=1)
    wet = (wide < dp).astype(jnp.float32)
    heavy = wet * (-0.2 * tp + 0.8 * sp)
    above, total = sums_above(heavy)
    press = above + 0.5 * heavy
    east = up + DT_FLOW * (CORIOLIS * vp - (row_after(press) - press))
    north = vp + DT_FLOW * (-CORIOLIS * up - (turn(press, -1, 1) - press))
    open_n = wet * turn(wet, -1, 1)
    flux_t = open_n * (turn(tp, -1, 1) - tp)
    flux_s = open_n * (turn(sp, -1, 1) - sp)
    total_e, total_n = row_after(total) - total, turn(total, -1, 1) - total
    depth_e, depth_n = jnp.minimum(dp, row_after(dp)), jnp.minimum(dp, turn(dp, -1, 1))

    def window(x, g):
        x = turn(x, -SLOTS * (sub_rows * g - NSUB), 1)[:, 0:cols]
        return jnp.where(lane < HALF, x, turn(x, HALF, 1))

    for g in range(blocks):
        send_ref[g, 13] = window(east, g)
        send_ref[g, 14] = window(north, g)
        send_ref[g, 15, 13:14, :] = window(total_e, g)[0:1]
        send_ref[g, 15, 14:15, :] = window(total_n, g)[0:1]
        send_ref[g, 15, 15:16, :] = jnp.zeros((1, cols), jnp.float32)
        depths_ref[g, 24:25, :] = window(depth_e, g)[0:1]
        depths_ref[g, 25:26, :] = window(depth_n, g)[0:1]
        depths_ref[g, 26:27, :] = window(dp, g)[0:1]

    slot = lanes_of(tp.shape) % SLOTS

    def edges(x, other):
        x = jnp.where(slot == 0, turn(x, -6, 1), other)
        return x[:, 0:cols], x[:, cols:]

    edge_p, edge_w = edges(press, press), edges(wet, wet)
    edge_t, edge_s = edges(tp, flux_t), edges(sp, flux_s)
    edge_total, edge_depth = edges(total, total), edges(dp, dp)

    def edge(pair, r):
        at = r % tile_rows
        return turn(pair[0] if 0 <= r < tile_rows else pair[1], -(SLOTS * at + 1), 1)

    depth = jnp.where(sea_ref[...] == 1, floor_ref[...], 0).astype(jnp.float32)

    def row_of(f, r):
        if r < 0:
            return before_ref[NSUB * f + r + NSUB]
        if r >= tile_rows:
            return after_ref[NSUB * f + r - tile_rows]
        return own_ref[f, r]

    def depth_of(r):
        if r < 0:
            x = before_ref[4 * NSUB, r + NSUB : r + NSUB + 1, :]
        elif r >= tile_rows:
            x = after_ref[4 * NSUB, r - tile_rows : r - tile_rows + 1, :]
        else:
            x = depth[r : r + 1]
        return jnp.broadcast_to(x, shape)

    lo, hi = -NSUB, tile_rows + NSUB
    for r in range(lo, hi):
        heavy = (level < depth_of(r)).astype(jnp.float32) * (-0.2 * row_of(2, r) + 0.8 * row_of(3, r))
        above, total = sums_above(heavy)
        press_ref[r - lo] = above + 0.5 * heavy
        total_ref[r - lo] = total

    def windows(r, before):
        for g in range(blocks):
            j = r - (sub_rows * g - before)
            if 0 <= j < sub_rows + 1 + before:
                yield g, j

    flux_before = [None, None]
    for r in range(lo, hi - 1):
        press, press_e = press_ref[r - lo], press_ref[r - lo + 1]
        total, total_a = total_ref[r - lo], total_ref[r - lo + 1]
        d, d_e = depth_of(r), depth_of(r + 1)
        d_n = jnp.where(last, edge(edge_depth, r), turn(d, -1, 1))
        face_e, face_n = jnp.minimum(d, d_e), jnp.minimum(d, d_n)
        u, v = row_of(0, r), row_of(1, r)
        east = u + DT_FLOW * (CORIOLIS * v - (press_e - press))
        press_n = jnp.where(last, edge(edge_p, r), turn(press, -1, 1))
        north = v + DT_FLOW * (-CORIOLIS * u - (press_n - press))
        total_e = total_a - total
        total_n = jnp.where(last, edge(edge_total, r), turn(total, -1, 1)) - total
        for g, j in windows(r, 2):
            send_ref[g, j] = east
            send_ref[g, 15, j : j + 1, :] = total_e[0:1]
            depths_ref[g, j : j + 1, :] = face_e[0:1]
        for g, j in windows(r, 1):
            send_ref[g, 7 + j] = north
            send_ref[g, 15, 7 + j : 8 + j, :] = total_n[0:1]
            depths_ref[g, 8 + j : 9 + j, :] = face_n[0:1]
            depths_ref[g, 16 + j : 17 + j, :] = d[0:1]
        if 0 <= r < tile_rows:
            local_ref[0, r] = east
            local_ref[1, r] = north
            faces_ref[0, r : r + 1, :] = face_e[0:1]
            faces_ref[1, r : r + 1, :] = face_n[0:1]
            for g in range(blocks):
                send_ref[g, 16, r : r + 1, :] = total_e[0:1]
                send_ref[g, 17, r : r + 1, :] = total_n[0:1]
        if r < -1 or r >= tile_rows:
            continue
        open_e = (level < face_e).astype(jnp.float32)
        open_n = (level < face_n).astype(jnp.float32)
        for i, (f, ends) in enumerate(((2, edge_t), (3, edge_s))):
            x = row_of(f, r)
            flux_e = open_e * (row_of(f, r + 1) - x)
            if r >= 0:
                ending = edge(ends, r)
                flux_n = open_n * (jnp.where(last, ending, turn(x, -1, 1)) - x)
                flux_b = jnp.where(first, ending, turn(flux_n, 1, 1))
                mixed = x + MIXING * ((flux_e - flux_before[i]) + (flux_n - flux_b))
                mixed_ref[i, r] = mixed
                if i == 1:
                    smix_ref[pl.ds(r, levels, stride=tile_rows), :] = mixed
            flux_before[i] = flux_e


def ocean_phase(blocks, levels, own, sea, packed, rim_after, rim_before, after):
    tile_rows, cols = sea[0].shape
    outs = [
        shaped(levels * tile_rows, cols),
        shaped(2, tile_rows, levels, cols),
        shaped(blocks, ENTRIES, levels, cols),
        shaped(2, tile_rows, levels, cols),
        shaped(2, tile_rows, cols),
        shaped(blocks, 32, cols),
    ]
    tall = tile_rows + 2 * NSUB
    return call_once(
        functools.partial(ocean_kernel, blocks, levels),
        [own, *sea, packed, rim_after, rim_before],
        outs,
        [pltpu.VMEM((tall, levels, cols), jnp.float32)] * 2,
        after=after,
    )


def velocity_kernel(local_ref, faces_ref, received_ref, east_ref, north_ref):
    blocks = received_ref.shape[0]
    _, tile_rows, levels, cols = local_ref.shape
    group = lax.axis_index("comp")
    level = (group * levels + subs_of((levels, cols))).astype(jnp.float32)
    for f, out_ref in enumerate((east_ref, north_ref)):
        above = jnp.zeros((tile_rows, cols), jnp.float32)
        for s in range(blocks - 1):
            above = above + jnp.where(s < group, received_ref[s, f], 0.0)
        for r in range(tile_rows):
            x = local_ref[f, r] - DT_FLOW * jnp.broadcast_to(above[r : r + 1], (levels, cols))
            x = jnp.where(level < faces_ref[f, r : r + 1, :], x, 0.0)
            out_ref[pl.ds(r, levels, stride=tile_rows), :] = x


def velocities(local, faces, received):
    blocks = received.shape[0]
    _, tile_rows, levels, cols = local.shape
    out = shaped(levels * tile_rows, cols)
    return pl.pallas_call(
        velocity_kernel,
        grid=(1,),
        in_specs=[
            whole(local.shape),
            whole(faces.shape),
            pl.BlockSpec((blocks, 2, levels, cols), lambda i: (0, ENTRIES // 2 - 1, 0, 0)),
        ],
        out_specs=[whole(out.shape)] * 2,
        out_shape=[out] * 2,
        compiler_params=params(),
    )(local, faces, received)


def advection_kernel(first_part, parts, level_count, *refs):
    (
        absorb_ref,
        surface_ref,
        depth_ref,
        totals_ref,
        courant_ref,
        low_ref,
        high_ref,
        after_ref,
        before_ref,
        side_ref,
        left_ref,
        right_ref,
    ) = refs[:12]
    moved_ref, light_ref, heat_ref, carry_out_ref = refs[-10:-6]
    coef_ref, side_coef_ref, edge_ref, running_ref, above_ref, shift_ref = refs[-6:]
    depth_ref = depth_ref.at[lax.axis_index("comp")]
    step = pl.program_id(0)
    tracers, _, _, cols = low_ref.shape
    levels = courant_ref.shape[2]
    sub_rows = surface_ref.shape[0]
    rows = sub_rows + 2
    shape = (levels, cols)
    lane = lanes_of(shape)
    first, last = lane == 0, lane == cols - 1
    first8, last8 = first[0:SUB], last[0:SUB]
    slot = lane % SLOTS

    @pl.when(step == 0)
    def _():
        running_ref[...] = refs[12][...] if first_part else jnp.zeros_like(running_ref)
        size = (2 * cols, 2 * cols)
        source, to = subs_of(size) % cols, lanes_of(size)
        hit = ((to < cols) & (source == to + 1)) | ((to >= cols) & (source == to - cols - 1))
        shift_ref[...] = hit.astype(jnp.float32).astype(jnp.bfloat16)

    part = first_part + step
    above = jnp.zeros(above_ref.shape, jnp.float32)
    for s in range(totals_ref.shape[0] - 1):
        above = above + jnp.where(s < part // parts, totals_ref[s, 0], 0.0)
    above_ref[...] = above
    level = (part * levels + subs_of(shape)).astype(jnp.float32)

    def spread(ref, r):
        return jnp.broadcast_to(ref[r : r + 1, :], shape)

    def courant(entry, face):
        x = courant_ref[0, entry] - DT_FLOW * spread(above_ref, entry)
        return COURANT * jnp.tanh(jnp.where(level < spread(depth_ref, face), x, 0.0))

    def coefficients(wet, ce, ce_b, cn, cn_b):
        return (
            wet
            * (
                1.0
                - jnp.maximum(ce, 0.0)
                + jnp.minimum(ce_b, 0.0)
                - jnp.maximum(cn, 0.0)
                + jnp.minimum(cn_b, 0.0)
            ),
            -wet * jnp.minimum(ce, 0.0),
            wet * jnp.maximum(ce_b, 0.0),
            -wet * jnp.minimum(cn, 0.0),
            wet * jnp.maximum(cn_b, 0.0),
        )

    side_e, side_n = courant(13, 24), courant(14, 25)
    wet = (level < spread(depth_ref, 26)).astype(jnp.float32)
    packed_coef = coefficients(wet, side_e, turn(side_e, SLOTS, 1), side_n, turn(side_n, 1, 1))
    for i in range(5):
        side_coef_ref[i] = packed_coef[i]
    ce_b = courant(0, 0)
    for j in range(rows):
        ce, cn = courant(1 + j, 1 + j), courant(7 + j, 8 + j)
        cn_b = jnp.where(first, turn(side_n, -(SLOTS * (j + 1) + 1), 1), turn(cn, 1, 1))
        wet = (level < spread(depth_ref, 16 + j)).astype(jnp.float32)
        for i, x in enumerate(coefficients(wet, ce, ce_b, cn, cn_b)):
            coef_ref[5 * j + i] = x
        ce_b = ce
    for i in range(side_ref.shape[0]):
        x = with_sides(side_ref[i], left_ref[i], right_ref[i])
        edge_ref[i, 0] = jnp.where(slot == 0, turn(x, -6, 1), x)
        x = (
            (side_coef_ref[0] * x + side_coef_ref[1] * turn(x, -SLOTS, 1))
            + (side_coef_ref[2] * turn(x, SLOTS, 1) + side_coef_ref[3] * turn(x, -1, 1))
            + side_coef_ref[4] * turn(x, 1, 1)
        )
        edge_ref[i, 1] = jnp.where(slot == 0, turn(x, -6, 1), x)

    layer = 2.0 / level_count
    zero = jnp.zeros((SUB, cols), jnp.float32)
    for k in range(0, levels, SUB):
        at = slice(k, k + SUB)

        def shifted(tiles):
            high, low = halves(jnp.concatenate(tiles, axis=0))
            return jnp.dot(
                jnp.concatenate([high, low], axis=1),
                shift_ref[...],
                preferred_element_type=jnp.float32,
            )

        def stencil(x, coef, edge, beside):
            north = jnp.where(last8, edge, beside[:, :cols])
            south = jnp.where(first8, edge, beside[:, cols:])
            return (
                (coef[0] * x[1] + coef[1] * x[2])
                + (coef[2] * x[0] + coef[3] * north)
                + coef[4] * south
            )

        def advect(i, sums):
            sums = list(sums)
            fields = []
            for t in range(GROUP):
                t = GROUP * i + t
                rows_of = (before_ref, low_ref, high_ref, after_ref)
                x = [ref[t, n, at] for ref in rows_of for n in range(NSUB)]
                fields.append(x)
            for stage in range(NSUB):
                inner = range(1 + stage, rows + 1 - stage)
                beside = shifted([x[j - stage] for j in inner for x in fields])
                fresh = [[] for _ in fields]
                for n, j in enumerate(inner):
                    coef = [coef_ref[5 * (j - 1) + c, at] for c in range(5)]
                    for t, x in enumerate(fields):
                        edges = edge_ref[GROUP // 2 * i + t // 2, stage, at]
                        edge = turn(edges, -(HALF * (t % 2) + SLOTS * j + 1), 1)
                        row = SUB * (len(fields) * n + t)
                        fresh[t].append(
                            stencil(x[n : n + 3], coef, edge, beside[row : row + SUB])
                        )
                fields = fresh
            for t, x in enumerate(fields):
                for r in range(sub_rows):
                    moved_ref[GROUP * i + t, r, at] = x[r]
                    sums[r] = sums[r] + absorb_ref[GROUP * i + t] * x[r]
            return tuple(sums)

        sums = (zero,) * sub_rows
        for i in range(tracers // GROUP):
            sums = advect(i, sums)
        for r in range(sub_rows):
            optical = layer * (CLEAR_WATER + sums[r])
            above, total = sums_above(optical)
            through = jnp.exp(-(running_ref[r] + above))
            running_ref[r] = running_ref[r] + total
            surface = jnp.broadcast_to(surface_ref[r : r + 1, :], (SUB, cols))
            light_ref[r, at] = surface * through * jnp.exp(-0.5 * optical)
            wet = (level[at] < jnp.broadcast_to(depth_ref[17 + r : 18 + r, :], (SUB, cols))).astype(
                jnp.float32
            )
            heat_ref[0, r, at] = wet * surface * through * (1.0 - jnp.exp(-optical)) / layer
    carry_out_ref[...] = running_ref[...]


def advection(cut, level_count, absorb, surface, depth, received, own, rim, sides, carry, heat, after):
    first_part, count = cut
    tracers, _, _, cols = own[0].shape
    every, _, levels, _ = received.shape
    parts = levels // SUB
    sub_rows = surface.shape[0]
    rows = pl.BlockSpec((tracers, NSUB, SUB, cols), lambda i: (0, 0, i, 0))
    side = pl.BlockSpec((tracers // 2, SUB, cols), lambda i: (0, i, 0))
    operands = [absorb, surface, depth, received, received, *own, *rim, *sides]
    in_specs = [
        smem(),
        whole(surface.shape),
        whole(depth.shape),
        pl.BlockSpec((every, 1, levels, cols), lambda i: (0, 15, 0, 0)),
        pl.BlockSpec(
            (1, ENTRIES, SUB, cols),
            lambda i: ((first_part + i) // parts, 0, (first_part + i) % parts, 0),
        ),
        rows,
        rows,
        rows,
        rows,
        side,
        side,
        side,
    ]
    aliases = {}
    carry_shape = (sub_rows, SUB, cols)
    if carry is not None:
        operands.append(carry)
        in_specs.append(whole(carry_shape))
        aliases = {len(operands): 2}
        operands.append(heat)
    operands += after
    in_specs += [pl.BlockSpec(memory_space=pl.ANY)] * (len(operands) - len(in_specs))
    outs = [
        shaped(tracers, sub_rows, count * SUB, cols),
        shaped(sub_rows, count * SUB, cols),
        shaped(every, sub_rows, levels, cols),
        shaped(*carry_shape),
    ]
    return pl.pallas_call(
        functools.partial(advection_kernel, first_part, parts, level_count),
        grid=(count,),
        in_specs=in_specs,
        out_specs=[
            pl.BlockSpec((tracers, sub_rows, SUB, cols), lambda i: (0, 0, i, 0)),
            pl.BlockSpec((sub_rows, SUB, cols), lambda i: (0, i, 0)),
            pl.BlockSpec(
                (1, sub_rows, SUB, cols),
                lambda i: ((first_part + i) // parts, 0, (first_part + i) % parts, 0),
            ),
            whole(carry_shape),
        ],
        out_shape=outs,
        scratch_shapes=[
            pltpu.VMEM((5 * (sub_rows + 2), SUB, cols), jnp.float32),
            pltpu.VMEM((5, SUB, cols), jnp.float32),
            pltpu.VMEM((tracers // 2, 2, SUB, cols), jnp.float32),
            pltpu.VMEM((sub_rows, SUB, cols), jnp.float32),
            pltpu.VMEM((levels, cols), jnp.float32),
            pltpu.VMEM((2 * cols, 2 * cols), jnp.bfloat16),
        ],
        input_output_aliases=aliases,
        compiler_params=params(),
    )(*operands)


def spread_kernel(matrix_ref, out_ref):
    tracers = matrix_ref.shape[0]
    size = tracers * SUB
    tall = (subs_of((size, tracers)) // SUB == lanes_of((size, tracers))).astype(jnp.float32)
    wide = (lanes_of((tracers, size)) // SUB == subs_of((tracers, size))).astype(jnp.float32)
    exact = functools.partial(
        jnp.dot, precision=lax.Precision.HIGHEST, preferred_element_type=jnp.float32
    )
    same = subs_of((size, size)) % SUB == lanes_of((size, size)) % SUB
    out_ref[...] = jnp.where(same, exact(exact(tall, matrix_ref[...]), wide), 0.0)


def uptake_kernel(first_level, *refs):
    growth_ref, half_ref, dim_ref, matrix_ref, depth_ref, moved_ref, light_ref = refs[:7]
    depth_ref = depth_ref.at[lax.axis_index("comp")]
    result_ref, token_ref, uptake_ref = refs[-3:]
    token_ref[...] = jnp.zeros_like(token_ref)
    tracers, sub_rows, levels, cols = moved_ref.shape
    step = pl.program_id(0)
    matrix_high, matrix_low = halves(matrix_ref[...])
    for k in range(0, levels, SUB):
        at = slice(k, k + SUB)
        level = (first_level + step * levels + k + subs_of((SUB, cols))).astype(jnp.float32)
        light = [light_ref[r, at] for r in range(sub_rows)]
        food = [moved_ref[0, r, at] for r in range(sub_rows)]
        both = [light[r] * food[r] for r in range(sub_rows)]

        def uptake(t, _):
            for r in range(sub_rows):
                scale = (half_ref[t] + food[r]) * (light[r] + dim_ref[t])
                value = growth_ref[t] * moved_ref[t, r, at] * (both[r] / scale)
                uptake_ref[pl.ds(t * SUB, SUB), r * cols : (r + 1) * cols] = value
            return _

        lax.fori_loop(0, tracers, uptake, 0, unroll=4)
        amount = uptake_ref[...]
        high, low = halves(amount)
        dot = functools.partial(jnp.dot, preferred_element_type=jnp.float32)
        change = dot(matrix_high, high) + (dot(matrix_high, low) + dot(matrix_low, high))
        for r in range(sub_rows):
            depth = jnp.broadcast_to(depth_ref[17 + r : 18 + r, :], (SUB, cols))
            scale = DT_BIO * (level < depth).astype(jnp.float32)
            for t in range(tracers):
                result_ref[t, pl.ds(sub_rows * k + r, SUB, stride=sub_rows), :] = (
                    moved_ref[t, r, at]
                    + scale * change[SUB * t : SUB * (t + 1), r * cols : (r + 1) * cols]
                )


def uptake(cut, all_rows, scalars, matrix, depth, moved, light, result):
    first_part, count = cut
    tracers, sub_rows, _, cols = moved.shape
    operands = [*scalars, matrix, depth, moved, light]
    in_specs = [smem()] * 3 + [
        whole(matrix.shape),
        whole(depth.shape),
        pl.BlockSpec((tracers, sub_rows, SUB, cols), lambda i: (0, 0, i, 0)),
        pl.BlockSpec((sub_rows, SUB, cols), lambda i: (0, i, 0)),
    ]
    aliases = {}
    if result is not None:
        aliases = {len(operands): 0}
        operands.append(result)
        in_specs.append(pl.BlockSpec(memory_space=pl.ANY))
    return pl.pallas_call(
        functools.partial(uptake_kernel, first_part * SUB),
        grid=(count,),
        in_specs=in_specs,
        out_specs=[
            pl.BlockSpec((tracers, SUB * sub_rows, cols), lambda i: (0, first_part + i, 0)),
            whole((SUB, cols)),
        ],
        out_shape=[shaped(tracers, all_rows, cols), shaped(SUB, cols)],
        scratch_shapes=[pltpu.VMEM((tracers * SUB, sub_rows * cols), jnp.float32)],
        input_output_aliases=aliases,
        compiler_params=params(),
    )(*operands)


def warming_kernel(sea_ref, floor_ref, heat_ref, mixed_ref, warm_ref, buoyant_ref):
    blocks, sub_rows, levels, cols = heat_ref.shape
    tile_rows = blocks * sub_rows
    base = lax.axis_index("comp") * levels
    level = (base + subs_of((levels, cols))).astype(jnp.float32)
    depth = jnp.where(sea_ref[...] == 1, floor_ref[...], 0).astype(jnp.float32)
    for r in range(tile_rows):
        at = pl.ds(r, levels, stride=tile_rows)
        warm = mixed_ref[0, r] + WARMING_FACTOR * heat_ref[r // sub_rows, r % sub_rows]
        wet = (level < depth[r : r + 1]).astype(jnp.float32)
        warm_ref[at, :] = warm
        buoyant_ref[at, :] = wet * (0.2 * warm - 0.8 * mixed_ref[1, r])


def warming(heat, mixed, sea):
    _, tile_rows, levels, cols = mixed.shape
    outs = [shaped(levels * tile_rows, cols)] * 2
    return call_once(warming_kernel, [*sea, heat, mixed], outs)


def from_before(x, axis):
    return lax.ppermute(x, axis, [(i, i + 1) for i in range(lax.axis_size(axis) - 1)])


def from_after(x, axis):
    return lax.ppermute(x, axis, [(i + 1, i) for i in range(lax.axis_size(axis) - 1)])


def row_pairs():
    blocks, tiles = lax.axis_size("comp"), lax.axis_size("gx")
    places = [b * tiles + tile for tile in range(tiles) for b in range(blocks)]
    return list(zip(places[:-1], places[1:]))


def from_block_before(x):
    return lax.ppermute(x, ("comp", "gx"), row_pairs())


def from_block_after(x):
    return lax.ppermute(x, ("comp", "gx"), [(later, own) for own, later in row_pairs()])


def from_sides(x):
    if lax.axis_size("gy") == 2:
        other = lax.ppermute(x, "gy", [(0, 1), (1, 0)])
        return other, other
    return from_before(x, "gy"), from_after(x, "gy")


def on_device(
    zonal_flow_speed,
    meridional_flow_speed,
    thermal_anomaly,
    brine_anomaly_values,
    marine_indicator,
    seafloor_layer,
    dissolved_species,
    topmost_sunshine,
    attenuation_coefficient,
    peak_intake_speed,
    feedstock_midpoint_constant,
    photon_midpoint_constant,
    stoichiometry_matrix,
):
    blocks = lax.axis_size("comp")
    levels, tile_rows, tile_cols = zonal_flow_speed.shape
    tracer_count, level_count = dissolved_species.shape[:2]
    sub_rows = dissolved_species.shape[4]
    ocean = (zonal_flow_speed, meridional_flow_speed, thermal_anomaly, brine_anomaly_values)
    sea = (marine_indicator, seafloor_layer)
    flat = [x.reshape(levels * tile_rows, tile_cols) for x in ocean]
    q = dissolved_species.reshape(tracer_count, level_count, sub_rows, 1, tile_cols)
    parts = levels // SUB
    every = parts * blocks
    sizes = [every - 5 * every // 8, 3 * every // 8, every // 4]
    cuts = [(sum(sizes[:i]), size) for i, size in enumerate(sizes)]
    matrix = call_once(
        spread_kernel,
        [stoichiometry_matrix],
        [shaped(SUB * tracer_count, SUB * tracer_count)],
    )[0]
    scalars_of_uptake = (
        peak_intake_speed,
        feedstock_midpoint_constant,
        photon_midpoint_constant,
    )

    def rims(own):
        return own, (from_block_after(own[0]), from_block_before(own[1]))

    def sides(x):
        return (x, *from_sides(x))

    packed, edges, ocean_rows = pack_ocean(flat, sea, levels)
    ranges = [(first * SUB, size * SUB) for first, size in cuts]
    chunks = [rims(cut_rows(q, ranges[:1], [packed]))]
    later = cut_rows(q, ranges[1:], chunks[0][0][:1])
    up, down, packed = ocean_sides(packed, *from_sides(packed), edges)
    after, before = from_after(up, "gx"), from_before(down, "gx")
    smix, mixed, send, local, faces, depths = ocean_phase(
        blocks, levels, ocean_rows, sea, packed, after, before, later[:1]
    )
    received = lax.all_to_all(send, "comp", split_axis=0, concat_axis=0, tiled=True)
    east_new, north_new = velocities(local, faces, received)
    own = pack_tracers(*chunks[0], [depths], COVER)
    chunks.append(rims(held_until(later[:2], [own])))

    surface = topmost_sunshine.reshape(sub_rows, tile_cols)
    carry, heat, result = None, None, None
    near = sides(own)
    for i, cut in enumerate(cuts):
        moved, light, heat, carry = advection(
            cut,
            level_count,
            attenuation_coefficient,
            surface,
            depths,
            received,
            *chunks[i],
            near,
            carry,
            heat,
            [] if i == 0 else [token],
        )
        if i == 0:
            chunks.append(rims(held_until(later[2:], [carry])))
        if i + 1 < len(cuts):
            near = sides(pack_tracers(*chunks[i + 1], [carry]))
        result, token = uptake(
            cut,
            level_count * sub_rows,
            scalars_of_uptake,
            matrix,
            depths,
            moved,
            light,
            result,
        )
    heat = lax.all_to_all(heat, "comp", split_axis=0, concat_axis=0, tiled=True)
    warmed_result, buoyancy = warming(heat, mixed, sea)
    fields = (east_new, north_new, warmed_result, smix, buoyancy)
    return (
        *[x.reshape(zonal_flow_speed.shape) for x in fields],
        result.reshape(dissolved_species.shape),
    )


def solution(mesh):
    return jax.shard_map(
        on_device,
        mesh=mesh,
        in_specs=(
            P("comp", "gx", "gy"),
            P("comp", "gx", "gy"),
            P("comp", "gx", "gy"),
            P("comp", "gx", "gy"),
            P("gx", "gy"),
            P("gx", "gy"),
            P(None, None, "gx", "comp", None, "gy"),
            P("gx", "comp", None, "gy"),
            P(),
            P(),
            P(),
            P(),
            P(),
        ),
        out_specs=(
            P("comp", "gx", "gy"),
            P("comp", "gx", "gy"),
            P("comp", "gx", "gy"),
            P("comp", "gx", "gy"),
            P("comp", "gx", "gy"),
            P(None, None, "gx", "comp", None, "gy"),
        ),
        check_vma=False,
    )
```

profile of v0, /device:TPU:0, one launch (start us, length us, event | category | flops | bytes accessed | tf_op | source)
XLA Modules:
  0.0 112.8 jit_solution(17396994402948906801)
XLA Ops:
  0.7 2.1 %shard_map.172 = (f32[5,16,128]{2,1,0:T(8,128)}, f32[2,9,16,128]{3,2,1,0:T(8,128)}, f32[4,16,16,128]{3,2,1,0:T(8,128)}) custom-call(f32[256,128]{1,0:T(8,128)} %bitcast.35, f32[256,128]{1,0:T(8,128)} %bitcast.36, f32[256,128]{1,0:T(8,128)} %bitcast.37, f32[256,128]{1,0:T(8,128)} %bitcast.38, s32[16,128]{1,0:T(8,128)} %refs_0_.14, s32[16,128]{1,0:T(8,128)} %refs_1_.6), custom_call_target="tpu_custom_call" | custom-call | tf_op jit(solution)/shard_map/pallas_call | solution.py:160
  2.8 1.9 %copy-done = f32[24,64,1,1,4,128]{5,4,3,2,1,0:T(4,128)S(1)} copy-done((f32[24,64,1,1,4,128]{5,4,3,2,1,0:T(4,128)S(1)}, f32[24,64,1,1,4,128]{5,4,3,2,1,0:T(4,128)}, u32[]{:S(2)}) %copy-start) | copy-done | bytes 3145752
  4.7 0.8 copy-done.8
  5.4 1.2 %shard_map.173 = (f32[24,2,24,1,128]{4,3,2,1,0:T(1,128)S(1)}, f32[24,2,24,1,128]{4,3,2,1,0:T(1,128)}) custom-call(f32[24,64,4,1,128]{4,3,2,1,0:T(1,128)S(1)} %bitcast.20, f32[5,16,128]{2,1,0:T(8,128)S(1)} %copy-done.8), custom_call_target="tpu_custom_call" | custom-call | tf_op jit(solution)/shard_map/pallas_call | solution.py:96
  6.7 1.4 %collective-permute-start.3 = (f32[24,2,24,128]{3,2,1,0:T(8,128)S(1)}, f32[24,2,24,128]{3,2,1,0:T(8,128)}, u32[]{:S(2)}, u32[]{:S(2)}) collective-permute-start(f32[24,2,24,128]{3,2,1,0:T(8,128)S(1)} %bitcast.25), channel_id=1, source_target_pairs={{8,0},{16,8},{24,16},{2,24},{10,2},{18,10},{26,18},{4,26},{12,4},{... | collective-permute-start | bytes 1769480 | tf_op jit(solution)/shard_map/ppermute | solution.py:785
  8.1 6.3 %collective-permute-start.4 = (f32[24,2,24,128]{3,2,1,0:T(8,128)}, f32[24,2,24,128]{3,2,1,0:T(8,128)}, u32[]{:S(2)}, u32[]{:S(2)}) collective-permute-start(f32[24,2,24,128]{3,2,1,0:T(8,128)} %bitcast.12.refs_2_.refs_6_), channel_id=1, source_target_pairs={{0,8},{8,16},{16,24},{24,2},{2,10},{10,18},{18,26},{26,4},{4,12},{... | collective-permute-start | bytes 1769480 | tf_op jit(solution)/shard_map/ppermute | solution.py:781
  14.5 0.0 collective-permute-start
  14.5 1.2 %collective-permute-done.refs_1_.refs_2_ = f32[5,16,128]{2,1,0:T(8,128)S(1)} collective-permute-done((f32[5,16,128]{2,1,0:T(8,128)S(1)}, f32[5,16,128]{2,1,0:T(8,128)S(1)}, u32[]{:S(2)}, u32[]{:S(2)}) %collective-permute-start) | collective-permute-done | bytes 40992 | tf_op jit(solution)/shard_map/ppermute | solution.py:790
  15.7 0.9 copy-done.9
  16.6 1.3 %collective-permute-start.1 = (f32[14,16,128]{2,1,0:T(8,128)S(1)}, f32[14,16,128]{2,1,0:T(8,128)S(1)}, u32[]{:S(2)}, u32[]{:S(2)}) collective-permute-start(f32[14,16,128]{2,1,0:T(8,128)S(1)} %get-tuple-element.54), channel_id=1, source_target_pairs={{2,0},{4,2},{6,4},{3,1},{5,3},{7,5},{10,8},{12,10},{14,12},{11,9},... | collective-permute-start | bytes 344072 | tf_op jit(solution)/shard_map/ppermute | solution.py:771
  17.9 4.6 %collective-permute-start.2 = (f32[14,16,128]{2,1,0:T(8,128)S(1)}, f32[14,16,128]{2,1,0:T(8,128)S(1)}, u32[]{:S(2)}, u32[]{:S(2)}) collective-permute-start(f32[14,16,128]{2,1,0:T(8,128)S(1)} %get-tuple-element.55), channel_id=1, source_target_pairs={{0,2},{2,4},{4,6},{1,3},{3,5},{5,7},{8,10},{10,12},{12,14},{9,11},... | collective-permute-start | bytes 344072 | tf_op jit(solution)/shard_map/ppermute | solution.py:767
  22.5 1.4 %shard_map.174 = (f32[24,2,24,1,128]{4,3,2,1,0:T(1,128)S(1)}, f32[24,2,24,1,128]{4,3,2,1,0:T(1,128)S(1)}, f32[24,2,16,1,128]{4,3,2,1,0:T(1,128)S(1)}, f32[24,2,16,1,128]{4,3,2,1,0:T(1,128)S(1)}) custom-call(f32[24,64,4,1,128]{4,3,2,1,0:T(1,128)S(1)} %bitcast.21, f32[24,2,24,128]{3,2,1,0:T(8,128)S(1)} %bitcast.26), custom_call_target="tpu_custom_call" | custom-call | tf_op jit(solution)/shard_map/pallas_call | solution.py:96
  23.9 5.7 %collective-permute-done.1.refs_5_ = f32[14,16,128]{2,1,0:T(8,128)S(1)} collective-permute-done((f32[14,16,128]{2,1,0:T(8,128)S(1)}, f32[14,16,128]{2,1,0:T(8,128)S(1)}, u32[]{:S(2)}, u32[]{:S(2)}) %collective-permute-start.1) | collective-permute-done | bytes 114720 | tf_op jit(solution)/shard_map/ppermute | solution.py:771
  29.6 0.0 collective-permute-done.2.refs_6_
  29.7 0.0 copy-start.12
  29.7 0.0 copy-start.14
  29.7 3.2 %shard_map.176 = (f32[256,128]{1,0:T(8,128)}, f32[2,16,16,128]{3,2,1,0:T(8,128)S(1)}, f32[4,18,16,128]{3,2,1,0:T(8,128)S(1)}, f32[2,16,16,128]{3,2,1,0:T(8,128)S...) custom-call(f32[24,2,24,128]{3,2,1,0:T(8,128)S(1)} %bitcast.22, f32[4,16,16,128]{3,2,1,0:T(8,128)S(1)} %copy-done.3, ...), custom_call_target="tpu_custom_call" | custom-call | tf_op jit(solution)/shard_map/pallas_call | solution.py:160
  32.9 0.8 copy-done.2
  33.7 0.7 copy-done.4
  34.4 0.7 copy-done.6
  35.1 5.0 %all-to-all-start = ((f32[4,18,16,128]{3,2,1,0:T(8,128)}), f32[4,18,16,128]{3,2,1,0:T(8,128)S(1)}, u32[]{:S(2)}, u32[]{:S(2)}) async-start(f32[4,18,16,128]{3,2,1,0:T(8,128)} %copy-done.2), calls=%async_computation | async-start | bytes 1179648 | tf_op jit(solution)/shard_map/all_to_all | solution.py:848
  40.1 0.0 collective-permute-done.3.refs_3_.refs_7_
  40.1 0.0 collective-permute-done.4.refs_4_.refs_8_
  40.1 3.1 %shard_map.178.refs_9_.refs_2_ = f32[12,24,128]{2,1,0:T(8,128)S(1)} custom-call(f32[4,32,128]{2,1,0:T(8,128)S(1)} %get-tuple-element.61.refs_0_.refs_2_.refs_4_, f32[24,2,24,128]{3,2,1,0:T(8,128)S(1)} %bitcast.27, f32[24,2,24,128]{3,2,1,0:T(8,128)} %bitcast.12.refs_2_.refs_6_, f32[24,2,24,128]{3,2,1,0:T(8,128)} %collective-permute-done.3.refs_3_.refs_7_, ...), custom_call_target="tpu_custom_call" | custom-call | bytes 200000000 | tf_op jit(solution)/shard_map/pallas_call | solution.py:144
  43.2 1.3 %collective-permute-start.8 = (f32[24,2,24,128]{3,2,1,0:T(8,128)S(1)}, f32[24,2,24,128]{3,2,1,0:T(8,128)}, u32[]{:S(2)}, u32[]{:S(2)}) collective-permute-start(f32[24,2,24,128]{3,2,1,0:T(8,128)S(1)} %get-tuple-element.69.refs_1_.refs_5_), channel_id=1, source_target_pairs={{8,0},{16,8},{24,16},{2,24},{10,2},{18,10},{26,18},{4,26},{12,4},{... | collective-permute-start | bytes 1769480 | tf_op jit(solution)/shard_map/ppermute | solution.py:785
  44.5 5.4 %collective-permute-start.9 = (f32[24,2,24,128]{3,2,1,0:T(8,128)S(1)}, f32[24,2,24,128]{3,2,1,0:T(8,128)}, u32[]{:S(2)}, u32[]{:S(2)}) collective-permute-start(f32[24,2,24,128]{3,2,1,0:T(8,128)S(1)} %get-tuple-element.70.refs_2_.refs_6_), channel_id=1, source_target_pairs={{0,8},{8,16},{16,24},{24,2},{2,10},{10,18},{18,26},{26,4},{4,12},{... | collective-permute-start | bytes 1769480 | tf_op jit(solution)/shard_map/ppermute | solution.py:781
  49.9 1.4 %collective-permute-done.5.refs_10_.refs_11_ = f32[12,24,128]{2,1,0:T(8,128)S(1)} collective-permute-done((f32[12,24,128]{2,1,0:T(8,128)S(1)}, f32[12,24,128]{2,1,0:T(8,128)S(1)}, u32[]{:S(2)}, u32[]{:S(2)}) %collective-permute-start.5) | collective-permute-done | bytes 147488 | tf_op jit(solution)/shard_map/ppermute | solution.py:790
  51.3 0.0 copy-start.16
  51.3 0.0 copy-start.17
  51.3 6.1 %shard_map.179 = (f32[24,4,24,128]{3,2,1,0:T(8,128)S(1)}, f32[4,24,128]{2,1,0:T(8,128)S(1)}, f32[4,4,16,128]{3,2,1,0:T(8,128)}, f32[4,8,128]{2,1,0:T(8,128)S(1)}) custom-call(f32[24]{0:T(128)S(1)} %copy-done.14, f32[4,128]{1,0:T(4,128)S(1)} %bitcast.31, f32[4,32,128]{2,1,0:T(8,128)S(1)} %get-tuple-element.61.refs_0_.refs_2_.refs_4_, ...), custom_call_target="tpu_custom_call" | custom-call | tf_op jit(solution)/shard_map/pallas_call | solution.py:640
  57.4 1.3 %collective-permute-start.6 = (f32[24,2,16,128]{3,2,1,0:T(8,128)S(1)}, f32[24,2,16,128]{3,2,1,0:T(8,128)S(1)}, u32[]{:S(2)}, u32[]{:S(2)}) collective-permute-start(f32[24,2,16,128]{3,2,1,0:T(8,128)S(1)} %get-tuple-element.66.refs_1_.refs_5_), channel_id=1, source_target_pairs={{8,0},{16,8},{24,16},{2,24},{10,2},{18,10},{26,18},{4,26},{12,4},{... | collective-permute-start | bytes 1179656 | tf_op jit(solution)/shard_map/ppermute | solution.py:785
  58.7 4.7 %collective-permute-start.7 = (f32[24,2,16,128]{3,2,1,0:T(8,128)S(1)}, f32[24,2,16,128]{3,2,1,0:T(8,128)S(1)}, u32[]{:S(2)}, u32[]{:S(2)}) collective-permute-start(f32[24,2,16,128]{3,2,1,0:T(8,128)S(1)} %get-tuple-element.67.refs_2_.refs_6_), channel_id=1, source_target_pairs={{0,8},{8,16},{16,24},{24,2},{2,10},{10,18},{18,26},{26,4},{4,12},{... | collective-permute-start | bytes 1179656 | tf_op jit(solution)/shard_map/ppermute | solution.py:781
  63.4 17.5 %collective-permute-done.9.refs_4_.refs_8_ = f32[24,2,24,128]{3,2,1,0:T(8,128)} collective-permute-done((f32[24,2,24,128]{3,2,1,0:T(8,128)S(1)}, f32[24,2,24,128]{3,2,1,0:T(8,128)}, u32[]{:S(2)}, u32[]{:S(2)}) %collective-permute-start.9) | collective-permute-done | bytes 589856 | tf_op jit(solution)/shard_map/ppermute | solution.py:781
  81.0 2.9 %shard_map.182.refs_9_ = f32[12,24,128]{2,1,0:T(8,128)S(1)} custom-call(f32[4,8,128]{2,1,0:T(8,128)S(1)} %get-tuple-element.65.refs_2_.refs_0_.refs_12_, f32[24,2,24,128]{3,2,1,0:T(8,128)S(1)} %get-tuple-element.69.refs_1_.refs_5_, f32[24,2,24,128]{3,2,1,0:T(8,128)S(1)} %get-tuple-element.70.refs_2_.refs_6_, ...), custom_call_target="tpu_custom_call" | custom-call | tf_op jit(solution)/shard_map/pallas_call | solution.py:144
  83.9 0.1 collective-permute-start.10
  84.0 0.6 shard_map.183.refs_3_
  84.7 3.3 %shard_map.184 = (f32[24,256,128]{2,1,0:T(8,128)}, f32[8,128]{1,0:T(8,128)S(1)}) custom-call(f32[24]{0:T(128)S(1)} %copy-done.15, f32[24]{0:T(128)S(1)} %copy-done.16, f32[24]{0:T(128)S(1)} %copy-done.17, f32[192,192]{1,0:T(8,128)S(1)} %shard_map.183.refs_3_, f32[4,32,128]{2,1,0:T(8,128)S(1)} %get-tuple-element.61.refs_0_.refs_2_.refs_4_, ...), custom_call_target="tpu_custom_call" | custom-call | tf_op jit(solution)/shard_map/pallas_call | solution.py:731
  87.9 0.0 collective-permute-done.10.refs_10_.refs_11_
  87.9 6.1 %shard_map.185 = (f32[24,4,24,128]{3,2,1,0:T(8,128)S(1)}, f32[4,24,128]{2,1,0:T(8,128)S(1)}, f32[4,4,16,128]{3,2,1,0:T(8,128)}, f32[4,8,128]{2,1,0:T(8,128)S(1)}) custom-call(f32[24]{0:T(128)S(1)} %copy-done.14, f32[4,128]{1,0:T(4,128)S(1)} %bitcast.32, ...), custom_call_target="tpu_custom_call", output_to_operand_aliasing={{2}: (13, {})} | custom-call | tf_op jit(solution)/shard_map/pallas_call | solution.py:640
  94.0 1.0 shard_map.186.refs_9_
  95.0 0.6 collective-permute-start.11
  95.5 3.2 %shard_map.187 = (f32[24,256,128]{2,1,0:T(8,128)}, f32[8,128]{1,0:T(8,128)S(1)}) custom-call(f32[24]{0:T(128)S(1)} %copy-done.15, f32[24]{0:T(128)S(1)} %copy-done.16, f32[24]{0:T(128)S(1)} %copy-done.17, f32[192,192]{1,0:T(8,128)S(1)} %shard_map.183.refs_3_, ...), custom_call_target="tpu_custom_call", output_to_operand_aliasing={{0}: (7, {})} | custom-call | tf_op jit(solution)/shard_map/pallas_call | solution.py:731
  98.8 4.2 %shard_map.188 = (f32[24,4,16,128]{3,2,1,0:T(8,128)S(1)}, f32[4,16,128]{2,1,0:T(8,128)S(1)}, f32[4,4,16,128]{3,2,1,0:T(8,128)}, f32[4,8,128]{2,1,0:T(8,128)}) custom-call(f32[24]{0:T(128)S(1)} %copy-done.14, f32[4,128]{1,0:T(4,128)S(1)} %bitcast.33, f32[4,32,128]{2,1,0:T(8,128)S(1)} %get-tuple-element.61.refs_0_.refs_2_.refs_4_, ...), custom_call_target="tpu_custom_call", output_to_operand_aliasing={{2}: (13, {})} | custom-call | tf_op jit(solution)/shard_map/pallas_call | solution.py:640
  102.9 4.0 %all-to-all-start.1 = ((f32[4,4,16,128]{3,2,1,0:T(8,128)}), f32[4,4,16,128]{3,2,1,0:T(8,128)S(1)}, u32[]{:S(2)}, u32[]{:S(2)}) async-start(f32[4,4,16,128]{3,2,1,0:T(8,128)} %get-tuple-element.81), calls=%async_computation.1 | async-start | bytes 262144 | tf_op jit(solution)/shard_map/all_to_all | solution.py:884
  106.9 0.8 shard_map.177
  107.7 2.5 %shard_map.190 = (f32[24,256,128]{2,1,0:T(8,128)}, f32[8,128]{1,0:T(8,128)}) custom-call(f32[24]{0:T(128)S(1)} %copy-done.15, f32[24]{0:T(128)S(1)} %copy-done.16, f32[24]{0:T(128)S(1)} %copy-done.18, f32[192,192]{1,0:T(8,128)S(1)} %shard_map.183.refs_3_, ...), custom_call_target="tpu_custom_call", output_to_operand_aliasing={{0}: (7, {})} | custom-call | tf_op jit(solution)/shard_map/pallas_call | solution.py:731
  110.2 1.7 %all-to-all-done.1.refs_2_ = f32[4,4,16,128]{3,2,1,0:T(8,128)S(1)} async-done(((f32[4,4,16,128]{3,2,1,0:T(8,128)}), f32[4,4,16,128]{3,2,1,0:T(8,128)S(1)}, u32[]{:S(2)}, u32[]{:S(2)}) %all-to-all-start.1) | async-done | bytes 131104 | tf_op jit(solution)/shard_map/all_to_all | solution.py:884
  112.0 0.8 shard_map.189
  (37 shorter events, 0.1 us)
Async XLA Ops:
  0.6 29.0 %copy-start.10 = (s32[16,128]{1,0:T(8,128)S(1)}, s32[16,128]{1,0:T(8,128)}, u32[]{:S(2)}) copy-start(s32[16,128]{1,0:T(8,128)} %refs_0_.14) | copy-start | bytes 24580
  0.6 29.0 %copy-start.11 = (s32[16,128]{1,0:T(8,128)S(1)}, s32[16,128]{1,0:T(8,128)}, u32[]{:S(2)}) copy-start(s32[16,128]{1,0:T(8,128)} %refs_1_.6) | copy-start | bytes 24580
  2.8 1.9 %copy-start = (f32[24,64,1,1,4,128]{5,4,3,2,1,0:T(4,128)S(1)}, f32[24,64,1,1,4,128]{5,4,3,2,1,0:T(4,128)}, u32[]{:S(2)}) copy-start(f32[24,64,1,1,4,128]{5,4,3,2,1,0:T(4,128)} %param.19) | copy-start | bytes 9437188
  4.7 0.8 copy-start.8
  5.4 17.0 %copy-start.1 = (f32[24,64,1,1,4,128]{5,4,3,2,1,0:T(4,128)S(1)}, f32[24,64,1,1,4,128]{5,4,3,2,1,0:T(4,128)}, u32[]{:S(2)}) copy-start(f32[24,64,1,1,4,128]{5,4,3,2,1,0:T(4,128)} %param.19) | copy-start | bytes 9437188
  5.4 24.2 %copy-start.3 = (f32[4,16,16,128]{3,2,1,0:T(8,128)S(1)}, f32[4,16,16,128]{3,2,1,0:T(8,128)}, u32[]{:S(2)}) copy-start(f32[4,16,16,128]{3,2,1,0:T(8,128)} %get-tuple-element.51.refs_1_) | copy-start | bytes 1572868
  6.7 33.4 %collective-permute-start.3 = (f32[24,2,24,128]{3,2,1,0:T(8,128)S(1)}, f32[24,2,24,128]{3,2,1,0:T(8,128)}, u32[]{:S(2)}, u32[]{:S(2)}) collective-permute-start(f32[24,2,24,128]{3,2,1,0:T(8,128)S(1)} %bitcast.25), channel_id=1, source_target_pairs={{8,0},{16,8},{24,16},{2,24},{10,2},{18,10},{26,18},{4,26},{12,4},{... | collective-permute-start | bytes 1769480 | tf_op jit(solution)/shard_map/ppermute | solution.py:785
  8.1 31.9 %collective-permute-start.4 = (f32[24,2,24,128]{3,2,1,0:T(8,128)}, f32[24,2,24,128]{3,2,1,0:T(8,128)}, u32[]{:S(2)}, u32[]{:S(2)}) collective-permute-start(f32[24,2,24,128]{3,2,1,0:T(8,128)} %bitcast.12.refs_2_.refs_6_), channel_id=1, source_target_pairs={{0,8},{8,16},{16,24},{24,2},{2,10},{10,18},{18,26},{26,4},{4,12},{... | collective-permute-start | bytes 1769480 | tf_op jit(solution)/shard_map/ppermute | solution.py:781
  14.5 1.2 %collective-permute-start = (f32[5,16,128]{2,1,0:T(8,128)S(1)}, f32[5,16,128]{2,1,0:T(8,128)S(1)}, u32[]{:S(2)}, u32[]{:S(2)}) collective-permute-start(f32[5,16,128]{2,1,0:T(8,128)S(1)} %copy-done.8), channel_id=1, source_target_pairs={{0,1},{1,0},{2,3},{3,2},{4,5},{5,4},{6,7},{7,6},{8,9},{9,8},{10,11... | collective-permute-start | bytes 122888 | tf_op jit(solution)/shard_map/ppermute | solution.py:790
  15.7 0.9 copy-start.9
  16.6 13.0 %collective-permute-start.1 = (f32[14,16,128]{2,1,0:T(8,128)S(1)}, f32[14,16,128]{2,1,0:T(8,128)S(1)}, u32[]{:S(2)}, u32[]{:S(2)}) collective-permute-start(f32[14,16,128]{2,1,0:T(8,128)S(1)} %get-tuple-element.54), channel_id=1, source_target_pairs={{2,0},{4,2},{6,4},{3,1},{5,3},{7,5},{10,8},{12,10},{14,12},{11,9},... | collective-permute-start | bytes 344072 | tf_op jit(solution)/shard_map/ppermute | solution.py:771
  17.9 11.7 %collective-permute-start.2 = (f32[14,16,128]{2,1,0:T(8,128)S(1)}, f32[14,16,128]{2,1,0:T(8,128)S(1)}, u32[]{:S(2)}, u32[]{:S(2)}) collective-permute-start(f32[14,16,128]{2,1,0:T(8,128)S(1)} %get-tuple-element.55), channel_id=1, source_target_pairs={{0,2},{2,4},{4,6},{1,3},{3,5},{5,7},{8,10},{10,12},{12,14},{9,11},... | collective-permute-start | bytes 344072 | tf_op jit(solution)/shard_map/ppermute | solution.py:767
  29.7 21.6 %copy-start.12 = (f32[1,1,4,128]{3,2,1,0:T(4,128)S(1)}, f32[1,1,4,128]{3,2,1,0:T(4,128)}, u32[]{:S(2)}) copy-start(f32[1,1,4,128]{3,2,1,0:T(4,128)} %param.20) | copy-start | bytes 6148
  29.7 21.6 %copy-start.14 = (f32[24]{0:T(128)S(1)}, f32[24]{0:T(128)}, u32[]{:S(2)}) copy-start(f32[24]{0:T(128)} %refs_0_.13) | copy-start | bytes 292
  32.8 0.8 copy-start.2
  33.7 0.7 copy-start.4
  34.4 0.7 copy-start.6
  35.1 14.8 %all-to-all-start = ((f32[4,18,16,128]{3,2,1,0:T(8,128)}), f32[4,18,16,128]{3,2,1,0:T(8,128)S(1)}, u32[]{:S(2)}, u32[]{:S(2)}) async-start(f32[4,18,16,128]{3,2,1,0:T(8,128)} %copy-done.2), calls=%async_computation | async-start | bytes 1179648 | tf_op jit(solution)/shard_map/all_to_all | solution.py:848
  43.2 20.2 %collective-permute-start.8 = (f32[24,2,24,128]{3,2,1,0:T(8,128)S(1)}, f32[24,2,24,128]{3,2,1,0:T(8,128)}, u32[]{:S(2)}, u32[]{:S(2)}) collective-permute-start(f32[24,2,24,128]{3,2,1,0:T(8,128)S(1)} %get-tuple-element.69.refs_1_.refs_5_), channel_id=1, source_target_pairs={{8,0},{16,8},{24,16},{2,24},{10,2},{18,10},{26,18},{4,26},{12,4},{... | collective-permute-start | bytes 1769480 | tf_op jit(solution)/shard_map/ppermute | solution.py:785
  44.5 36.4 %collective-permute-start.9 = (f32[24,2,24,128]{3,2,1,0:T(8,128)S(1)}, f32[24,2,24,128]{3,2,1,0:T(8,128)}, u32[]{:S(2)}, u32[]{:S(2)}) collective-permute-start(f32[24,2,24,128]{3,2,1,0:T(8,128)S(1)} %get-tuple-element.70.refs_2_.refs_6_), channel_id=1, source_target_pairs={{0,8},{8,16},{16,24},{24,2},{2,10},{10,18},{18,26},{26,4},{4,12},{... | collective-permute-start | bytes 1769480 | tf_op jit(solution)/shard_map/ppermute | solution.py:781
  49.9 1.4 %collective-permute-start.5 = (f32[12,24,128]{2,1,0:T(8,128)S(1)}, f32[12,24,128]{2,1,0:T(8,128)S(1)}, u32[]{:S(2)}, u32[]{:S(2)}) collective-permute-start(f32[12,24,128]{2,1,0:T(8,128)S(1)} %shard_map.178.refs_9_.refs_2_), channel_id=1, source_target_pairs={{0,1},{1,0},{2,3},{3,2},{4,5},{5,4},{6,7},{7,6},{8,9},{9,8},{10,11... | collective-permute-start | bytes 442376 | tf_op jit(solution)/shard_map/ppermute | solution.py:790
  51.3 32.7 %copy-start.13 = (f32[24,24]{1,0:T(8,128)S(1)}, f32[24,24]{1,0:T(8,128)}, u32[]{:S(2)}) copy-start(f32[24,24]{1,0:T(8,128)} %refs_0_.9) | copy-start | bytes 6916
  51.3 33.4 %copy-start.15 = (f32[24]{0:T(128)S(1)}, f32[24]{0:T(128)}, u32[]{:S(2)}) copy-start(f32[24]{0:T(128)} %refs_0_.15) | copy-start | bytes 292
  51.3 33.4 %copy-start.16 = (f32[24]{0:T(128)S(1)}, f32[24]{0:T(128)}, u32[]{:S(2)}) copy-start(f32[24]{0:T(128)} %refs_1_.7) | copy-start | bytes 292
  51.3 33.4 %copy-start.17 = (f32[24]{0:T(128)S(1)}, f32[24]{0:T(128)}, u32[]{:S(2)}) copy-start(f32[24]{0:T(128)} %refs_2_.7) | copy-start | bytes 292
  57.4 36.6 %collective-permute-start.6 = (f32[24,2,16,128]{3,2,1,0:T(8,128)S(1)}, f32[24,2,16,128]{3,2,1,0:T(8,128)S(1)}, u32[]{:S(2)}, u32[]{:S(2)}) collective-permute-start(f32[24,2,16,128]{3,2,1,0:T(8,128)S(1)} %get-tuple-element.66.refs_1_.refs_5_), channel_id=1, source_target_pairs={{8,0},{16,8},{24,16},{2,24},{10,2},{18,10},{26,18},{4,26},{12,4},{... | collective-permute-start | bytes 1179656 | tf_op jit(solution)/shard_map/ppermute | solution.py:785
  58.7 35.3 %collective-permute-start.7 = (f32[24,2,16,128]{3,2,1,0:T(8,128)S(1)}, f32[24,2,16,128]{3,2,1,0:T(8,128)S(1)}, u32[]{:S(2)}, u32[]{:S(2)}) collective-permute-start(f32[24,2,16,128]{3,2,1,0:T(8,128)S(1)} %get-tuple-element.67.refs_2_.refs_6_), channel_id=1, source_target_pairs={{0,8},{8,16},{16,24},{24,2},{2,10},{10,18},{18,26},{26,4},{4,12},{... | collective-permute-start | bytes 1179656 | tf_op jit(solution)/shard_map/ppermute | solution.py:781
  83.9 4.0 %collective-permute-start.10 = (f32[12,24,128]{2,1,0:T(8,128)S(1)}, f32[12,24,128]{2,1,0:T(8,128)S(1)}, u32[]{:S(2)}, u32[]{:S(2)}) collective-permute-start(f32[12,24,128]{2,1,0:T(8,128)S(1)} %shard_map.182.refs_9_), channel_id=1, source_target_pairs={{0,1},{1,0},{2,3},{3,2},{4,5},{5,4},{6,7},{7,6},{8,9},{9,8},{10,11... | collective-permute-start | bytes 442376 | tf_op jit(solution)/shard_map/ppermute | solution.py:790
  95.0 3.8 %collective-permute-start.11 = (f32[12,16,128]{2,1,0:T(8,128)S(1)}, f32[12,16,128]{2,1,0:T(8,128)S(1)}, u32[]{:S(2)}, u32[]{:S(2)}) collective-permute-start(f32[12,16,128]{2,1,0:T(8,128)S(1)} %shard_map.186.refs_9_), channel_id=1, source_target_pairs={{0,1},{1,0},{2,3},{3,2},{4,5},{5,4},{6,7},{7,6},{8,9},{9,8},{10,11... | collective-permute-start | bytes 294920 | tf_op jit(solution)/shard_map/ppermute | solution.py:790
  95.5 11.4 %copy-start.7 = (f32[2,16,16,128]{3,2,1,0:T(8,128)S(1)}, f32[2,16,16,128]{3,2,1,0:T(8,128)}, u32[]{:S(2)}) copy-start(f32[2,16,16,128]{3,2,1,0:T(8,128)} %copy-done.6) | copy-start | bytes 786436
  98.8 8.9 %copy-start.18 = (f32[24]{0:T(128)S(1)}, f32[24]{0:T(128)}, u32[]{:S(2)}) copy-start(f32[24]{0:T(128)} %refs_2_.7) | copy-start | bytes 292
  102.9 9.0 %copy-start.5 = (f32[2,16,16,128]{3,2,1,0:T(8,128)S(1)}, f32[2,16,16,128]{3,2,1,0:T(8,128)}, u32[]{:S(2)}) copy-start(f32[2,16,16,128]{3,2,1,0:T(8,128)} %copy-done.4) | copy-start | bytes 786436
  102.9 9.0 %all-to-all-start.1 = ((f32[4,4,16,128]{3,2,1,0:T(8,128)}), f32[4,4,16,128]{3,2,1,0:T(8,128)S(1)}, u32[]{:S(2)}, u32[]{:S(2)}) async-start(f32[4,4,16,128]{3,2,1,0:T(8,128)} %get-tuple-element.81), calls=%async_computation.1 | async-start | bytes 262144 | tf_op jit(solution)/shard_map/all_to_all | solution.py:884
where the time goes:
time: 114 us; the launch traced here: 113 us
  Pallas kernels  42.6 us (37%)
  starting transfers between devices  35.9 us (31%)
  waiting for transfers between devices  27.5 us (24%)
  local copies, waits for them, and re-layouts  5.84 us (5%)
    ppermute x3, waiting for transfers between devices, from_block_before(): return lax.ppermute(x, ('comp', 'gx'), row_pairs())  17.5 us
    ppermute x3, starting transfers between devices, from_block_before(): return lax.ppermute(x, ('comp', 'gx'), row_pairs())  16.4 us
    pallas_call x3, Pallas kernels, advection(): pl.pallas_call(functools.partial(advection_kernel, first_part, parts, lev...  16.3 us
    pallas_call x3, Pallas kernels, uptake(): pl.pallas_call(functools.partial(uptake_kernel, first_part * SUB), grid=(...  9.03 us
    pallas_call x3, Pallas kernels, pack_tracers(): pl.pallas_call(functools.partial(ignoring, len(after), pack_tracers_kerne...  7.06 us
    pallas_call x5, Pallas kernels, call_once(): pl.pallas_call(functools.partial(ignoring, len(after), kernel), grid=(1,)...  6.75 us
    unnamed x38, local copies, waits for them, and re-layouts  5.84 us
    ppermute x1, waiting for transfers between devices, from_after(): lax.ppermute(x, axis, [(i + 1, i) for i in range(lax.axis_size(axis) - 1)])  5.7 us
  transfers between devices with their start and end apart: 14, of which 5 were waited for; matrix products, arithmetic and copies ran while one was open for 0% of the time, Pallas kernels for 30%

commit v1 on v0

--- a/solution.py
+++ b/solution.py
@@ -21,7 +21,7 @@
 DT_BIO = 0.5
 WARMING_FACTOR = 0.5
 CLEAR_WATER = 0.5
-VMEM_LIMIT = 16 * 1024 * 1024
+VMEM_LIMIT = 10 * 1024 * 1024
 COVER = pl.CostEstimate(flops=0, bytes_accessed=200_000_000, transcendentals=0)
 VMEM_MOST = 62 * 1024 * 1024
 
@@ -867,9 +867,7 @@
             heat,
             [] if i == 0 else [token],
         )
-        if i == 0:
-            chunks.append(rims(held_until(later[2:], [carry])))
-        if i + 1 < len(cuts):
+        if i > 0 and i + 1 < len(cuts):
             near = sides(pack_tracers(*chunks[i + 1], [carry]))
         result, token = uptake(
             cut,
@@ -881,6 +879,9 @@
             light,
             result,
         )
+        if i == 0:
+            chunks.append(rims(held_until(later[2:], [token])))
+            near = sides(pack_tracers(*chunks[1], [token]))
     heat = lax.all_to_all(heat, "comp", split_axis=0, concat_axis=0, tiled=True)
     warmed_result, buoyancy = warming(heat, mixed, sea)
     fields = (east_new, north_new, warmed_result, smix, buoyancy)

time: 114 us -> 113 us (level)
  local copies, waits for them, and re-layouts: 5.84 us -> 10.2 us
  waiting for transfers between devices: 27.5 us -> 24.9 us
    unnamed x38 -> x56, local copies, waits for them, and re-layouts: 5.84 us -> 10.2 us
    ppermute x3, waiting for transfers between devices: 17.5 us -> 13.8 us  [from_block_before(): return lax.ppermute(x, ('comp', 'gx'), row_pairs())]
    ppermute x1, waiting for transfers between devices: 5.7 us -> 7.72 us  [from_after(): lax.ppermute(x, axis, [(i + 1, i) for i in range(lax.axis_size(axis) - 1)])]
    ppermute x1, starting transfers between devices: 4.55 us -> 6.26 us  [from_before(): lax.ppermute(x, axis, [(i, i + 1) for i in range(lax.axis_size(axis) - 1)])]
    all_to_all x1, starting transfers between devices: 5.01 us -> 3.48 us  [on_device(): lax.all_to_all(send, 'comp', split_axis=0, concat_axis=0, tiled=True)]
    pallas_call x3, Pallas kernels: 16.3 us -> 15.1 us  [advection(): pl.pallas_call(functools.partial(advection_kernel, first_part, parts, lev...]
  transfers between devices with their start and end apart: 14 -> 14, of which waited for: 5 -> 6; matrix products, arithmetic and copies ran while one was open for 0% -> 0% of each run, Pallas kernels for 30% -> 29%
where the time goes in v1:
time: 113 us
  Pallas kernels  41.5 us (37%)
  starting transfers between devices  35.1 us (31%)
  waiting for transfers between devices  24.9 us (22%)
  local copies, waits for them, and re-layouts  10.2 us (9%)
    ppermute x3, starting transfers between devices, from_block_before(): return lax.ppermute(x, ('comp', 'gx'), row_pairs())  15.9 us
    pallas_call x3, Pallas kernels, advection(): pl.pallas_call(functools.partial(advection_kernel, first_part, parts, lev...  15.1 us
    ppermute x3, waiting for transfers between devices, from_block_before(): return lax.ppermute(x, ('comp', 'gx'), row_pairs())  13.8 us
    unnamed x56, local copies, waits for them, and re-layouts  10.2 us
    pallas_call x3, Pallas kernels, uptake(): pl.pallas_call(functools.partial(uptake_kernel, first_part * SUB), grid=(...  9.06 us
    ppermute x1, waiting for transfers between devices, from_after(): lax.ppermute(x, axis, [(i + 1, i) for i in range(lax.axis_size(axis) - 1)])  7.72 us
    pallas_call x3, Pallas kernels, pack_tracers(): pl.pallas_call(functools.partial(ignoring, len(after), pack_tracers_kerne...  7.06 us
    pallas_call x5, Pallas kernels, call_once(): pl.pallas_call(functools.partial(ignoring, len(after), kernel), grid=(1,)...  6.75 us
  transfers between devices with their start and end apart: 14, of which 6 were waited for; matrix products, arithmetic and copies ran while one was open for 0% of the time, Pallas kernels for 29%

profile of v1, /device:TPU:0, one launch (start us, length us, event | category | flops | bytes accessed | tf_op | source)
XLA Modules:
  0.0 112.6 jit_solution(3215654800631659762)
XLA Ops:
  0.6 0.0 copy-start.11
  0.7 2.1 %shard_map.172 = (f32[5,16,128]{2,1,0:T(8,128)}, f32[2,9,16,128]{3,2,1,0:T(8,128)}, f32[4,16,16,128]{3,2,1,0:T(8,128)}) custom-call(f32[256,128]{1,0:T(8,128)} %bitcast.35, f32[256,128]{1,0:T(8,128)} %bitcast.36, f32[256,128]{1,0:T(8,128)} %bitcast.37, f32[256,128]{1,0:T(8,128)} %bitcast.38, s32[16,128]{1,0:T(8,128)} %refs_0_.14, s32[16,128]{1,0:T(8,128)} %refs_1_.6), custom_call_target="tpu_custom_call" | custom-call | tf_op jit(solution)/shard_map/pallas_call | solution.py:160
  2.8 1.9 %copy-done = f32[24,64,1,1,4,128]{5,4,3,2,1,0:T(4,128)S(1)} copy-done((f32[24,64,1,1,4,128]{5,4,3,2,1,0:T(4,128)S(1)}, f32[24,64,1,1,4,128]{5,4,3,2,1,0:T(4,128)}, u32[]{:S(2)}) %copy-start) | copy-done | bytes 3145752
  4.7 0.8 copy-done.9
  5.4 1.2 %shard_map.173 = (f32[24,2,24,1,128]{4,3,2,1,0:T(1,128)S(1)}, f32[24,2,24,1,128]{4,3,2,1,0:T(1,128)}) custom-call(f32[24,64,4,1,128]{4,3,2,1,0:T(1,128)S(1)} %bitcast.20, f32[5,16,128]{2,1,0:T(8,128)S(1)} %copy-done.9), custom_call_target="tpu_custom_call" | custom-call | tf_op jit(solution)/shard_map/pallas_call | solution.py:96
  6.7 5.8 %collective-permute-start.4 = (f32[24,2,24,128]{3,2,1,0:T(8,128)}, f32[24,2,24,128]{3,2,1,0:T(8,128)}, u32[]{:S(2)}, u32[]{:S(2)}) collective-permute-start(f32[24,2,24,128]{3,2,1,0:T(8,128)} %bitcast.12.refs_2_.refs_6_), channel_id=1, source_target_pairs={{0,8},{8,16},{16,24},{24,2},{2,10},{10,18},{18,26},{26,4},{4,12},{... | collective-permute-start | bytes 1769480 | tf_op jit(solution)/shard_map/ppermute | solution.py:781
  12.5 1.3 %collective-permute-start.3 = (f32[24,2,24,128]{3,2,1,0:T(8,128)S(1)}, f32[24,2,24,128]{3,2,1,0:T(8,128)}, u32[]{:S(2)}, u32[]{:S(2)}) collective-permute-start(f32[24,2,24,128]{3,2,1,0:T(8,128)S(1)} %bitcast.25), channel_id=1, source_target_pairs={{8,0},{16,8},{24,16},{2,24},{10,2},{18,10},{26,18},{4,26},{12,4},{... | collective-permute-start | bytes 1769480 | tf_op jit(solution)/shard_map/ppermute | solution.py:785
  13.8 0.1 collective-permute-start
  13.9 1.2 %collective-permute-done.refs_1_.refs_2_ = f32[5,16,128]{2,1,0:T(8,128)S(1)} collective-permute-done((f32[5,16,128]{2,1,0:T(8,128)S(1)}, f32[5,16,128]{2,1,0:T(8,128)S(1)}, u32[]{:S(2)}, u32[]{:S(2)}) %collective-permute-start) | collective-permute-done | bytes 40992 | tf_op jit(solution)/shard_map/ppermute | solution.py:790
  15.1 0.9 copy-done.10
  16.0 1.3 %collective-permute-start.1 = (f32[14,16,128]{2,1,0:T(8,128)S(1)}, f32[14,16,128]{2,1,0:T(8,128)S(1)}, u32[]{:S(2)}, u32[]{:S(2)}) collective-permute-start(f32[14,16,128]{2,1,0:T(8,128)S(1)} %get-tuple-element.54), channel_id=1, source_target_pairs={{2,0},{4,2},{6,4},{3,1},{5,3},{7,5},{10,8},{12,10},{14,12},{11,9},... | collective-permute-start | bytes 344072 | tf_op jit(solution)/shard_map/ppermute | solution.py:771
  17.3 6.3 %collective-permute-start.2 = (f32[14,16,128]{2,1,0:T(8,128)S(1)}, f32[14,16,128]{2,1,0:T(8,128)S(1)}, u32[]{:S(2)}, u32[]{:S(2)}) collective-permute-start(f32[14,16,128]{2,1,0:T(8,128)S(1)} %get-tuple-element.55), channel_id=1, source_target_pairs={{0,2},{2,4},{4,6},{1,3},{3,5},{5,7},{8,10},{10,12},{12,14},{9,11},... | collective-permute-start | bytes 344072 | tf_op jit(solution)/shard_map/ppermute | solution.py:767
  23.6 1.4 %shard_map.174 = (f32[24,2,24,1,128]{4,3,2,1,0:T(1,128)S(1)}, f32[24,2,24,1,128]{4,3,2,1,0:T(1,128)S(1)}, f32[24,2,16,1,128]{4,3,2,1,0:T(1,128)S(1)}, f32[24,2,16,1,128]{4,3,2,1,0:T(1,128)S(1)}) custom-call(f32[24,64,4,1,128]{4,3,2,1,0:T(1,128)S(1)} %bitcast.21, f32[24,2,24,128]{3,2,1,0:T(8,128)S(1)} %bitcast.26), custom_call_target="tpu_custom_call" | custom-call | tf_op jit(solution)/shard_map/pallas_call | solution.py:96
  25.0 7.7 %collective-permute-done.1.refs_5_ = f32[14,16,128]{2,1,0:T(8,128)S(1)} collective-permute-done((f32[14,16,128]{2,1,0:T(8,128)S(1)}, f32[14,16,128]{2,1,0:T(8,128)S(1)}, u32[]{:S(2)}, u32[]{:S(2)}) %collective-permute-start.1) | collective-permute-done | bytes 114720 | tf_op jit(solution)/shard_map/ppermute | solution.py:771
  32.8 3.2 %shard_map.176 = (f32[256,128]{1,0:T(8,128)}, f32[2,16,16,128]{3,2,1,0:T(8,128)S(1)}, f32[4,18,16,128]{3,2,1,0:T(8,128)S(1)}, f32[2,16,16,128]{3,2,1,0:T(8,128)S...) custom-call(f32[24,2,24,128]{3,2,1,0:T(8,128)S(1)} %bitcast.22, f32[4,16,16,128]{3,2,1,0:T(8,128)S(1)} %copy-done.4, ...), custom_call_target="tpu_custom_call" | custom-call | tf_op jit(solution)/shard_map/pallas_call | solution.py:160
  36.0 0.8 copy-done.3
  36.8 0.7 copy-done.5
  37.5 0.7 copy-done.7
  38.2 0.6 copy-done.17
  38.8 3.5 %all-to-all-start = ((f32[4,18,16,128]{3,2,1,0:T(8,128)}), f32[4,18,16,128]{3,2,1,0:T(8,128)S(1)}, u32[]{:S(2)}, u32[]{:S(2)}) async-start(f32[4,18,16,128]{3,2,1,0:T(8,128)} %copy-done.3), calls=%async_computation | async-start | bytes 1179648 | tf_op jit(solution)/shard_map/all_to_all | solution.py:848
  42.3 3.1 %shard_map.179.refs_9_.refs_2_ = f32[12,24,128]{2,1,0:T(8,128)S(1)} custom-call(f32[4,32,128]{2,1,0:T(8,128)S(1)} %get-tuple-element.61.refs_0_.refs_2_.refs_4_, f32[24,2,24,128]{3,2,1,0:T(8,128)S(1)} %bitcast.27, f32[24,2,24,128]{3,2,1,0:T(8,128)} %bitcast.12.refs_2_.refs_6_, f32[24,2,24,128]{3,2,1,0:T(8,128)} %collective-permute-done.3.refs_3_.refs_7_, ...), custom_call_target="tpu_custom_call" | custom-call | bytes 200000000 | tf_op jit(solution)/shard_map/pallas_call | solution.py:144
  45.5 1.3 %collective-permute-start.8 = (f32[24,2,24,128]{3,2,1,0:T(8,128)S(1)}, f32[24,2,24,128]{3,2,1,0:T(8,128)}, u32[]{:S(2)}, u32[]{:S(2)}) collective-permute-start(f32[24,2,24,128]{3,2,1,0:T(8,128)S(1)} %get-tuple-element.71.refs_1_.refs_5_), channel_id=1, source_target_pairs={{8,0},{16,8},{24,16},{2,24},{10,2},{18,10},{26,18},{4,26},{12,4},{... | collective-permute-start | bytes 1769480 | tf_op jit(solution)/shard_map/ppermute | solution.py:785
  46.8 5.4 %collective-permute-start.9 = (f32[24,2,24,128]{3,2,1,0:T(8,128)S(1)}, f32[24,2,24,128]{3,2,1,0:T(8,128)}, u32[]{:S(2)}, u32[]{:S(2)}) collective-permute-start(f32[24,2,24,128]{3,2,1,0:T(8,128)S(1)} %get-tuple-element.72.refs_2_.refs_6_), channel_id=1, source_target_pairs={{0,8},{8,16},{16,24},{24,2},{2,10},{10,18},{18,26},{26,4},{4,12},{... | collective-permute-start | bytes 1769480 | tf_op jit(solution)/shard_map/ppermute | solution.py:781
  52.1 0.7 copy-done.19
  52.8 0.6 shard_map.178.refs_3_
  53.5 0.1 collective-permute-done.5.refs_10_.refs_11_
  53.6 0.7 copy-done.15
  54.3 0.7 copy-done.20
  55.0 5.5 %shard_map.180 = (f32[24,4,24,128]{3,2,1,0:T(8,128)S(1)}, f32[4,24,128]{2,1,0:T(8,128)S(1)}, f32[4,4,16,128]{3,2,1,0:T(8,128)S(1)}, f32[4,8,128]{2,1,0:T(8,128)S(1)}) custom-call(f32[24]{0:T(128)S(1)} %copy-done.20, f32[4,128]{1,0:T(4,128)S(1)} %bitcast.31, f32[4,32,128]{2,1,0:T(8,128)S(1)} %get-tuple-element.61.refs_0_.refs_2_.refs_4_, ...), custom_call_target="tpu_custom_call" | custom-call | tf_op jit(solution)/shard_map/pallas_call | solution.py:640
  60.5 3.3 %shard_map.181 = (f32[24,256,128]{2,1,0:T(8,128)}, f32[8,128]{1,0:T(8,128)S(1)}) custom-call(f32[24]{0:T(128)S(1)} %copy-done.22, f32[24]{0:T(128)S(1)} %copy-done.24, f32[24]{0:T(128)S(1)} %copy-done.26, f32[192,192]{1,0:T(8,128)S(1)} %shard_map.178.refs_3_, f32[4,32,128]{2,1,0:T(8,128)S(1)} %get-tuple-element.61.refs_0_.refs_2_.refs_4_, ...), custom_call_target="tpu_custom_call" | custom-call | tf_op jit(solution)/shard_map/pallas_call | solution.py:731
  63.8 1.3 %collective-permute-start.6 = (f32[24,2,16,128]{3,2,1,0:T(8,128)S(1)}, f32[24,2,16,128]{3,2,1,0:T(8,128)S(1)}, u32[]{:S(2)}, u32[]{:S(2)}) collective-permute-start(f32[24,2,16,128]{3,2,1,0:T(8,128)S(1)} %get-tuple-element.68.refs_1_.refs_5_), channel_id=1, source_target_pairs={{8,0},{16,8},{24,16},{2,24},{10,2},{18,10},{26,18},{4,26},{12,4},{... | collective-permute-start | bytes 1179656 | tf_op jit(solution)/shard_map/ppermute | solution.py:785
  65.1 4.7 %collective-permute-start.7 = (f32[24,2,16,128]{3,2,1,0:T(8,128)S(1)}, f32[24,2,16,128]{3,2,1,0:T(8,128)S(1)}, u32[]{:S(2)}, u32[]{:S(2)}) collective-permute-start(f32[24,2,16,128]{3,2,1,0:T(8,128)S(1)} %get-tuple-element.69.refs_2_.refs_6_), channel_id=1, source_target_pairs={{0,8},{8,16},{16,24},{24,2},{2,10},{10,18},{18,26},{26,4},{4,12},{... | collective-permute-start | bytes 1179656 | tf_op jit(solution)/shard_map/ppermute | solution.py:781
  69.8 13.8 %collective-permute-done.9.refs_4_.refs_8_ = f32[24,2,24,128]{3,2,1,0:T(8,128)} collective-permute-done((f32[24,2,24,128]{3,2,1,0:T(8,128)S(1)}, f32[24,2,24,128]{3,2,1,0:T(8,128)}, u32[]{:S(2)}, u32[]{:S(2)}) %collective-permute-start.9) | collective-permute-done | bytes 589856 | tf_op jit(solution)/shard_map/ppermute | solution.py:781
  83.5 2.9 %shard_map.184.refs_9_ = f32[12,24,128]{2,1,0:T(8,128)S(1)} custom-call(f32[8,128]{1,0:T(8,128)S(1)} %get-tuple-element.67.refs_2_.refs_0_.refs_14_, f32[24,2,24,128]{3,2,1,0:T(8,128)S(1)} %get-tuple-element.71.refs_1_.refs_5_, f32[24,2,24,128]{3,2,1,0:T(8,128)S(1)} %get-tuple-element.72.refs_2_.refs_6_, ...), custom_call_target="tpu_custom_call" | custom-call | tf_op jit(solution)/shard_map/pallas_call | solution.py:144
  86.5 0.1 collective-permute-start.10
  86.6 1.4 %collective-permute-done.10.refs_10_.refs_11_ = f32[12,24,128]{2,1,0:T(8,128)S(1)} collective-permute-done((f32[12,24,128]{2,1,0:T(8,128)S(1)}, f32[12,24,128]{2,1,0:T(8,128)S(1)}, u32[]{:S(2)}, u32[]{:S(2)}) %collective-permute-start.10) | collective-permute-done | bytes 147488 | tf_op jit(solution)/shard_map/ppermute | solution.py:790
  87.9 5.5 %shard_map.185 = (f32[24,4,24,128]{3,2,1,0:T(8,128)S(1)}, f32[4,24,128]{2,1,0:T(8,128)S(1)}, f32[4,4,16,128]{3,2,1,0:T(8,128)S(1)}, f32[4,8,128]{2,1,0:T(8,128)S(1)}) custom-call(f32[24]{0:T(128)S(1)} %copy-done.21, f32[4,128]{1,0:T(4,128)S(1)} %bitcast.32, ...), custom_call_target="tpu_custom_call", output_to_operand_aliasing={{2}: (13, {})} | custom-call | tf_op jit(solution)/shard_map/pallas_call | solution.py:640
  93.4 1.0 shard_map.186.refs_9_
  94.4 0.2 collective-permute-start.11
  94.6 3.2 %shard_map.187 = (f32[24,256,128]{2,1,0:T(8,128)}, f32[8,128]{1,0:T(8,128)S(1)}) custom-call(f32[24]{0:T(128)S(1)} %copy-done.22, f32[24]{0:T(128)S(1)} %copy-done.24, f32[24]{0:T(128)S(1)} %copy-done.26, f32[192,192]{1,0:T(8,128)S(1)} %shard_map.178.refs_3_, ...), custom_call_target="tpu_custom_call", output_to_operand_aliasing={{0}: (7, {})} | custom-call | tf_op jit(solution)/shard_map/pallas_call | solution.py:731
  97.9 4.2 %shard_map.188 = (f32[24,4,16,128]{3,2,1,0:T(8,128)S(1)}, f32[4,16,128]{2,1,0:T(8,128)S(1)}, f32[4,4,16,128]{3,2,1,0:T(8,128)S(1)}, f32[4,8,128]{2,1,0:T(8,128)}) custom-call(f32[24]{0:T(128)S(1)} %copy-done.21, f32[4,128]{1,0:T(4,128)S(1)} %bitcast.33, ...), custom_call_target="tpu_custom_call", output_to_operand_aliasing={{2}: (13, {})} | custom-call | tf_op jit(solution)/shard_map/pallas_call | solution.py:640
  102.0 0.7 copy-done.2
  102.7 4.0 %all-to-all-start.1 = ((f32[4,4,16,128]{3,2,1,0:T(8,128)}), f32[4,4,16,128]{3,2,1,0:T(8,128)S(1)}, u32[]{:S(2)}, u32[]{:S(2)}) async-start(f32[4,4,16,128]{3,2,1,0:T(8,128)} %copy-done.2), calls=%async_computation.1 | async-start | bytes 262144 | tf_op jit(solution)/shard_map/all_to_all | solution.py:885
  106.7 0.9 copy-done.8
  107.7 0.8 shard_map.177
  108.5 2.6 %shard_map.190 = (f32[24,256,128]{2,1,0:T(8,128)}, f32[8,128]{1,0:T(8,128)}) custom-call(f32[24]{0:T(128)S(1)} %copy-done.23, f32[24]{0:T(128)S(1)} %copy-done.25, f32[24]{0:T(128)S(1)} %copy-done.27, f32[192,192]{1,0:T(8,128)S(1)} %shard_map.178.refs_3_, ...), custom_call_target="tpu_custom_call", output_to_operand_aliasing={{0}: (7, {})} | custom-call | tf_op jit(solution)/shard_map/pallas_call | solution.py:731
  111.0 0.7 all-to-all-done.1.refs_2_
  111.8 0.8 shard_map.189
  (55 shorter events, 0.1 us)
Async XLA Ops:
  0.6 32.1 %copy-start.11 = (s32[16,128]{1,0:T(8,128)S(1)}, s32[16,128]{1,0:T(8,128)}, u32[]{:S(2)}) copy-start(s32[16,128]{1,0:T(8,128)} %refs_0_.14) | copy-start | bytes 24580
  0.6 32.1 %copy-start.13 = (s32[16,128]{1,0:T(8,128)S(1)}, s32[16,128]{1,0:T(8,128)}, u32[]{:S(2)}) copy-start(s32[16,128]{1,0:T(8,128)} %refs_1_.6) | copy-start | bytes 24580
  2.8 1.9 %copy-start = (f32[24,64,1,1,4,128]{5,4,3,2,1,0:T(4,128)S(1)}, f32[24,64,1,1,4,128]{5,4,3,2,1,0:T(4,128)}, u32[]{:S(2)}) copy-start(f32[24,64,1,1,4,128]{5,4,3,2,1,0:T(4,128)} %param.19) | copy-start | bytes 9437188
  4.7 0.8 copy-start.9
  5.4 18.1 %copy-start.1 = (f32[24,64,1,1,4,128]{5,4,3,2,1,0:T(4,128)S(1)}, f32[24,64,1,1,4,128]{5,4,3,2,1,0:T(4,128)}, u32[]{:S(2)}) copy-start(f32[24,64,1,1,4,128]{5,4,3,2,1,0:T(4,128)} %param.19) | copy-start | bytes 9437188
  5.4 27.3 %copy-start.4 = (f32[4,16,16,128]{3,2,1,0:T(8,128)S(1)}, f32[4,16,16,128]{3,2,1,0:T(8,128)}, u32[]{:S(2)}) copy-start(f32[4,16,16,128]{3,2,1,0:T(8,128)} %get-tuple-element.51.refs_1_) | copy-start | bytes 1572868
  6.7 35.6 %collective-permute-start.4 = (f32[24,2,24,128]{3,2,1,0:T(8,128)}, f32[24,2,24,128]{3,2,1,0:T(8,128)}, u32[]{:S(2)}, u32[]{:S(2)}) collective-permute-start(f32[24,2,24,128]{3,2,1,0:T(8,128)} %bitcast.12.refs_2_.refs_6_), channel_id=1, source_target_pairs={{0,8},{8,16},{16,24},{24,2},{2,10},{10,18},{18,26},{26,4},{4,12},{... | collective-permute-start | bytes 1769480 | tf_op jit(solution)/shard_map/ppermute | solution.py:781
  12.5 29.8 %collective-permute-start.3 = (f32[24,2,24,128]{3,2,1,0:T(8,128)S(1)}, f32[24,2,24,128]{3,2,1,0:T(8,128)}, u32[]{:S(2)}, u32[]{:S(2)}) collective-permute-start(f32[24,2,24,128]{3,2,1,0:T(8,128)S(1)} %bitcast.25), channel_id=1, source_target_pairs={{8,0},{16,8},{24,16},{2,24},{10,2},{18,10},{26,18},{4,26},{12,4},{... | collective-permute-start | bytes 1769480 | tf_op jit(solution)/shard_map/ppermute | solution.py:785
  13.8 1.3 %collective-permute-start = (f32[5,16,128]{2,1,0:T(8,128)S(1)}, f32[5,16,128]{2,1,0:T(8,128)S(1)}, u32[]{:S(2)}, u32[]{:S(2)}) collective-permute-start(f32[5,16,128]{2,1,0:T(8,128)S(1)} %copy-done.9), channel_id=1, source_target_pairs={{0,1},{1,0},{2,3},{3,2},{4,5},{5,4},{6,7},{7,6},{8,9},{9,8},{10,11... | collective-permute-start | bytes 122888 | tf_op jit(solution)/shard_map/ppermute | solution.py:790
  15.1 0.9 copy-start.10
  16.0 16.7 %collective-permute-start.1 = (f32[14,16,128]{2,1,0:T(8,128)S(1)}, f32[14,16,128]{2,1,0:T(8,128)S(1)}, u32[]{:S(2)}, u32[]{:S(2)}) collective-permute-start(f32[14,16,128]{2,1,0:T(8,128)S(1)} %get-tuple-element.54), channel_id=1, source_target_pairs={{2,0},{4,2},{6,4},{3,1},{5,3},{7,5},{10,8},{12,10},{14,12},{11,9},... | collective-permute-start | bytes 344072 | tf_op jit(solution)/shard_map/ppermute | solution.py:771
  17.3 15.4 %collective-permute-start.2 = (f32[14,16,128]{2,1,0:T(8,128)S(1)}, f32[14,16,128]{2,1,0:T(8,128)S(1)}, u32[]{:S(2)}, u32[]{:S(2)}) collective-permute-start(f32[14,16,128]{2,1,0:T(8,128)S(1)} %get-tuple-element.55), channel_id=1, source_target_pairs={{0,2},{2,4},{4,6},{1,3},{3,5},{5,7},{8,10},{10,12},{12,14},{9,11},... | collective-permute-start | bytes 344072 | tf_op jit(solution)/shard_map/ppermute | solution.py:767
  36.0 0.8 copy-start.3
  36.8 0.7 copy-start.5
  37.5 0.7 copy-start.7
  38.2 0.6 copy-start.17
  38.8 14.7 %all-to-all-start = ((f32[4,18,16,128]{3,2,1,0:T(8,128)}), f32[4,18,16,128]{3,2,1,0:T(8,128)S(1)}, u32[]{:S(2)}, u32[]{:S(2)}) async-start(f32[4,18,16,128]{3,2,1,0:T(8,128)} %copy-done.3), calls=%async_computation | async-start | bytes 1179648 | tf_op jit(solution)/shard_map/all_to_all | solution.py:848
  45.5 24.3 %collective-permute-start.8 = (f32[24,2,24,128]{3,2,1,0:T(8,128)S(1)}, f32[24,2,24,128]{3,2,1,0:T(8,128)}, u32[]{:S(2)}, u32[]{:S(2)}) collective-permute-start(f32[24,2,24,128]{3,2,1,0:T(8,128)S(1)} %get-tuple-element.71.refs_1_.refs_5_), channel_id=1, source_target_pairs={{8,0},{16,8},{24,16},{2,24},{10,2},{18,10},{26,18},{4,26},{12,4},{... | collective-permute-start | bytes 1769480 | tf_op jit(solution)/shard_map/ppermute | solution.py:785
  46.8 36.8 %collective-permute-start.9 = (f32[24,2,24,128]{3,2,1,0:T(8,128)S(1)}, f32[24,2,24,128]{3,2,1,0:T(8,128)}, u32[]{:S(2)}, u32[]{:S(2)}) collective-permute-start(f32[24,2,24,128]{3,2,1,0:T(8,128)S(1)} %get-tuple-element.72.refs_2_.refs_6_), channel_id=1, source_target_pairs={{0,8},{8,16},{16,24},{24,2},{2,10},{10,18},{18,26},{26,4},{4,12},{... | collective-permute-start | bytes 1769480 | tf_op jit(solution)/shard_map/ppermute | solution.py:781
  52.1 1.5 %collective-permute-start.5 = (f32[12,24,128]{2,1,0:T(8,128)S(1)}, f32[12,24,128]{2,1,0:T(8,128)}, u32[]{:S(2)}, u32[]{:S(2)}) collective-permute-start(f32[12,24,128]{2,1,0:T(8,128)S(1)} %shard_map.179.refs_9_.refs_2_), channel_id=1, source_target_pairs={{0,1},{1,0},{2,3},{3,2},{4,5},{5,4},{6,7},{7,6},{8,9},{9,8},{10,11... | collective-permute-start | bytes 442376 | tf_op jit(solution)/shard_map/ppermute | solution.py:790
  52.1 0.7 copy-start.19
  53.5 7.0 %copy-start.22 = (f32[24]{0:T(128)S(1)}, f32[24]{0:T(128)}, u32[]{:S(2)}) copy-start(f32[24]{0:T(128)} %refs_0_.15) | copy-start | bytes 292
  53.5 7.0 %copy-start.24 = (f32[24]{0:T(128)S(1)}, f32[24]{0:T(128)}, u32[]{:S(2)}) copy-start(f32[24]{0:T(128)} %refs_1_.7) | copy-start | bytes 292
  53.5 7.0 %copy-start.26 = (f32[24]{0:T(128)S(1)}, f32[24]{0:T(128)}, u32[]{:S(2)}) copy-start(f32[24]{0:T(128)} %refs_2_.7) | copy-start | bytes 292
  53.6 0.7 copy-start.15
  54.3 0.7 copy-start.20
  60.5 27.4 %copy-start.16 = (f32[1,1,4,128]{3,2,1,0:T(4,128)S(1)}, f32[1,1,4,128]{3,2,1,0:T(4,128)}, u32[]{:S(2)}) copy-start(f32[1,1,4,128]{3,2,1,0:T(4,128)} %param.20) | copy-start | bytes 6148
  60.5 27.4 %copy-start.21 = (f32[24]{0:T(128)S(1)}, f32[24]{0:T(128)}, u32[]{:S(2)}) copy-start(f32[24]{0:T(128)} %refs_0_.13) | copy-start | bytes 292
  63.8 29.6 %collective-permute-start.6 = (f32[24,2,16,128]{3,2,1,0:T(8,128)S(1)}, f32[24,2,16,128]{3,2,1,0:T(8,128)S(1)}, u32[]{:S(2)}, u32[]{:S(2)}) collective-permute-start(f32[24,2,16,128]{3,2,1,0:T(8,128)S(1)} %get-tuple-element.68.refs_1_.refs_5_), channel_id=1, source_target_pairs={{8,0},{16,8},{24,16},{2,24},{10,2},{18,10},{26,18},{4,26},{12,4},{... | collective-permute-start | bytes 1179656 | tf_op jit(solution)/shard_map/ppermute | solution.py:785
  65.1 28.3 %collective-permute-start.7 = (f32[24,2,16,128]{3,2,1,0:T(8,128)S(1)}, f32[24,2,16,128]{3,2,1,0:T(8,128)S(1)}, u32[]{:S(2)}, u32[]{:S(2)}) collective-permute-start(f32[24,2,16,128]{3,2,1,0:T(8,128)S(1)} %get-tuple-element.69.refs_2_.refs_6_), channel_id=1, source_target_pairs={{0,8},{8,16},{16,24},{24,2},{2,10},{10,18},{18,26},{26,4},{4,12},{... | collective-permute-start | bytes 1179656 | tf_op jit(solution)/shard_map/ppermute | solution.py:781
  86.5 1.4 %collective-permute-start.10 = (f32[12,24,128]{2,1,0:T(8,128)S(1)}, f32[12,24,128]{2,1,0:T(8,128)S(1)}, u32[]{:S(2)}, u32[]{:S(2)}) collective-permute-start(f32[12,24,128]{2,1,0:T(8,128)S(1)} %shard_map.184.refs_9_), channel_id=1, source_target_pairs={{0,1},{1,0},{2,3},{3,2},{4,5},{5,4},{6,7},{7,6},{8,9},{9,8},{10,11... | collective-permute-start | bytes 442376 | tf_op jit(solution)/shard_map/ppermute | solution.py:790
  94.4 3.4 %collective-permute-start.11 = (f32[12,16,128]{2,1,0:T(8,128)S(1)}, f32[12,16,128]{2,1,0:T(8,128)S(1)}, u32[]{:S(2)}, u32[]{:S(2)}) collective-permute-start(f32[12,16,128]{2,1,0:T(8,128)S(1)} %shard_map.186.refs_9_), channel_id=1, source_target_pairs={{0,1},{1,0},{2,3},{3,2},{4,5},{5,4},{6,7},{7,6},{8,9},{9,8},{10,11... | collective-permute-start | bytes 294920 | tf_op jit(solution)/shard_map/ppermute | solution.py:790
  94.6 12.1 %copy-start.18 = (f32[2,16,128]{2,1,0:T(8,128)S(1)}, f32[2,16,128]{2,1,0:T(8,128)}, u32[]{:S(2)}) copy-start(f32[2,16,128]{2,1,0:T(8,128)} %copy-done.17) | copy-start | bytes 49156
  97.8 10.6 %copy-start.23 = (f32[24]{0:T(128)S(1)}, f32[24]{0:T(128)}, u32[]{:S(2)}) copy-start(f32[24]{0:T(128)} %refs_0_.15) | copy-start | bytes 292
  97.8 10.6 %copy-start.25 = (f32[24]{0:T(128)S(1)}, f32[24]{0:T(128)}, u32[]{:S(2)}) copy-start(f32[24]{0:T(128)} %refs_1_.7) | copy-start | bytes 292
  97.8 10.6 %copy-start.27 = (f32[24]{0:T(128)S(1)}, f32[24]{0:T(128)}, u32[]{:S(2)}) copy-start(f32[24]{0:T(128)} %refs_2_.7) | copy-start | bytes 292
  97.9 13.9 %copy-start.12 = (s32[16,128]{1,0:T(8,128)S(1)}, s32[16,128]{1,0:T(8,128)}, u32[]{:S(2)}) copy-start(s32[16,128]{1,0:T(8,128)} %refs_0_.14) | copy-start | bytes 24580
  97.9 13.9 %copy-start.14 = (s32[16,128]{1,0:T(8,128)S(1)}, s32[16,128]{1,0:T(8,128)}, u32[]{:S(2)}) copy-start(s32[16,128]{1,0:T(8,128)} %refs_1_.6) | copy-start | bytes 24580
  102.0 0.7 copy-start.2
  102.7 9.1 %copy-start.6 = (f32[2,16,16,128]{3,2,1,0:T(8,128)S(1)}, f32[2,16,16,128]{3,2,1,0:T(8,128)}, u32[]{:S(2)}) copy-start(f32[2,16,16,128]{3,2,1,0:T(8,128)} %copy-done.5) | copy-start | bytes 786436
  102.7 9.0 %all-to-all-start.1 = ((f32[4,4,16,128]{3,2,1,0:T(8,128)}), f32[4,4,16,128]{3,2,1,0:T(8,128)S(1)}, u32[]{:S(2)}, u32[]{:S(2)}) async-start(f32[4,4,16,128]{3,2,1,0:T(8,128)} %copy-done.2), calls=%async_computation.1 | async-start | bytes 262144 | tf_op jit(solution)/shard_map/all_to_all | solution.py:885
  106.7 1.0 copy-start.8

commit v2 on v1

--- a/solution.py
+++ b/solution.py
@@ -138,7 +138,7 @@
         packed_ref[pair] = both_ends(acc)
 
 
-def pack_tracers(own, rim, after, cost=None):
+def pack_tracers(own, rim, after):
     tracers, _, levels, cols = own[0].shape
     rows = pl.BlockSpec((tracers, NSUB, SUB, cols), lambda i: (0, 0, i, 0))
     return pl.pallas_call(
@@ -148,7 +148,6 @@
         out_specs=pl.BlockSpec((tracers // 2, SUB, cols), lambda i: (0, i, 0)),
         out_shape=shaped(tracers // 2, levels, cols),
         compiler_params=params(),
-        cost_estimate=cost,
     )(*after, *own, *rim)
 
 
@@ -156,7 +155,7 @@
     kernel(*refs[count:])
 
 
-def call_once(kernel, operands, outs, scratch=(), scalars=(), after=(), limit=VMEM_LIMIT):
+def call_once(kernel, operands, outs, scratch=(), scalars=(), after=(), limit=VMEM_LIMIT, cost=None):
     return pl.pallas_call(
         functools.partial(ignoring, len(after), kernel),
         grid=(1,),
@@ -167,6 +166,7 @@
         out_shape=outs,
         scratch_shapes=list(scratch),
         compiler_params=params(limit),
+        cost_estimate=cost,
     )(*after, *scalars, *operands)
 
 
@@ -817,13 +817,8 @@
     q = dissolved_species.reshape(tracer_count, level_count, sub_rows, 1, tile_cols)
     parts = levels // SUB
     every = parts * blocks
-    sizes = [every - 5 * every // 8, 3 * every // 8, every // 4]
+    sizes = [every - 5 * every // 8, every // 4, every // 4, every // 8]
     cuts = [(sum(sizes[:i]), size) for i, size in enumerate(sizes)]
-    matrix = call_once(
-        spread_kernel,
-        [stoichiometry_matrix],
-        [shaped(SUB * tracer_count, SUB * tracer_count)],
-    )[0]
     scalars_of_uptake = (
         peak_intake_speed,
         feedstock_midpoint_constant,
@@ -847,8 +842,15 @@
     )
     received = lax.all_to_all(send, "comp", split_axis=0, concat_axis=0, tiled=True)
     east_new, north_new = velocities(local, faces, received)
-    own = pack_tracers(*chunks[0], [depths], COVER)
-    chunks.append(rims(held_until(later[:2], [own])))
+    matrix = call_once(
+        spread_kernel,
+        [stoichiometry_matrix],
+        [shaped(SUB * tracer_count, SUB * tracer_count)],
+        after=[depths],
+        cost=COVER,
+    )[0]
+    chunks.append(rims(held_until(later[:2], [matrix])))
+    own = pack_tracers(*chunks[0], [matrix])
 
     surface = topmost_sunshine.reshape(sub_rows, tile_cols)
     carry, heat, result = None, None, None
@@ -879,8 +881,10 @@
             light,
             result,
         )
+        if i + 2 < len(cuts):
+            at = 2 * (i + 1)
+            chunks.append(rims(held_until(later[at : at + 2], [token])))
         if i == 0:
-            chunks.append(rims(held_until(later[2:], [token])))
             near = sides(pack_tracers(*chunks[1], [token]))
     heat = lax.all_to_all(heat, "comp", split_axis=0, concat_axis=0, tiled=True)
     warmed_result, buoyancy = warming(heat, mixed, sea)

time: 113 us -> 117 us (1.035)
  starting transfers between devices: 35.1 us -> 43 us
  waiting for transfers between devices: 24.9 us -> 19.5 us
  Pallas kernels: 41.5 us -> 44.7 us
  local copies, waits for them, and re-layouts: 10.2 us -> 7.84 us
    ppermute x3 -> x4, waiting for transfers between devices: 13.8 us -> 1.9 us  [from_block_before(): return lax.ppermute(x, ('comp', 'gx'), row_pairs())]
    ppermute x3 -> x4, starting transfers between devices: 15.9 us -> 20.2 us  [from_block_before(): return lax.ppermute(x, ('comp', 'gx'), row_pairs())]
    all_to_all x1, waiting for transfers between devices: 0.01 us -> 3.77 us  [on_device(): lax.all_to_all(send, 'comp', split_axis=0, concat_axis=0, tiled=True)]
    unnamed x56 -> x50, local copies, waits for them, and re-layouts: 10.2 us -> 7.84 us
    all_to_all x1, starting transfers between devices: 4.02 us -> 6.34 us  [on_device(): heat = lax.all_to_all(heat, 'comp', split_axis=0, concat_axis=0, tiled=True)]
    pallas_call x3 -> x4, Pallas kernels: 15.1 us -> 17.2 us  [advection(): pl.pallas_call(functools.partial(advection_kernel, first_part, parts, lev...]
    all_to_all x1, waiting for transfers between devices: 0.73 us -> 2.37 us  [on_device(): heat = lax.all_to_all(heat, 'comp', split_axis=0, concat_axis=0, tiled=True)]
    ppermute x3 -> x4, starting transfers between devices: 3.85 us -> 5.13 us  [from_block_after(): lax.ppermute(x, ('comp', 'gx'), [(later, own) for own, later in row_pairs...]
  transfers between devices with their start and end apart: 14 -> 17, of which waited for: 6 -> 7; matrix products, arithmetic and copies ran while one was open for 0% -> 0% of each run, Pallas kernels for 29% -> 32%
where the time goes in v2:
time: 117 us; the launch traced here: 116 us
  Pallas kernels  44.7 us (38%)
  starting transfers between devices  43 us (37%)
  waiting for transfers between devices  19.5 us (17%)
  local copies, waits for them, and re-layouts  7.84 us (7%)
    ppermute x4, starting transfers between devices, from_block_before(): return lax.ppermute(x, ('comp', 'gx'), row_pairs())  20.2 us
    pallas_call x4, Pallas kernels, advection(): pl.pallas_call(functools.partial(advection_kernel, first_part, parts, lev...  17.2 us
    pallas_call x4, Pallas kernels, uptake(): pl.pallas_call(functools.partial(uptake_kernel, first_part * SUB), grid=(...  10.2 us
    unnamed x50, local copies, waits for them, and re-layouts  7.84 us
    ppermute x1, waiting for transfers between devices, from_after(): lax.ppermute(x, axis, [(i + 1, i) for i in range(lax.axis_size(axis) - 1)])  7.67 us
    pallas_call x4, Pallas kernels, pack_tracers(): pl.pallas_call(functools.partial(ignoring, len(after), pack_tracers_kerne...  7.05 us
    pallas_call x5, Pallas kernels, call_once(): pl.pallas_call(functools.partial(ignoring, len(after), kernel), grid=(1,)...  6.76 us
    all_to_all x1, starting transfers between devices, on_device(): heat = lax.all_to_all(heat, 'comp', split_axis=0, concat_axis=0, tiled=True)  6.34 us
  transfers between devices with their start and end apart: 17, of which 7 were waited for; matrix products, arithmetic and copies ran while one was open for 0% of the time, Pallas kernels for 32%

profile of v2, /device:TPU:0, one launch (start us, length us, event | category | flops | bytes accessed | tf_op | source)
XLA Modules:
  0.0 116.0 jit_solution(14415506950439558656)
XLA Ops:
  0.7 2.1 %shard_map.172 = (f32[5,16,128]{2,1,0:T(8,128)}, f32[2,9,16,128]{3,2,1,0:T(8,128)}, f32[4,16,16,128]{3,2,1,0:T(8,128)}) custom-call(f32[256,128]{1,0:T(8,128)} %bitcast.40, f32[256,128]{1,0:T(8,128)} %bitcast.41, f32[256,128]{1,0:T(8,128)} %bitcast.42, f32[256,128]{1,0:T(8,128)} %bitcast.43, s32[16,128]{1,0:T(8,128)} %refs_0_.16, s32[16,128]{1,0:T(8,128)} %refs_1_.10), custom_call_target="tpu_custom_call" | custom-call | tf_op jit(solution)/shard_map/pallas_call | solution.py:159
  2.8 1.9 %copy-done = f32[24,64,1,1,4,128]{5,4,3,2,1,0:T(4,128)S(1)} copy-done((f32[24,64,1,1,4,128]{5,4,3,2,1,0:T(4,128)S(1)}, f32[24,64,1,1,4,128]{5,4,3,2,1,0:T(4,128)}, u32[]{:S(2)}) %copy-start) | copy-done | bytes 3145752
  4.7 0.8 copy-done.8
  5.5 1.2 %shard_map.173 = (f32[24,2,24,1,128]{4,3,2,1,0:T(1,128)S(1)}, f32[24,2,24,1,128]{4,3,2,1,0:T(1,128)}) custom-call(f32[24,64,4,1,128]{4,3,2,1,0:T(1,128)S(1)} %bitcast.22, f32[5,16,128]{2,1,0:T(8,128)S(1)} %copy-done.8), custom_call_target="tpu_custom_call" | custom-call | tf_op jit(solution)/shard_map/pallas_call | solution.py:96
  6.7 5.8 %collective-permute-start.6 = (f32[24,2,24,128]{3,2,1,0:T(8,128)}, f32[24,2,24,128]{3,2,1,0:T(8,128)}, u32[]{:S(2)}, u32[]{:S(2)}) collective-permute-start(f32[24,2,24,128]{3,2,1,0:T(8,128)} %bitcast.13.refs_2_.refs_6_), channel_id=1, source_target_pairs={{0,8},{8,16},{16,24},{24,2},{2,10},{10,18},{18,26},{26,4},{4,12},{... | collective-permute-start | bytes 1769480 | tf_op jit(solution)/shard_map/ppermute | solution.py:781
  12.5 1.3 %collective-permute-start.5 = (f32[24,2,24,128]{3,2,1,0:T(8,128)S(1)}, f32[24,2,24,128]{3,2,1,0:T(8,128)}, u32[]{:S(2)}, u32[]{:S(2)}) collective-permute-start(f32[24,2,24,128]{3,2,1,0:T(8,128)S(1)} %bitcast.26), channel_id=1, source_target_pairs={{8,0},{16,8},{24,16},{2,24},{10,2},{18,10},{26,18},{4,26},{12,4},{... | collective-permute-start | bytes 1769480 | tf_op jit(solution)/shard_map/ppermute | solution.py:785
  13.8 0.1 collective-permute-start
  13.9 1.2 %collective-permute-done.refs_1_.refs_2_ = f32[5,16,128]{2,1,0:T(8,128)S(1)} collective-permute-done((f32[5,16,128]{2,1,0:T(8,128)S(1)}, f32[5,16,128]{2,1,0:T(8,128)S(1)}, u32[]{:S(2)}, u32[]{:S(2)}) %collective-permute-start) | collective-permute-done | bytes 40992 | tf_op jit(solution)/shard_map/ppermute | solution.py:790
  15.1 0.9 copy-done.9
  16.0 1.3 %collective-permute-start.1 = (f32[14,16,128]{2,1,0:T(8,128)S(1)}, f32[14,16,128]{2,1,0:T(8,128)S(1)}, u32[]{:S(2)}, u32[]{:S(2)}) collective-permute-start(f32[14,16,128]{2,1,0:T(8,128)S(1)} %get-tuple-element.64), channel_id=1, source_target_pairs={{2,0},{4,2},{6,4},{3,1},{5,3},{7,5},{10,8},{12,10},{14,12},{11,9},... | collective-permute-start | bytes 344072 | tf_op jit(solution)/shard_map/ppermute | solution.py:771
  17.3 6.3 %collective-permute-start.2 = (f32[14,16,128]{2,1,0:T(8,128)S(1)}, f32[14,16,128]{2,1,0:T(8,128)S(1)}, u32[]{:S(2)}, u32[]{:S(2)}) collective-permute-start(f32[14,16,128]{2,1,0:T(8,128)S(1)} %get-tuple-element.65), channel_id=1, source_target_pairs={{0,2},{2,4},{4,6},{1,3},{3,5},{5,7},{8,10},{10,12},{12,14},{9,11},... | collective-permute-start | bytes 344072 | tf_op jit(solution)/shard_map/ppermute | solution.py:767
  23.6 1.5 %shard_map.174 = (f32[24,2,16,1,128]{4,3,2,1,0:T(1,128)S(1)}, f32[24,2,16,1,128]{4,3,2,1,0:T(1,128)S(1)}, f32[24,2,16,1,128]{4,3,2,1,0:T(1,128)S(1)}, f32[24,2,1...) custom-call(f32[24,64,4,1,128]{4,3,2,1,0:T(1,128)S(1)} %bitcast.23, ...), custom_call_target="tpu_custom_call" | custom-call | tf_op jit(solution)/shard_map/pallas_call | solution.py:96
  25.1 7.7 %collective-permute-done.1.refs_5_ = f32[14,16,128]{2,1,0:T(8,128)S(1)} collective-permute-done((f32[14,16,128]{2,1,0:T(8,128)S(1)}, f32[14,16,128]{2,1,0:T(8,128)S(1)}, u32[]{:S(2)}, u32[]{:S(2)}) %collective-permute-start.1) | collective-permute-done | bytes 114720 | tf_op jit(solution)/shard_map/ppermute | solution.py:771
  32.8 3.2 %shard_map.176 = (f32[256,128]{1,0:T(8,128)}, f32[2,16,16,128]{3,2,1,0:T(8,128)S(1)}, f32[4,18,16,128]{3,2,1,0:T(8,128)S(1)}, f32[2,16,16,128]{3,2,1,0:T(8,128)S...) custom-call(f32[24,2,16,128]{3,2,1,0:T(8,128)S(1)} %bitcast.24, f32[4,16,16,128]{3,2,1,0:T(8,128)S(1)} %copy-done.3, ...), custom_call_target="tpu_custom_call" | custom-call | tf_op jit(solution)/shard_map/pallas_call | solution.py:159
  36.0 0.8 copy-done.2
  36.8 0.7 copy-done.4
  37.5 0.7 copy-done.6
  38.2 0.6 copy-done.15
  38.8 3.5 %all-to-all-start = ((f32[4,18,16,128]{3,2,1,0:T(8,128)}), f32[4,18,16,128]{3,2,1,0:T(8,128)S(1)}, u32[]{:S(2)}, u32[]{:S(2)}) async-start(f32[4,18,16,128]{3,2,1,0:T(8,128)} %copy-done.2), calls=%async_computation | async-start | bytes 1179648 | tf_op jit(solution)/shard_map/all_to_all | solution.py:843
  42.3 0.6 shard_map.178.refs_2_.refs_0_.refs_3_
  42.9 1.3 %collective-permute-start.3 = (f32[24,2,16,128]{3,2,1,0:T(8,128)S(1)}, f32[24,2,16,128]{3,2,1,0:T(8,128)}, u32[]{:S(2)}, u32[]{:S(2)}) collective-permute-start(f32[24,2,16,128]{3,2,1,0:T(8,128)S(1)} %get-tuple-element.75.refs_1_.refs_5_), channel_id=1, source_target_pairs={{8,0},{16,8},{24,16},{2,24},{10,2},{18,10},{26,18},{4,26},{12,4},{... | collective-permute-start | bytes 1179656 | tf_op jit(solution)/shard_map/ppermute | solution.py:785
  44.2 5.3 %collective-permute-start.4 = (f32[24,2,16,128]{3,2,1,0:T(8,128)S(1)}, f32[24,2,16,128]{3,2,1,0:T(8,128)}, u32[]{:S(2)}, u32[]{:S(2)}) collective-permute-start(f32[24,2,16,128]{3,2,1,0:T(8,128)S(1)} %get-tuple-element.76.refs_2_.refs_6_), channel_id=1, source_target_pairs={{0,8},{8,16},{16,24},{24,2},{2,10},{10,18},{18,26},{26,4},{4,12},{... | collective-permute-start | bytes 1179656 | tf_op jit(solution)/shard_map/ppermute | solution.py:781
  49.6 3.7 %shard_map.180.refs_9_ = f32[12,24,128]{2,1,0:T(8,128)} custom-call(f32[192,192]{1,0:T(8,128)S(1)} %shard_map.178.refs_2_.refs_0_.refs_3_, f32[24,2,24,128]{3,2,1,0:T(8,128)S(1)} %bitcast.28, f32[24,2,24,128]{3,2,1,0:T(8,128)} %bitcast.13.refs_2_.refs_6_, f32[24,2,24,128]{3,2,1,0:T(8,128)} %collective-permute-done.5.refs_3_.refs_7_, ...), custom_call_target="tpu_custom_call" | custom-call | tf_op jit(solution)/shard_map/pallas_call | solution.py:144
  53.3 3.8 %all-to-all-done.received_ref.refs_3_.refs_4_ = f32[4,18,16,128]{3,2,1,0:T(8,128)S(1)} async-done(((f32[4,18,16,128]{3,2,1,0:T(8,128)}), f32[4,18,16,128]{3,2,1,0:T(8,128)S(1)}, u32[]{:S(2)}, u32[]{:S(2)}) %all-to-all-start) | async-done | bytes 589856 | tf_op jit(solution)/shard_map/all_to_all | solution.py:843
  57.1 0.7 copy-done.14
  57.8 0.7 copy-done.24
  58.5 6.1 %shard_map.181 = (f32[24,4,24,128]{3,2,1,0:T(8,128)S(1)}, f32[4,24,128]{2,1,0:T(8,128)S(1)}, f32[4,4,16,128]{3,2,1,0:T(8,128)}, f32[4,8,128]{2,1,0:T(8,128)S(1)}) custom-call(f32[24]{0:T(128)S(1)} %copy-done.24, f32[4,128]{1,0:T(4,128)S(1)} %bitcast.35, f32[4,32,128]{2,1,0:T(8,128)S(1)} %get-tuple-element.71.refs_0_.refs_2_.refs_4_, ...), custom_call_target="tpu_custom_call" | custom-call | tf_op jit(solution)/shard_map/pallas_call | solution.py:640
  64.6 3.3 %shard_map.182 = (f32[24,256,128]{2,1,0:T(8,128)}, f32[8,128]{1,0:T(8,128)S(1)}) custom-call(f32[24]{0:T(128)S(1)} %copy-done.18, f32[24]{0:T(128)S(1)} %copy-done.20, f32[24]{0:T(128)S(1)} %copy-done.22, f32[192,192]{1,0:T(8,128)S(1)} %shard_map.178.refs_2_.refs_0_.refs_3_, f32[4,32,128]{2,1,0:T(8,128)S(1)} %get-tuple-element.71.refs_0_.refs_2_.refs_4_, ...), custom_call_target="tpu_custom_call" | custom-call | tf_op jit(solution)/shard_map/pallas_call | solution.py:731
  67.8 1.3 %collective-permute-start.11 = (f32[24,2,16,128]{3,2,1,0:T(8,128)S(1)}, f32[24,2,16,128]{3,2,1,0:T(8,128)S(1)}, u32[]{:S(2)}, u32[]{:S(2)}) collective-permute-start(f32[24,2,16,128]{3,2,1,0:T(8,128)S(1)} %get-tuple-element.91.refs_1_.refs_5_), channel_id=1, source_target_pairs={{8,0},{16,8},{24,16},{2,24},{10,2},{18,10},{26,18},{4,26},{12,4},{... | collective-permute-start | bytes 1179656 | tf_op jit(solution)/shard_map/ppermute | solution.py:785
  69.1 4.6 %collective-permute-start.12 = (f32[24,2,16,128]{3,2,1,0:T(8,128)S(1)}, f32[24,2,16,128]{3,2,1,0:T(8,128)S(1)}, u32[]{:S(2)}, u32[]{:S(2)}) collective-permute-start(f32[24,2,16,128]{3,2,1,0:T(8,128)S(1)} %get-tuple-element.92.refs_2_.refs_6_), channel_id=1, source_target_pairs={{0,8},{8,16},{16,24},{24,2},{2,10},{10,18},{18,26},{26,4},{4,12},{... | collective-permute-start | bytes 1179656 | tf_op jit(solution)/shard_map/ppermute | solution.py:781
  73.7 1.9 %shard_map.183.refs_9_ = f32[12,16,128]{2,1,0:T(8,128)S(1)} custom-call(f32[8,128]{1,0:T(8,128)S(1)} %get-tuple-element.80.refs_0_.refs_14_.refs_2_, f32[24,2,16,128]{3,2,1,0:T(8,128)S(1)} %get-tuple-element.75.refs_1_.refs_5_, f32[24,2,16,128]{3,2,1,0:T(8,128)S(1)} %get-tuple-element.76.refs_2_.refs_6_, ...), custom_call_target="tpu_custom_call" | custom-call | tf_op jit(solution)/shard_map/pallas_call | solution.py:144
  75.7 1.3 %collective-permute-done.8.refs_10_.refs_11_ = f32[12,16,128]{2,1,0:T(8,128)S(1)} collective-permute-done((f32[12,16,128]{2,1,0:T(8,128)S(1)}, f32[12,16,128]{2,1,0:T(8,128)S(1)}, u32[]{:S(2)}, u32[]{:S(2)}) %collective-permute-start.8) | collective-permute-done | bytes 98336 | tf_op jit(solution)/shard_map/ppermute | solution.py:790
  77.0 4.5 %shard_map.184 = (f32[24,4,16,128]{3,2,1,0:T(8,128)S(1)}, f32[4,16,128]{2,1,0:T(8,128)S(1)}, f32[4,4,16,128]{3,2,1,0:T(8,128)}, f32[4,8,128]{2,1,0:T(8,128)S(1)}) custom-call(f32[24]{0:T(128)S(1)} %copy-done.24, f32[4,128]{1,0:T(4,128)S(1)} %bitcast.36, ...), custom_call_target="tpu_custom_call", output_to_operand_aliasing={{2}: (13, {})} | custom-call | tf_op jit(solution)/shard_map/pallas_call | solution.py:640
  81.5 2.5 %shard_map.185 = (f32[24,256,128]{2,1,0:T(8,128)}, f32[8,128]{1,0:T(8,128)S(1)}) custom-call(f32[24]{0:T(128)S(1)} %copy-done.18, f32[24]{0:T(128)S(1)} %copy-done.20, f32[24]{0:T(128)S(1)} %copy-done.22, f32[192,192]{1,0:T(8,128)S(1)} %shard_map.178.refs_2_.refs_0_.refs_3_, ...), custom_call_target="tpu_custom_call", output_to_operand_aliasing={{0}: (7, {})} | custom-call | tf_op jit(solution)/shard_map/pallas_call | solution.py:731
  84.0 1.3 %collective-permute-start.9 = (f32[24,2,8,128]{3,2,1,0:T(8,128)S(1)}, f32[24,2,8,128]{3,2,1,0:T(8,128)S(1)}, u32[]{:S(2)}, u32[]{:S(2)}) collective-permute-start(f32[24,2,8,128]{3,2,1,0:T(8,128)S(1)} %get-tuple-element.87.refs_1_.refs_5_), channel_id=1, source_target_pairs={{8,0},{16,8},{24,16},{2,24},{10,2},{18,10},{26,18},{4,26},{12,4},{... | collective-permute-start | bytes 589832 | tf_op jit(solution)/shard_map/ppermute | solution.py:785
  85.3 4.6 %collective-permute-start.10 = (f32[24,2,8,128]{3,2,1,0:T(8,128)S(1)}, f32[24,2,8,128]{3,2,1,0:T(8,128)S(1)}, u32[]{:S(2)}, u32[]{:S(2)}) collective-permute-start(f32[24,2,8,128]{3,2,1,0:T(8,128)S(1)} %get-tuple-element.88.refs_2_.refs_6_), channel_id=1, source_target_pairs={{0,8},{8,16},{16,24},{24,2},{2,10},{10,18},{18,26},{26,4},{4,12},{... | collective-permute-start | bytes 589832 | tf_op jit(solution)/shard_map/ppermute | solution.py:781
  89.9 1.0 shard_map.188.refs_9_
  91.0 1.3 %collective-permute-done.13.refs_10_.refs_11_ = f32[12,16,128]{2,1,0:T(8,128)S(1)} collective-permute-done((f32[12,16,128]{2,1,0:T(8,128)S(1)}, f32[12,16,128]{2,1,0:T(8,128)S(1)}, u32[]{:S(2)}, u32[]{:S(2)}) %collective-permute-start.13) | collective-permute-done | bytes 98336 | tf_op jit(solution)/shard_map/ppermute | solution.py:790
  92.3 4.1 %shard_map.189 = (f32[24,4,16,128]{3,2,1,0:T(8,128)S(1)}, f32[4,16,128]{2,1,0:T(8,128)S(1)}, f32[4,4,16,128]{3,2,1,0:T(8,128)}, f32[4,8,128]{2,1,0:T(8,128)S(1)}) custom-call(f32[24]{0:T(128)S(1)} %copy-done.24, f32[4,128]{1,0:T(4,128)S(1)} %bitcast.37, ...), custom_call_target="tpu_custom_call", output_to_operand_aliasing={{2}: (13, {})} | custom-call | tf_op jit(solution)/shard_map/pallas_call | solution.py:640
  96.4 1.9 %collective-permute-done.10.refs_4_.refs_8_ = f32[24,2,8,128]{3,2,1,0:T(8,128)S(1)} collective-permute-done((f32[24,2,8,128]{3,2,1,0:T(8,128)S(1)}, f32[24,2,8,128]{3,2,1,0:T(8,128)S(1)}, u32[]{:S(2)}, u32[]{:S(2)}) %collective-permute-start.10) | collective-permute-done | bytes 196640 | tf_op jit(solution)/shard_map/ppermute | solution.py:781
  98.3 0.4 shard_map.190.refs_9_
  98.8 2.6 %shard_map.191 = (f32[24,256,128]{2,1,0:T(8,128)}, f32[8,128]{1,0:T(8,128)S(1)}) custom-call(f32[24]{0:T(128)S(1)} %copy-done.18, f32[24]{0:T(128)S(1)} %copy-done.20, f32[24]{0:T(128)S(1)} %copy-done.22, f32[192,192]{1,0:T(8,128)S(1)} %shard_map.178.refs_2_.refs_0_.refs_3_, ...), custom_call_target="tpu_custom_call", output_to_operand_aliasing={{0}: (7, {})} | custom-call | tf_op jit(solution)/shard_map/pallas_call | solution.py:731
  101.4 2.5 %shard_map.192 = (f32[24,4,8,128]{3,2,1,0:T(8,128)S(1)}, f32[4,8,128]{2,1,0:T(8,128)S(1)}, f32[4,4,16,128]{3,2,1,0:T(8,128)}, f32[4,8,128]{2,1,0:T(8,128)}) custom-call(f32[24]{0:T(128)S(1)} %copy-done.24, f32[4,128]{1,0:T(4,128)S(1)} %bitcast.38, f32[4,32,128]{2,1,0:T(8,128)S(1)} %get-tuple-element.71.refs_0_.refs_2_.refs_4_, ...), custom_call_target="tpu_custom_call", output_to_operand_aliasing={{2}: (13, {})} | custom-call | tf_op jit(solution)/shard_map/pallas_call | solution.py:640
  103.9 6.3 %all-to-all-start.1 = ((f32[4,4,16,128]{3,2,1,0:T(8,128)}), f32[4,4,16,128]{3,2,1,0:T(8,128)S(1)}, u32[]{:S(2)}, u32[]{:S(2)}) async-start(f32[4,4,16,128]{3,2,1,0:T(8,128)} %get-tuple-element.101), calls=%async_computation.1 | async-start | bytes 262144 | tf_op jit(solution)/shard_map/all_to_all | solution.py:889
  110.2 0.8 shard_map.177
  111.0 1.9 %shard_map.194 = (f32[24,256,128]{2,1,0:T(8,128)}, f32[8,128]{1,0:T(8,128)}) custom-call(f32[24]{0:T(128)S(1)} %copy-done.19, f32[24]{0:T(128)S(1)} %copy-done.21, f32[24]{0:T(128)S(1)} %copy-done.23, f32[192,192]{1,0:T(8,128)S(1)} %shard_map.178.refs_2_.refs_0_.refs_3_, ...), custom_call_target="tpu_custom_call", output_to_operand_aliasing={{0}: (7, {})} | custom-call | tf_op jit(solution)/shard_map/pallas_call | solution.py:731
  112.9 2.4 %all-to-all-done.1.refs_2_ = f32[4,4,16,128]{3,2,1,0:T(8,128)S(1)} async-done(((f32[4,4,16,128]{3,2,1,0:T(8,128)}), f32[4,4,16,128]{3,2,1,0:T(8,128)S(1)}, u32[]{:S(2)}, u32[]{:S(2)}) %all-to-all-start.1) | async-done | bytes 131104 | tf_op jit(solution)/shard_map/all_to_all | solution.py:889
  115.2 0.8 shard_map.193
  (59 shorter events, 0.3 us)
Async XLA Ops:
  0.6 32.1 %copy-start.10 = (s32[16,128]{1,0:T(8,128)S(1)}, s32[16,128]{1,0:T(8,128)}, u32[]{:S(2)}) copy-start(s32[16,128]{1,0:T(8,128)} %refs_0_.16) | copy-start | bytes 24580
  0.6 32.1 %copy-start.12 = (s32[16,128]{1,0:T(8,128)S(1)}, s32[16,128]{1,0:T(8,128)}, u32[]{:S(2)}) copy-start(s32[16,128]{1,0:T(8,128)} %refs_1_.10) | copy-start | bytes 24580
  2.8 1.9 %copy-start = (f32[24,64,1,1,4,128]{5,4,3,2,1,0:T(4,128)S(1)}, f32[24,64,1,1,4,128]{5,4,3,2,1,0:T(4,128)}, u32[]{:S(2)}) copy-start(f32[24,64,1,1,4,128]{5,4,3,2,1,0:T(4,128)} %param.19) | copy-start | bytes 9437188
  4.7 0.8 copy-start.8
  5.5 18.1 %copy-start.1 = (f32[24,64,1,1,4,128]{5,4,3,2,1,0:T(4,128)S(1)}, f32[24,64,1,1,4,128]{5,4,3,2,1,0:T(4,128)}, u32[]{:S(2)}) copy-start(f32[24,64,1,1,4,128]{5,4,3,2,1,0:T(4,128)} %param.19) | copy-start | bytes 9437188
  5.5 27.3 %copy-start.3 = (f32[4,16,16,128]{3,2,1,0:T(8,128)S(1)}, f32[4,16,16,128]{3,2,1,0:T(8,128)}, u32[]{:S(2)}) copy-start(f32[4,16,16,128]{3,2,1,0:T(8,128)} %get-tuple-element.61.refs_1_) | copy-start | bytes 1572868
  6.7 42.8 %collective-permute-start.6 = (f32[24,2,24,128]{3,2,1,0:T(8,128)}, f32[24,2,24,128]{3,2,1,0:T(8,128)}, u32[]{:S(2)}, u32[]{:S(2)}) collective-permute-start(f32[24,2,24,128]{3,2,1,0:T(8,128)} %bitcast.13.refs_2_.refs_6_), channel_id=1, source_target_pairs={{0,8},{8,16},{16,24},{24,2},{2,10},{10,18},{18,26},{26,4},{4,12},{... | collective-permute-start | bytes 1769480 | tf_op jit(solution)/shard_map/ppermute | solution.py:781
  12.5 37.0 %collective-permute-start.5 = (f32[24,2,24,128]{3,2,1,0:T(8,128)S(1)}, f32[24,2,24,128]{3,2,1,0:T(8,128)}, u32[]{:S(2)}, u32[]{:S(2)}) collective-permute-start(f32[24,2,24,128]{3,2,1,0:T(8,128)S(1)} %bitcast.26), channel_id=1, source_target_pairs={{8,0},{16,8},{24,16},{2,24},{10,2},{18,10},{26,18},{4,26},{12,4},{... | collective-permute-start | bytes 1769480 | tf_op jit(solution)/shard_map/ppermute | solution.py:785
  13.8 1.3 %collective-permute-start = (f32[5,16,128]{2,1,0:T(8,128)S(1)}, f32[5,16,128]{2,1,0:T(8,128)S(1)}, u32[]{:S(2)}, u32[]{:S(2)}) collective-permute-start(f32[5,16,128]{2,1,0:T(8,128)S(1)} %copy-done.8), channel_id=1, source_target_pairs={{0,1},{1,0},{2,3},{3,2},{4,5},{5,4},{6,7},{7,6},{8,9},{9,8},{10,11... | collective-permute-start | bytes 122888 | tf_op jit(solution)/shard_map/ppermute | solution.py:790
  15.1 0.9 copy-start.9
  16.0 26.3 %copy-start.17 = (f32[24,24]{1,0:T(8,128)S(1)}, f32[24,24]{1,0:T(8,128)}, u32[]{:S(2)}) copy-start(f32[24,24]{1,0:T(8,128)} %refs_1_.6) | copy-start | bytes 6916
  16.0 16.7 %collective-permute-start.1 = (f32[14,16,128]{2,1,0:T(8,128)S(1)}, f32[14,16,128]{2,1,0:T(8,128)S(1)}, u32[]{:S(2)}, u32[]{:S(2)}) collective-permute-start(f32[14,16,128]{2,1,0:T(8,128)S(1)} %get-tuple-element.64), channel_id=1, source_target_pairs={{2,0},{4,2},{6,4},{3,1},{5,3},{7,5},{10,8},{12,10},{14,12},{11,9},... | collective-permute-start | bytes 344072 | tf_op jit(solution)/shard_map/ppermute | solution.py:771
  17.3 15.4 %collective-permute-start.2 = (f32[14,16,128]{2,1,0:T(8,128)S(1)}, f32[14,16,128]{2,1,0:T(8,128)S(1)}, u32[]{:S(2)}, u32[]{:S(2)}) collective-permute-start(f32[14,16,128]{2,1,0:T(8,128)S(1)} %get-tuple-element.65), channel_id=1, source_target_pairs={{0,2},{2,4},{4,6},{1,3},{3,5},{5,7},{8,10},{10,12},{12,14},{9,11},... | collective-permute-start | bytes 344072 | tf_op jit(solution)/shard_map/ppermute | solution.py:767
  36.0 0.8 copy-start.2
  36.8 0.7 copy-start.4
  37.5 0.7 copy-start.6
  38.2 0.6 copy-start.15
  38.8 18.3 %all-to-all-start = ((f32[4,18,16,128]{3,2,1,0:T(8,128)}), f32[4,18,16,128]{3,2,1,0:T(8,128)S(1)}, u32[]{:S(2)}, u32[]{:S(2)}) async-start(f32[4,18,16,128]{3,2,1,0:T(8,128)} %copy-done.2), calls=%async_computation | async-start | bytes 1179648 | tf_op jit(solution)/shard_map/all_to_all | solution.py:843
  42.9 30.8 %collective-permute-start.3 = (f32[24,2,16,128]{3,2,1,0:T(8,128)S(1)}, f32[24,2,16,128]{3,2,1,0:T(8,128)}, u32[]{:S(2)}, u32[]{:S(2)}) collective-permute-start(f32[24,2,16,128]{3,2,1,0:T(8,128)S(1)} %get-tuple-element.75.refs_1_.refs_5_), channel_id=1, source_target_pairs={{8,0},{16,8},{24,16},{2,24},{10,2},{18,10},{26,18},{4,26},{12,4},{... | collective-permute-start | bytes 1179656 | tf_op jit(solution)/shard_map/ppermute | solution.py:785
  44.2 29.5 %collective-permute-start.4 = (f32[24,2,16,128]{3,2,1,0:T(8,128)S(1)}, f32[24,2,16,128]{3,2,1,0:T(8,128)}, u32[]{:S(2)}, u32[]{:S(2)}) collective-permute-start(f32[24,2,16,128]{3,2,1,0:T(8,128)S(1)} %get-tuple-element.76.refs_2_.refs_6_), channel_id=1, source_target_pairs={{0,8},{8,16},{16,24},{24,2},{2,10},{10,18},{18,26},{26,4},{4,12},{... | collective-permute-start | bytes 1179656 | tf_op jit(solution)/shard_map/ppermute | solution.py:781
  53.3 3.8 %collective-permute-start.7 = (f32[12,24,128]{2,1,0:T(8,128)}, f32[12,24,128]{2,1,0:T(8,128)S(1)}, u32[]{:S(2)}, u32[]{:S(2)}) collective-permute-start(f32[12,24,128]{2,1,0:T(8,128)} %shard_map.180.refs_9_), channel_id=1, source_target_pairs={{0,1},{1,0},{2,3},{3,2},{4,5},{5,4},{6,7},{7,6},{8,9},{9,8},{10,11... | collective-permute-start | bytes 442376 | tf_op jit(solution)/shard_map/ppermute | solution.py:790
  57.1 7.5 %copy-start.18 = (f32[24]{0:T(128)S(1)}, f32[24]{0:T(128)}, u32[]{:S(2)}) copy-start(f32[24]{0:T(128)} %refs_0_.17) | copy-start | bytes 292
  57.1 7.5 %copy-start.20 = (f32[24]{0:T(128)S(1)}, f32[24]{0:T(128)}, u32[]{:S(2)}) copy-start(f32[24]{0:T(128)} %refs_1_.11) | copy-start | bytes 292
  57.1 7.5 %copy-start.22 = (f32[24]{0:T(128)S(1)}, f32[24]{0:T(128)}, u32[]{:S(2)}) copy-start(f32[24]{0:T(128)} %refs_2_.9) | copy-start | bytes 292
  57.1 0.7 copy-start.14
  57.8 0.7 copy-start.24
  67.8 22.1 %collective-permute-start.11 = (f32[24,2,16,128]{3,2,1,0:T(8,128)S(1)}, f32[24,2,16,128]{3,2,1,0:T(8,128)S(1)}, u32[]{:S(2)}, u32[]{:S(2)}) collective-permute-start(f32[24,2,16,128]{3,2,1,0:T(8,128)S(1)} %get-tuple-element.91.refs_1_.refs_5_), channel_id=1, source_target_pairs={{8,0},{16,8},{24,16},{2,24},{10,2},{18,10},{26,18},{4,26},{12,4},{... | collective-permute-start | bytes 1179656 | tf_op jit(solution)/shard_map/ppermute | solution.py:785
  69.1 20.8 %collective-permute-start.12 = (f32[24,2,16,128]{3,2,1,0:T(8,128)S(1)}, f32[24,2,16,128]{3,2,1,0:T(8,128)S(1)}, u32[]{:S(2)}, u32[]{:S(2)}) collective-permute-start(f32[24,2,16,128]{3,2,1,0:T(8,128)S(1)} %get-tuple-element.92.refs_2_.refs_6_), channel_id=1, source_target_pairs={{0,8},{8,16},{16,24},{24,2},{2,10},{10,18},{18,26},{26,4},{4,12},{... | collective-permute-start | bytes 1179656 | tf_op jit(solution)/shard_map/ppermute | solution.py:781
  75.6 1.4 %collective-permute-start.8 = (f32[12,16,128]{2,1,0:T(8,128)S(1)}, f32[12,16,128]{2,1,0:T(8,128)S(1)}, u32[]{:S(2)}, u32[]{:S(2)}) collective-permute-start(f32[12,16,128]{2,1,0:T(8,128)S(1)} %shard_map.183.refs_9_), channel_id=1, source_target_pairs={{0,1},{1,0},{2,3},{3,2},{4,5},{5,4},{6,7},{7,6},{8,9},{9,8},{10,11... | collective-permute-start | bytes 294920 | tf_op jit(solution)/shard_map/ppermute | solution.py:790
  84.0 12.3 %collective-permute-start.9 = (f32[24,2,8,128]{3,2,1,0:T(8,128)S(1)}, f32[24,2,8,128]{3,2,1,0:T(8,128)S(1)}, u32[]{:S(2)}, u32[]{:S(2)}) collective-permute-start(f32[24,2,8,128]{3,2,1,0:T(8,128)S(1)} %get-tuple-element.87.refs_1_.refs_5_), channel_id=1, source_target_pairs={{8,0},{16,8},{24,16},{2,24},{10,2},{18,10},{26,18},{4,26},{12,4},{... | collective-permute-start | bytes 589832 | tf_op jit(solution)/shard_map/ppermute | solution.py:785
  85.3 13.0 %collective-permute-start.10 = (f32[24,2,8,128]{3,2,1,0:T(8,128)S(1)}, f32[24,2,8,128]{3,2,1,0:T(8,128)S(1)}, u32[]{:S(2)}, u32[]{:S(2)}) collective-permute-start(f32[24,2,8,128]{3,2,1,0:T(8,128)S(1)} %get-tuple-element.88.refs_2_.refs_6_), channel_id=1, source_target_pairs={{0,8},{8,16},{16,24},{24,2},{2,10},{10,18},{18,26},{26,4},{4,12},{... | collective-permute-start | bytes 589832 | tf_op jit(solution)/shard_map/ppermute | solution.py:781
  90.9 1.4 %collective-permute-start.13 = (f32[12,16,128]{2,1,0:T(8,128)S(1)}, f32[12,16,128]{2,1,0:T(8,128)S(1)}, u32[]{:S(2)}, u32[]{:S(2)}) collective-permute-start(f32[12,16,128]{2,1,0:T(8,128)S(1)} %shard_map.188.refs_9_), channel_id=1, source_target_pairs={{0,1},{1,0},{2,3},{3,2},{4,5},{5,4},{6,7},{7,6},{8,9},{9,8},{10,11... | collective-permute-start | bytes 294920 | tf_op jit(solution)/shard_map/ppermute | solution.py:790
  98.7 2.7 %collective-permute-start.14 = (f32[12,8,128]{2,1,0:T(8,128)S(1)}, f32[12,8,128]{2,1,0:T(8,128)S(1)}, u32[]{:S(2)}, u32[]{:S(2)}) collective-permute-start(f32[12,8,128]{2,1,0:T(8,128)S(1)} %shard_map.190.refs_9_), channel_id=1, source_target_pairs={{0,1},{1,0},{2,3},{3,2},{4,5},{5,4},{6,7},{7,6},{8,9},{9,8},{10,11... | collective-permute-start | bytes 147464 | tf_op jit(solution)/shard_map/ppermute | solution.py:790
  98.7 11.5 %copy-start.7 = (f32[2,16,16,128]{3,2,1,0:T(8,128)S(1)}, f32[2,16,16,128]{3,2,1,0:T(8,128)}, u32[]{:S(2)}) copy-start(f32[2,16,16,128]{3,2,1,0:T(8,128)} %copy-done.6) | copy-start | bytes 786436
  98.7 11.5 %copy-start.16 = (f32[2,16,128]{2,1,0:T(8,128)S(1)}, f32[2,16,128]{2,1,0:T(8,128)}, u32[]{:S(2)}) copy-start(f32[2,16,128]{2,1,0:T(8,128)} %copy-done.15) | copy-start | bytes 49156
  98.7 12.2 %copy-start.19 = (f32[24]{0:T(128)S(1)}, f32[24]{0:T(128)}, u32[]{:S(2)}) copy-start(f32[24]{0:T(128)} %refs_0_.17) | copy-start | bytes 292
  98.7 12.2 %copy-start.21 = (f32[24]{0:T(128)S(1)}, f32[24]{0:T(128)}, u32[]{:S(2)}) copy-start(f32[24]{0:T(128)} %refs_1_.11) | copy-start | bytes 292
  98.8 12.2 %copy-start.23 = (f32[24]{0:T(128)S(1)}, f32[24]{0:T(128)}, u32[]{:S(2)}) copy-start(f32[24]{0:T(128)} %refs_2_.9) | copy-start | bytes 292
  101.3 13.9 %copy-start.5 = (f32[2,16,16,128]{3,2,1,0:T(8,128)S(1)}, f32[2,16,16,128]{3,2,1,0:T(8,128)}, u32[]{:S(2)}) copy-start(f32[2,16,16,128]{3,2,1,0:T(8,128)} %copy-done.4) | copy-start | bytes 786436
  101.3 13.9 %copy-start.11 = (s32[16,128]{1,0:T(8,128)S(1)}, s32[16,128]{1,0:T(8,128)}, u32[]{:S(2)}) copy-start(s32[16,128]{1,0:T(8,128)} %refs_0_.16) | copy-start | bytes 24580
  101.3 13.9 %copy-start.13 = (s32[16,128]{1,0:T(8,128)S(1)}, s32[16,128]{1,0:T(8,128)}, u32[]{:S(2)}) copy-start(s32[16,128]{1,0:T(8,128)} %refs_1_.10) | copy-start | bytes 24580
  103.9 11.4 %all-to-all-start.1 = ((f32[4,4,16,128]{3,2,1,0:T(8,128)}), f32[4,4,16,128]{3,2,1,0:T(8,128)S(1)}, u32[]{:S(2)}, u32[]{:S(2)}) async-start(f32[4,4,16,128]{3,2,1,0:T(8,128)} %get-tuple-element.101), calls=%async_computation.1 | async-start | bytes 262144 | tf_op jit(solution)/shard_map/all_to_all | solution.py:889

commit v3 on v2

--- a/solution.py
+++ b/solution.py
@@ -125,27 +125,31 @@
 
 
 def pack_tracers_kernel(low_ref, high_ref, after_ref, before_ref, packed_ref):
-    tracers, _, _, cols = low_ref.shape
+    tracers, _, levels, cols = low_ref.shape
     lane = lanes_of((SUB, cols))
     for pair in range(tracers // 2):
-        acc = jnp.zeros((SUB, cols), jnp.float32)
-        for odd in range(2):
-            t = 2 * pair + odd
-            rows = [before_ref[t, 1], low_ref[t, 0], low_ref[t, 1], high_ref[t, 0], high_ref[t, 1]]
-            for r, x in enumerate(rows + [after_ref[t, 0]]):
-                at = HALF * odd + SLOTS * (r + 1)
-                acc = jnp.where(lane // SLOTS == at // SLOTS, turn(x, at + NSUB, 1), acc)
-        packed_ref[pair] = both_ends(acc)
+        for k in range(0, levels, SUB):
+            near = slice(k, k + SUB)
+            acc = jnp.zeros((SUB, cols), jnp.float32)
+            for odd in range(2):
+                t = 2 * pair + odd
+                rows = [(before_ref, 1), (low_ref, 0), (low_ref, 1), (high_ref, 0), (high_ref, 1)]
+                for r, (ref, n) in enumerate(rows + [(after_ref, 0)]):
+                    at = HALF * odd + SLOTS * (r + 1)
+                    x = turn(ref[t, n, near], at + NSUB, 1)
+                    acc = jnp.where(lane // SLOTS == at // SLOTS, x, acc)
+            packed_ref[pair, near] = both_ends(acc)
 
 
 def pack_tracers(own, rim, after):
     tracers, _, levels, cols = own[0].shape
-    rows = pl.BlockSpec((tracers, NSUB, SUB, cols), lambda i: (0, 0, i, 0))
+    group = 4 if tracers % 4 == 0 else 2
+    rows = pl.BlockSpec((group, NSUB, levels, cols), lambda i: (i, 0, 0, 0))
     return pl.pallas_call(
         functools.partial(ignoring, len(after), pack_tracers_kernel),
-        grid=(levels // SUB,),
+        grid=(tracers // group,),
         in_specs=[pl.BlockSpec(memory_space=pl.ANY)] * len(after) + [rows] * 4,
-        out_specs=pl.BlockSpec((tracers // 2, SUB, cols), lambda i: (0, i, 0)),
+        out_specs=pl.BlockSpec((group // 2, levels, cols), lambda i: (i, 0, 0)),
         out_shape=shaped(tracers // 2, levels, cols),
         compiler_params=params(),
     )(*after, *own, *rim)
@@ -406,9 +410,10 @@
     )
 
 
-def velocity_kernel(local_ref, faces_ref, received_ref, east_ref, north_ref):
+def velocity_kernel(local_ref, faces_ref, received_ref, east_ref, north_ref, token_ref):
     blocks = received_ref.shape[0]
     _, tile_rows, levels, cols = local_ref.shape
+    token_ref[...] = jnp.zeros_like(token_ref)
     group = lax.axis_index("comp")
     level = (group * levels + subs_of((levels, cols))).astype(jnp.float32)
     for f, out_ref in enumerate((east_ref, north_ref)):
@@ -433,8 +438,8 @@
             whole(faces.shape),
             pl.BlockSpec((blocks, 2, levels, cols), lambda i: (0, ENTRIES // 2 - 1, 0, 0)),
         ],
-        out_specs=[whole(out.shape)] * 2,
-        out_shape=[out] * 2,
+        out_specs=[whole(out.shape)] * 2 + [whole((SUB, cols))],
+        out_shape=[out] * 2 + [shaped(SUB, cols)],
         compiler_params=params(),
     )(local, faces, received)
 
@@ -817,7 +822,7 @@
     q = dissolved_species.reshape(tracer_count, level_count, sub_rows, 1, tile_cols)
     parts = levels // SUB
     every = parts * blocks
-    sizes = [every - 5 * every // 8, every // 4, every // 4, every // 8]
+    sizes = [every - 5 * every // 8, 3 * every // 8, every // 4]
     cuts = [(sum(sizes[:i]), size) for i, size in enumerate(sizes)]
     scalars_of_uptake = (
         peak_intake_speed,
@@ -841,7 +846,7 @@
         blocks, levels, ocean_rows, sea, packed, after, before, later[:1]
     )
     received = lax.all_to_all(send, "comp", split_axis=0, concat_axis=0, tiled=True)
-    east_new, north_new = velocities(local, faces, received)
+    east_new, north_new, finished = velocities(local, faces, received)
     matrix = call_once(
         spread_kernel,
         [stoichiometry_matrix],
@@ -885,7 +890,7 @@
             at = 2 * (i + 1)
             chunks.append(rims(held_until(later[at : at + 2], [token])))
         if i == 0:
-            near = sides(pack_tracers(*chunks[1], [token]))
+            near = sides(pack_tracers(*chunks[1], [token, finished]))
     heat = lax.all_to_all(heat, "comp", split_axis=0, concat_axis=0, tiled=True)
     warmed_result, buoyancy = warming(heat, mixed, sea)
     fields = (east_new, north_new, warmed_result, smix, buoyancy)

time: 117 us -> 113 us (0.966)
  starting transfers between devices: 43 us -> 37.1 us
  local copies, waits for them, and re-layouts: 7.84 us -> 9.88 us
    ppermute x4 -> x3, starting transfers between devices: 20.2 us -> 15.7 us  [from_block_before(): return lax.ppermute(x, ('comp', 'gx'), row_pairs())]
    all_to_all x1, waiting for transfers between devices: 3.77 us -> 6.76 us  [on_device(): lax.all_to_all(send, 'comp', split_axis=0, concat_axis=0, tiled=True)]
    pallas_call x4 -> x3, Pallas kernels: 7.05 us -> 9.74 us  [pack_tracers(): pl.pallas_call(functools.partial(ignoring, len(after), pack_tracers_kerne...]
    unnamed x50 -> x58, local copies, waits for them, and re-layouts: 7.84 us -> 9.88 us
    ppermute x4 -> x3, waiting for transfers between devices: 1.9 us -> 0.14 us  [from_block_before(): return lax.ppermute(x, ('comp', 'gx'), row_pairs())]
    ppermute x4 -> x3, starting transfers between devices: 5.13 us -> 3.85 us  [from_block_after(): lax.ppermute(x, ('comp', 'gx'), [(later, own) for own, later in row_pairs...]
    ppermute x5 -> x4, waiting for transfers between devices: 3.79 us -> 2.57 us  [from_sides(): other = lax.ppermute(x, 'gy', [(0, 1), (1, 0)])]
    pallas_call x4 -> x3, Pallas kernels: 10.2 us -> 9.07 us  [uptake(): pl.pallas_call(functools.partial(uptake_kernel, first_part * SUB), grid=(...]
  transfers between devices with their start and end apart: 17 -> 14, of which waited for: 7 -> 6; matrix products, arithmetic and copies ran while one was open for 0% -> 0% of each run, Pallas kernels for 32% -> 32%
where the time goes in v3:
time: 113 us; the launch traced here: 112 us
  Pallas kernels  45.4 us (40%)
  starting transfers between devices  37.1 us (33%)
  waiting for transfers between devices  18.5 us (16%)
  local copies, waits for them, and re-layouts  9.88 us (9%)
    pallas_call x3, Pallas kernels, advection(): pl.pallas_call(functools.partial(advection_kernel, first_part, parts, lev...  16.4 us
    ppermute x3, starting transfers between devices, from_block_before(): return lax.ppermute(x, ('comp', 'gx'), row_pairs())  15.7 us
    unnamed x58, local copies, waits for them, and re-layouts  9.88 us
    pallas_call x3, Pallas kernels, pack_tracers(): pl.pallas_call(functools.partial(ignoring, len(after), pack_tracers_kerne...  9.74 us
    pallas_call x3, Pallas kernels, uptake(): pl.pallas_call(functools.partial(uptake_kernel, first_part * SUB), grid=(...  9.07 us
    ppermute x1, waiting for transfers between devices, from_after(): lax.ppermute(x, axis, [(i + 1, i) for i in range(lax.axis_size(axis) - 1)])  7.7 us
    all_to_all x1, waiting for transfers between devices, on_device(): lax.all_to_all(send, 'comp', split_axis=0, concat_axis=0, tiled=True)  6.76 us
    pallas_call x5, Pallas kernels, call_once(): pl.pallas_call(functools.partial(ignoring, len(after), kernel), grid=(1,)...  6.76 us
  transfers between devices with their start and end apart: 14, of which 6 were waited for; matrix products, arithmetic and copies ran while one was open for 0% of the time, Pallas kernels for 32%

profile of v3, /device:TPU:0, one launch (start us, length us, event | category | flops | bytes accessed | tf_op | source)
XLA Modules:
  0.0 111.9 jit_solution(1734848944649925393)
XLA Ops:
  0.6 0.0 copy-start.12
  0.7 2.1 %shard_map.172 = (f32[5,16,128]{2,1,0:T(8,128)}, f32[2,9,16,128]{3,2,1,0:T(8,128)}, f32[4,16,16,128]{3,2,1,0:T(8,128)}) custom-call(f32[256,128]{1,0:T(8,128)} %bitcast.35, f32[256,128]{1,0:T(8,128)} %bitcast.36, f32[256,128]{1,0:T(8,128)} %bitcast.37, f32[256,128]{1,0:T(8,128)} %bitcast.38, s32[16,128]{1,0:T(8,128)} %refs_0_.12, s32[16,128]{1,0:T(8,128)} %refs_1_.8), custom_call_target="tpu_custom_call" | custom-call | tf_op jit(solution)/shard_map/pallas_call | solution.py:163
  2.8 1.9 %copy-done = f32[24,64,1,1,4,128]{5,4,3,2,1,0:T(4,128)S(1)} copy-done((f32[24,64,1,1,4,128]{5,4,3,2,1,0:T(4,128)S(1)}, f32[24,64,1,1,4,128]{5,4,3,2,1,0:T(4,128)}, u32[]{:S(2)}) %copy-start) | copy-done | bytes 3145752
  4.7 0.8 copy-done.10
  5.5 1.2 %shard_map.173 = (f32[24,2,24,1,128]{4,3,2,1,0:T(1,128)S(1)}, f32[24,2,24,1,128]{4,3,2,1,0:T(1,128)}) custom-call(f32[24,64,4,1,128]{4,3,2,1,0:T(1,128)S(1)} %bitcast.20, f32[5,16,128]{2,1,0:T(8,128)S(1)} %copy-done.10), custom_call_target="tpu_custom_call" | custom-call | tf_op jit(solution)/shard_map/pallas_call | solution.py:96
  6.7 5.8 %collective-permute-start.4 = (f32[24,2,24,128]{3,2,1,0:T(8,128)}, f32[24,2,24,128]{3,2,1,0:T(8,128)}, u32[]{:S(2)}, u32[]{:S(2)}) collective-permute-start(f32[24,2,24,128]{3,2,1,0:T(8,128)} %bitcast.12.refs_2_.refs_6_), channel_id=1, source_target_pairs={{0,8},{8,16},{16,24},{24,2},{2,10},{10,18},{18,26},{26,4},{4,12},{... | collective-permute-start | bytes 1769480 | tf_op jit(solution)/shard_map/ppermute | solution.py:786
  12.5 1.3 %collective-permute-start.3 = (f32[24,2,24,128]{3,2,1,0:T(8,128)S(1)}, f32[24,2,24,128]{3,2,1,0:T(8,128)}, u32[]{:S(2)}, u32[]{:S(2)}) collective-permute-start(f32[24,2,24,128]{3,2,1,0:T(8,128)S(1)} %bitcast.25), channel_id=1, source_target_pairs={{8,0},{16,8},{24,16},{2,24},{10,2},{18,10},{26,18},{4,26},{12,4},{... | collective-permute-start | bytes 1769480 | tf_op jit(solution)/shard_map/ppermute | solution.py:790
  13.8 0.1 collective-permute-start
  13.9 1.2 %collective-permute-done.refs_1_.refs_2_ = f32[5,16,128]{2,1,0:T(8,128)S(1)} collective-permute-done((f32[5,16,128]{2,1,0:T(8,128)S(1)}, f32[5,16,128]{2,1,0:T(8,128)S(1)}, u32[]{:S(2)}, u32[]{:S(2)}) %collective-permute-start) | collective-permute-done | bytes 40992 | tf_op jit(solution)/shard_map/ppermute | solution.py:795
  15.1 0.9 copy-done.11
  16.0 1.3 %collective-permute-start.1 = (f32[14,16,128]{2,1,0:T(8,128)S(1)}, f32[14,16,128]{2,1,0:T(8,128)S(1)}, u32[]{:S(2)}, u32[]{:S(2)}) collective-permute-start(f32[14,16,128]{2,1,0:T(8,128)S(1)} %get-tuple-element.55), channel_id=1, source_target_pairs={{2,0},{4,2},{6,4},{3,1},{5,3},{7,5},{10,8},{12,10},{14,12},{11,9},... | collective-permute-start | bytes 344072 | tf_op jit(solution)/shard_map/ppermute | solution.py:776
  17.3 0.0 copy-start.20
  17.3 6.3 %collective-permute-start.2 = (f32[14,16,128]{2,1,0:T(8,128)S(1)}, f32[14,16,128]{2,1,0:T(8,128)S(1)}, u32[]{:S(2)}, u32[]{:S(2)}) collective-permute-start(f32[14,16,128]{2,1,0:T(8,128)S(1)} %get-tuple-element.56), channel_id=1, source_target_pairs={{0,2},{2,4},{4,6},{1,3},{3,5},{5,7},{8,10},{10,12},{12,14},{9,11},... | collective-permute-start | bytes 344072 | tf_op jit(solution)/shard_map/ppermute | solution.py:772
  23.6 1.4 %shard_map.174 = (f32[24,2,24,1,128]{4,3,2,1,0:T(1,128)S(1)}, f32[24,2,24,1,128]{4,3,2,1,0:T(1,128)S(1)}, f32[24,2,16,1,128]{4,3,2,1,0:T(1,128)S(1)}, f32[24,2,16,1,128]{4,3,2,1,0:T(1,128)S(1)}) custom-call(f32[24,64,4,1,128]{4,3,2,1,0:T(1,128)S(1)} %bitcast.21, f32[24,2,24,128]{3,2,1,0:T(8,128)S(1)} %bitcast.26), custom_call_target="tpu_custom_call" | custom-call | tf_op jit(solution)/shard_map/pallas_call | solution.py:96
  25.1 7.7 %collective-permute-done.1.refs_5_ = f32[14,16,128]{2,1,0:T(8,128)S(1)} collective-permute-done((f32[14,16,128]{2,1,0:T(8,128)S(1)}, f32[14,16,128]{2,1,0:T(8,128)S(1)}, u32[]{:S(2)}, u32[]{:S(2)}) %collective-permute-start.1) | collective-permute-done | bytes 114720 | tf_op jit(solution)/shard_map/ppermute | solution.py:776
  32.8 3.2 %shard_map.176 = (f32[256,128]{1,0:T(8,128)}, f32[2,16,16,128]{3,2,1,0:T(8,128)S(1)}, f32[4,18,16,128]{3,2,1,0:T(8,128)S(1)}, f32[2,16,16,128]{3,2,1,0:T(8,128)S...) custom-call(f32[24,2,24,128]{3,2,1,0:T(8,128)S(1)} %bitcast.22, f32[4,16,16,128]{3,2,1,0:T(8,128)S(1)} %copy-done.5, ...), custom_call_target="tpu_custom_call" | custom-call | tf_op jit(solution)/shard_map/pallas_call | solution.py:163
  36.0 0.8 copy-done.4
  36.8 0.7 copy-done.6
  37.5 0.7 copy-done.8
  38.2 0.6 copy-done.18
  38.8 3.5 %all-to-all-start = ((f32[4,18,16,128]{3,2,1,0:T(8,128)}), f32[4,18,16,128]{3,2,1,0:T(8,128)S(1)}, u32[]{:S(2)}, u32[]{:S(2)}) async-start(f32[4,18,16,128]{3,2,1,0:T(8,128)} %copy-done.4), calls=%async_computation | async-start | bytes 1179648 | tf_op jit(solution)/shard_map/all_to_all | solution.py:848
  42.3 0.6 shard_map.178.refs_0_.refs_3_.refs_2_
  42.9 1.3 %collective-permute-start.8 = (f32[24,2,24,128]{3,2,1,0:T(8,128)S(1)}, f32[24,2,24,128]{3,2,1,0:T(8,128)}, u32[]{:S(2)}, u32[]{:S(2)}) collective-permute-start(f32[24,2,24,128]{3,2,1,0:T(8,128)S(1)} %get-tuple-element.72.refs_2_.refs_5_), channel_id=1, source_target_pairs={{8,0},{16,8},{24,16},{2,24},{10,2},{18,10},{26,18},{4,26},{12,4},{... | collective-permute-start | bytes 1769480 | tf_op jit(solution)/shard_map/ppermute | solution.py:790
  44.2 5.4 %collective-permute-start.9 = (f32[24,2,24,128]{3,2,1,0:T(8,128)S(1)}, f32[24,2,24,128]{3,2,1,0:T(8,128)}, u32[]{:S(2)}, u32[]{:S(2)}) collective-permute-start(f32[24,2,24,128]{3,2,1,0:T(8,128)S(1)} %get-tuple-element.73.refs_3_.refs_6_), channel_id=1, source_target_pairs={{0,8},{8,16},{16,24},{24,2},{2,10},{10,18},{18,26},{26,4},{4,12},{... | collective-permute-start | bytes 1769480 | tf_op jit(solution)/shard_map/ppermute | solution.py:786
  49.6 4.9 %shard_map.179.refs_9_ = f32[12,24,128]{2,1,0:T(8,128)} custom-call(f32[192,192]{1,0:T(8,128)S(1)} %shard_map.178.refs_0_.refs_3_.refs_2_, f32[24,2,24,128]{3,2,1,0:T(8,128)S(1)} %bitcast.27, f32[24,2,24,128]{3,2,1,0:T(8,128)} %bitcast.12.refs_2_.refs_6_, f32[24,2,24,128]{3,2,1,0:T(8,128)} %collective-permute-done.3.refs_3_.refs_7_, ...), custom_call_target="tpu_custom_call" | custom-call | tf_op jit(solution)/shard_map/pallas_call | solution.py:148
  54.5 6.8 %all-to-all-done.received_ref.refs_3_.refs_4_ = f32[4,18,16,128]{3,2,1,0:T(8,128)S(1)} async-done(((f32[4,18,16,128]{3,2,1,0:T(8,128)}), f32[4,18,16,128]{3,2,1,0:T(8,128)S(1)}, u32[]{:S(2)}, u32[]{:S(2)}) %all-to-all-start) | async-done | bytes 589856 | tf_op jit(solution)/shard_map/all_to_all | solution.py:848
  61.3 0.7 copy-done.16
  62.0 0.7 copy-done.21
  62.7 6.1 %shard_map.180 = (f32[24,4,24,128]{3,2,1,0:T(8,128)S(1)}, f32[4,24,128]{2,1,0:T(8,128)S(1)}, f32[4,4,16,128]{3,2,1,0:T(8,128)}, f32[4,8,128]{2,1,0:T(8,128)S(1)}) custom-call(f32[24]{0:T(128)S(1)} %copy-done.21, f32[4,128]{1,0:T(4,128)S(1)} %bitcast.31, f32[4,32,128]{2,1,0:T(8,128)S(1)} %get-tuple-element.62.refs_0_.refs_2_.refs_4_, ...), custom_call_target="tpu_custom_call" | custom-call | tf_op jit(solution)/shard_map/pallas_call | solution.py:645
  68.8 3.3 %shard_map.181 = (f32[24,256,128]{2,1,0:T(8,128)}, f32[8,128]{1,0:T(8,128)S(1)}) custom-call(f32[24]{0:T(128)S(1)} %copy-done.23, f32[24]{0:T(128)S(1)} %copy-done.25, f32[24]{0:T(128)S(1)} %copy-done.27, f32[192,192]{1,0:T(8,128)S(1)} %shard_map.178.refs_0_.refs_3_.refs_2_, f32[4,32,128]{2,1,0:T(8,128)S(1)} %get-tuple-element.62.refs_0_.refs_2_.refs_4_, ...), custom_call_target="tpu_custom_call" | custom-call | tf_op jit(solution)/shard_map/pallas_call | solution.py:736
  72.1 1.3 %collective-permute-start.6 = (f32[24,2,16,128]{3,2,1,0:T(8,128)S(1)}, f32[24,2,16,128]{3,2,1,0:T(8,128)S(1)}, u32[]{:S(2)}, u32[]{:S(2)}) collective-permute-start(f32[24,2,16,128]{3,2,1,0:T(8,128)S(1)} %get-tuple-element.69.refs_1_.refs_5_), channel_id=1, source_target_pairs={{8,0},{16,8},{24,16},{2,24},{10,2},{18,10},{26,18},{4,26},{12,4},{... | collective-permute-start | bytes 1179656 | tf_op jit(solution)/shard_map/ppermute | solution.py:790
  73.4 4.6 %collective-permute-start.7 = (f32[24,2,16,128]{3,2,1,0:T(8,128)S(1)}, f32[24,2,16,128]{3,2,1,0:T(8,128)S(1)}, u32[]{:S(2)}, u32[]{:S(2)}) collective-permute-start(f32[24,2,16,128]{3,2,1,0:T(8,128)S(1)} %get-tuple-element.70.refs_2_.refs_6_), channel_id=1, source_target_pairs={{0,8},{8,16},{16,24},{24,2},{2,10},{10,18},{18,26},{26,4},{4,12},{... | collective-permute-start | bytes 1179656 | tf_op jit(solution)/shard_map/ppermute | solution.py:786
  78.0 0.8 shard_map.177
  78.8 3.7 %shard_map.184.refs_9_ = f32[12,24,128]{2,1,0:T(8,128)S(1)} custom-call(f32[8,128]{1,0:T(8,128)S(1)} %get-tuple-element.68.refs_2_.refs_0_.refs_14_, f32[8,128]{1,0:T(8,128)S(1)} %get-tuple-element.74.refs_1_, f32[24,2,24,128]{3,2,1,0:T(8,128)S(1)} %get-tuple-element.72.refs_2_.refs_5_, f32[24,2,24,128]{3,2,1,0:T(8,128)S(1)} %get-tuple-element.73.refs_3_.refs_6_, ...), custom_call_target="tpu_custom_call" | custom-call | tf_op jit(solution)/shard_map/pallas_call | solution.py:148
  82.5 0.0 collective-permute-start.10
  82.5 1.4 %collective-permute-done.10.refs_10_.refs_11_ = f32[12,24,128]{2,1,0:T(8,128)S(1)} collective-permute-done((f32[12,24,128]{2,1,0:T(8,128)S(1)}, f32[12,24,128]{2,1,0:T(8,128)S(1)}, u32[]{:S(2)}, u32[]{:S(2)}) %collective-permute-start.10) | collective-permute-done | bytes 147488 | tf_op jit(solution)/shard_map/ppermute | solution.py:795
  83.9 6.1 %shard_map.185 = (f32[24,4,24,128]{3,2,1,0:T(8,128)S(1)}, f32[4,24,128]{2,1,0:T(8,128)S(1)}, f32[4,4,16,128]{3,2,1,0:T(8,128)}, f32[4,8,128]{2,1,0:T(8,128)S(1)}) custom-call(f32[24]{0:T(128)S(1)} %copy-done.22, f32[4,128]{1,0:T(4,128)S(1)} %bitcast.32, ...), custom_call_target="tpu_custom_call", output_to_operand_aliasing={{2}: (13, {})} | custom-call | tf_op jit(solution)/shard_map/pallas_call | solution.py:645
  90.0 0.1 collective-permute-done.7.refs_4_.refs_8_
  90.1 1.1 %shard_map.186.refs_9_ = f32[12,16,128]{2,1,0:T(8,128)S(1)} custom-call(f32[4,8,128]{2,1,0:T(8,128)S(1)} %get-tuple-element.77.refs_0_.refs_12_, f32[24,2,16,128]{3,2,1,0:T(8,128)S(1)} %get-tuple-element.69.refs_1_.refs_5_, f32[24,2,16,128]{3,2,1,0:T(8,128)S(1)} %get-tuple-element.70.refs_2_.refs_6_, ...), custom_call_target="tpu_custom_call" | custom-call | tf_op jit(solution)/shard_map/pallas_call | solution.py:148
  91.3 0.1 collective-permute-start.11
  91.3 3.3 %shard_map.187 = (f32[24,256,128]{2,1,0:T(8,128)}, f32[8,128]{1,0:T(8,128)S(1)}) custom-call(f32[24]{0:T(128)S(1)} %copy-done.23, f32[24]{0:T(128)S(1)} %copy-done.25, f32[24]{0:T(128)S(1)} %copy-done.27, f32[192,192]{1,0:T(8,128)S(1)} %shard_map.178.refs_0_.refs_3_.refs_2_, ...), custom_call_target="tpu_custom_call", output_to_operand_aliasing={{0}: (7, {})} | custom-call | tf_op jit(solution)/shard_map/pallas_call | solution.py:736
  94.6 4.2 %shard_map.188 = (f32[24,4,16,128]{3,2,1,0:T(8,128)S(1)}, f32[4,16,128]{2,1,0:T(8,128)S(1)}, f32[4,4,16,128]{3,2,1,0:T(8,128)}, f32[4,8,128]{2,1,0:T(8,128)}) custom-call(f32[24]{0:T(128)S(1)} %copy-done.22, f32[4,128]{1,0:T(4,128)S(1)} %bitcast.33, f32[4,32,128]{2,1,0:T(8,128)S(1)} %get-tuple-element.62.refs_0_.refs_2_.refs_4_, ...), custom_call_target="tpu_custom_call", output_to_operand_aliasing={{2}: (13, {})} | custom-call | tf_op jit(solution)/shard_map/pallas_call | solution.py:645
  98.8 0.9 copy-done.2
  99.7 6.3 %all-to-all-start.1 = ((f32[4,4,16,128]{3,2,1,0:T(8,128)}), f32[4,4,16,128]{3,2,1,0:T(8,128)S(1)}, u32[]{:S(2)}, u32[]{:S(2)}) async-start(f32[4,4,16,128]{3,2,1,0:T(8,128)} %get-tuple-element.83), calls=%async_computation.1 | async-start | bytes 262144 | tf_op jit(solution)/shard_map/all_to_all | solution.py:894
  106.1 1.1 %copy-done.3 = f32[24,4,16,128]{3,2,1,0:T(8,128)S(1)} copy-done((f32[24,4,16,128]{3,2,1,0:T(8,128)S(1)}, f32[24,4,16,128]{3,2,1,0:T(8,128)}, u32[]{:S(2)}) %copy-start.3) | copy-done | bytes 786456
  107.2 2.5 %shard_map.190 = (f32[24,256,128]{2,1,0:T(8,128)}, f32[8,128]{1,0:T(8,128)}) custom-call(f32[24]{0:T(128)S(1)} %copy-done.24, f32[24]{0:T(128)S(1)} %copy-done.26, f32[24]{0:T(128)S(1)} %copy-done.28, f32[192,192]{1,0:T(8,128)S(1)} %shard_map.178.refs_0_.refs_3_.refs_2_, ...), custom_call_target="tpu_custom_call", output_to_operand_aliasing={{0}: (7, {})} | custom-call | tf_op jit(solution)/shard_map/pallas_call | solution.py:736
  109.7 1.4 %all-to-all-done.1.refs_2_ = f32[4,4,16,128]{3,2,1,0:T(8,128)S(1)} async-done(((f32[4,4,16,128]{3,2,1,0:T(8,128)}), f32[4,4,16,128]{3,2,1,0:T(8,128)S(1)}, u32[]{:S(2)}, u32[]{:S(2)}) %all-to-all-start.1) | async-done | bytes 131104 | tf_op jit(solution)/shard_map/all_to_all | solution.py:894
  111.1 0.8 shard_map.189
  (57 shorter events, 0.1 us)
Async XLA Ops:
  0.6 32.1 %copy-start.12 = (s32[16,128]{1,0:T(8,128)S(1)}, s32[16,128]{1,0:T(8,128)}, u32[]{:S(2)}) copy-start(s32[16,128]{1,0:T(8,128)} %refs_0_.12) | copy-start | bytes 24580
  0.6 32.1 %copy-start.14 = (s32[16,128]{1,0:T(8,128)S(1)}, s32[16,128]{1,0:T(8,128)}, u32[]{:S(2)}) copy-start(s32[16,128]{1,0:T(8,128)} %refs_1_.8) | copy-start | bytes 24580
  2.8 1.9 %copy-start = (f32[24,64,1,1,4,128]{5,4,3,2,1,0:T(4,128)S(1)}, f32[24,64,1,1,4,128]{5,4,3,2,1,0:T(4,128)}, u32[]{:S(2)}) copy-start(f32[24,64,1,1,4,128]{5,4,3,2,1,0:T(4,128)} %param.19) | copy-start | bytes 9437188
  4.7 0.8 copy-start.10
  5.5 18.2 %copy-start.1 = (f32[24,64,1,1,4,128]{5,4,3,2,1,0:T(4,128)S(1)}, f32[24,64,1,1,4,128]{5,4,3,2,1,0:T(4,128)}, u32[]{:S(2)}) copy-start(f32[24,64,1,1,4,128]{5,4,3,2,1,0:T(4,128)} %param.19) | copy-start | bytes 9437188
  5.5 27.3 %copy-start.5 = (f32[4,16,16,128]{3,2,1,0:T(8,128)S(1)}, f32[4,16,16,128]{3,2,1,0:T(8,128)}, u32[]{:S(2)}) copy-start(f32[4,16,16,128]{3,2,1,0:T(8,128)} %get-tuple-element.52.refs_1_) | copy-start | bytes 1572868
  6.7 42.9 %collective-permute-start.4 = (f32[24,2,24,128]{3,2,1,0:T(8,128)}, f32[24,2,24,128]{3,2,1,0:T(8,128)}, u32[]{:S(2)}, u32[]{:S(2)}) collective-permute-start(f32[24,2,24,128]{3,2,1,0:T(8,128)} %bitcast.12.refs_2_.refs_6_), channel_id=1, source_target_pairs={{0,8},{8,16},{16,24},{24,2},{2,10},{10,18},{18,26},{26,4},{4,12},{... | collective-permute-start | bytes 1769480 | tf_op jit(solution)/shard_map/ppermute | solution.py:786
  12.5 37.1 %collective-permute-start.3 = (f32[24,2,24,128]{3,2,1,0:T(8,128)S(1)}, f32[24,2,24,128]{3,2,1,0:T(8,128)}, u32[]{:S(2)}, u32[]{:S(2)}) collective-permute-start(f32[24,2,24,128]{3,2,1,0:T(8,128)S(1)} %bitcast.25), channel_id=1, source_target_pairs={{8,0},{16,8},{24,16},{2,24},{10,2},{18,10},{26,18},{4,26},{12,4},{... | collective-permute-start | bytes 1769480 | tf_op jit(solution)/shard_map/ppermute | solution.py:790
  13.8 1.3 %collective-permute-start = (f32[5,16,128]{2,1,0:T(8,128)S(1)}, f32[5,16,128]{2,1,0:T(8,128)S(1)}, u32[]{:S(2)}, u32[]{:S(2)}) collective-permute-start(f32[5,16,128]{2,1,0:T(8,128)S(1)} %copy-done.10), channel_id=1, source_target_pairs={{0,1},{1,0},{2,3},{3,2},{4,5},{5,4},{6,7},{7,6},{8,9},{9,8},{10,11... | collective-permute-start | bytes 122888 | tf_op jit(solution)/shard_map/ppermute | solution.py:795
  15.1 0.9 copy-start.11
  16.0 16.8 %collective-permute-start.1 = (f32[14,16,128]{2,1,0:T(8,128)S(1)}, f32[14,16,128]{2,1,0:T(8,128)S(1)}, u32[]{:S(2)}, u32[]{:S(2)}) collective-permute-start(f32[14,16,128]{2,1,0:T(8,128)S(1)} %get-tuple-element.55), channel_id=1, source_target_pairs={{2,0},{4,2},{6,4},{3,1},{5,3},{7,5},{10,8},{12,10},{14,12},{11,9},... | collective-permute-start | bytes 344072 | tf_op jit(solution)/shard_map/ppermute | solution.py:776
  17.3 25.0 %copy-start.20 = (f32[24,24]{1,0:T(8,128)S(1)}, f32[24,24]{1,0:T(8,128)}, u32[]{:S(2)}) copy-start(f32[24,24]{1,0:T(8,128)} %refs_1_.5) | copy-start | bytes 6916
  17.3 15.4 %collective-permute-start.2 = (f32[14,16,128]{2,1,0:T(8,128)S(1)}, f32[14,16,128]{2,1,0:T(8,128)S(1)}, u32[]{:S(2)}, u32[]{:S(2)}) collective-permute-start(f32[14,16,128]{2,1,0:T(8,128)S(1)} %get-tuple-element.56), channel_id=1, source_target_pairs={{0,2},{2,4},{4,6},{1,3},{3,5},{5,7},{8,10},{10,12},{12,14},{9,11},... | collective-permute-start | bytes 344072 | tf_op jit(solution)/shard_map/ppermute | solution.py:772
  36.0 0.8 copy-start.4
  36.8 0.7 copy-start.6
  37.5 0.7 copy-start.8
  38.2 0.6 copy-start.18
  38.8 22.5 %all-to-all-start = ((f32[4,18,16,128]{3,2,1,0:T(8,128)}), f32[4,18,16,128]{3,2,1,0:T(8,128)S(1)}, u32[]{:S(2)}, u32[]{:S(2)}) async-start(f32[4,18,16,128]{3,2,1,0:T(8,128)} %copy-done.4), calls=%async_computation | async-start | bytes 1179648 | tf_op jit(solution)/shard_map/all_to_all | solution.py:848
  42.9 35.8 %collective-permute-start.8 = (f32[24,2,24,128]{3,2,1,0:T(8,128)S(1)}, f32[24,2,24,128]{3,2,1,0:T(8,128)}, u32[]{:S(2)}, u32[]{:S(2)}) collective-permute-start(f32[24,2,24,128]{3,2,1,0:T(8,128)S(1)} %get-tuple-element.72.refs_2_.refs_5_), channel_id=1, source_target_pairs={{8,0},{16,8},{24,16},{2,24},{10,2},{18,10},{26,18},{4,26},{12,4},{... | collective-permute-start | bytes 1769480 | tf_op jit(solution)/shard_map/ppermute | solution.py:790
  44.2 34.5 %collective-permute-start.9 = (f32[24,2,24,128]{3,2,1,0:T(8,128)S(1)}, f32[24,2,24,128]{3,2,1,0:T(8,128)}, u32[]{:S(2)}, u32[]{:S(2)}) collective-permute-start(f32[24,2,24,128]{3,2,1,0:T(8,128)S(1)} %get-tuple-element.73.refs_3_.refs_6_), channel_id=1, source_target_pairs={{0,8},{8,16},{16,24},{24,2},{2,10},{10,18},{18,26},{26,4},{4,12},{... | collective-permute-start | bytes 1769480 | tf_op jit(solution)/shard_map/ppermute | solution.py:786
  54.5 6.8 %collective-permute-start.5 = (f32[12,24,128]{2,1,0:T(8,128)}, f32[12,24,128]{2,1,0:T(8,128)S(1)}, u32[]{:S(2)}, u32[]{:S(2)}) collective-permute-start(f32[12,24,128]{2,1,0:T(8,128)} %shard_map.179.refs_9_), channel_id=1, source_target_pairs={{0,1},{1,0},{2,3},{3,2},{4,5},{5,4},{6,7},{7,6},{8,9},{9,8},{10,11... | collective-permute-start | bytes 442376 | tf_op jit(solution)/shard_map/ppermute | solution.py:795
  61.3 7.5 %copy-start.23 = (f32[24]{0:T(128)S(1)}, f32[24]{0:T(128)}, u32[]{:S(2)}) copy-start(f32[24]{0:T(128)} %refs_0_.13) | copy-start | bytes 292
  61.3 7.5 %copy-start.25 = (f32[24]{0:T(128)S(1)}, f32[24]{0:T(128)}, u32[]{:S(2)}) copy-start(f32[24]{0:T(128)} %refs_1_.9) | copy-start | bytes 292
  61.3 7.6 %copy-start.27 = (f32[24]{0:T(128)S(1)}, f32[24]{0:T(128)}, u32[]{:S(2)}) copy-start(f32[24]{0:T(128)} %refs_2_.7) | copy-start | bytes 292
  61.3 0.7 copy-start.16
  62.0 0.7 copy-start.21
  62.7 15.3 %copy-start.9 = (f32[2,16,16,128]{3,2,1,0:T(8,128)S(1)}, f32[2,16,16,128]{3,2,1,0:T(8,128)}, u32[]{:S(2)}) copy-start(f32[2,16,16,128]{3,2,1,0:T(8,128)} %copy-done.8) | copy-start | bytes 786436
  62.7 15.3 %copy-start.19 = (f32[2,16,128]{2,1,0:T(8,128)S(1)}, f32[2,16,128]{2,1,0:T(8,128)}, u32[]{:S(2)}) copy-start(f32[2,16,128]{2,1,0:T(8,128)} %copy-done.18) | copy-start | bytes 49156
  68.8 15.1 %copy-start.17 = (f32[1,1,4,128]{3,2,1,0:T(4,128)S(1)}, f32[1,1,4,128]{3,2,1,0:T(4,128)}, u32[]{:S(2)}) copy-start(f32[1,1,4,128]{3,2,1,0:T(4,128)} %param.20) | copy-start | bytes 6148
  68.8 15.1 %copy-start.22 = (f32[24]{0:T(128)S(1)}, f32[24]{0:T(128)}, u32[]{:S(2)}) copy-start(f32[24]{0:T(128)} %refs_0_.11) | copy-start | bytes 292
  72.1 17.9 %collective-permute-start.6 = (f32[24,2,16,128]{3,2,1,0:T(8,128)S(1)}, f32[24,2,16,128]{3,2,1,0:T(8,128)S(1)}, u32[]{:S(2)}, u32[]{:S(2)}) collective-permute-start(f32[24,2,16,128]{3,2,1,0:T(8,128)S(1)} %get-tuple-element.69.refs_1_.refs_5_), channel_id=1, source_target_pairs={{8,0},{16,8},{24,16},{2,24},{10,2},{18,10},{26,18},{4,26},{12,4},{... | collective-permute-start | bytes 1179656 | tf_op jit(solution)/shard_map/ppermute | solution.py:790
  73.4 16.7 %collective-permute-start.7 = (f32[24,2,16,128]{3,2,1,0:T(8,128)S(1)}, f32[24,2,16,128]{3,2,1,0:T(8,128)S(1)}, u32[]{:S(2)}, u32[]{:S(2)}) collective-permute-start(f32[24,2,16,128]{3,2,1,0:T(8,128)S(1)} %get-tuple-element.70.refs_2_.refs_6_), channel_id=1, source_target_pairs={{0,8},{8,16},{16,24},{24,2},{2,10},{10,18},{18,26},{26,4},{4,12},{... | collective-permute-start | bytes 1179656 | tf_op jit(solution)/shard_map/ppermute | solution.py:786
  82.5 1.4 %collective-permute-start.10 = (f32[12,24,128]{2,1,0:T(8,128)S(1)}, f32[12,24,128]{2,1,0:T(8,128)S(1)}, u32[]{:S(2)}, u32[]{:S(2)}) collective-permute-start(f32[12,24,128]{2,1,0:T(8,128)S(1)} %shard_map.184.refs_9_), channel_id=1, source_target_pairs={{0,1},{1,0},{2,3},{3,2},{4,5},{5,4},{6,7},{7,6},{8,9},{9,8},{10,11... | collective-permute-start | bytes 442376 | tf_op jit(solution)/shard_map/ppermute | solution.py:795
  91.3 3.4 %collective-permute-start.11 = (f32[12,16,128]{2,1,0:T(8,128)S(1)}, f32[12,16,128]{2,1,0:T(8,128)S(1)}, u32[]{:S(2)}, u32[]{:S(2)}) collective-permute-start(f32[12,16,128]{2,1,0:T(8,128)S(1)} %shard_map.186.refs_9_), channel_id=1, source_target_pairs={{0,1},{1,0},{2,3},{3,2},{4,5},{5,4},{6,7},{7,6},{8,9},{9,8},{10,11... | collective-permute-start | bytes 294920 | tf_op jit(solution)/shard_map/ppermute | solution.py:795
  91.3 14.7 %copy-start.24 = (f32[24]{0:T(128)S(1)}, f32[24]{0:T(128)}, u32[]{:S(2)}) copy-start(f32[24]{0:T(128)} %refs_0_.13) | copy-start | bytes 292
  91.3 14.7 %copy-start.26 = (f32[24]{0:T(128)S(1)}, f32[24]{0:T(128)}, u32[]{:S(2)}) copy-start(f32[24]{0:T(128)} %refs_1_.9) | copy-start | bytes 292
  91.3 14.7 %copy-start.28 = (f32[24]{0:T(128)S(1)}, f32[24]{0:T(128)}, u32[]{:S(2)}) copy-start(f32[24]{0:T(128)} %refs_2_.7) | copy-start | bytes 292
  94.6 16.4 %copy-start.7 = (f32[2,16,16,128]{3,2,1,0:T(8,128)S(1)}, f32[2,16,16,128]{3,2,1,0:T(8,128)}, u32[]{:S(2)}) copy-start(f32[2,16,16,128]{3,2,1,0:T(8,128)} %copy-done.6) | copy-start | bytes 786436
  94.6 16.4 %copy-start.13 = (s32[16,128]{1,0:T(8,128)S(1)}, s32[16,128]{1,0:T(8,128)}, u32[]{:S(2)}) copy-start(s32[16,128]{1,0:T(8,128)} %refs_0_.12) | copy-start | bytes 24580
  94.6 16.4 %copy-start.15 = (s32[16,128]{1,0:T(8,128)S(1)}, s32[16,128]{1,0:T(8,128)}, u32[]{:S(2)}) copy-start(s32[16,128]{1,0:T(8,128)} %refs_1_.8) | copy-start | bytes 24580
  98.8 0.9 copy-start.2
  99.7 11.3 %all-to-all-start.1 = ((f32[4,4,16,128]{3,2,1,0:T(8,128)}), f32[4,4,16,128]{3,2,1,0:T(8,128)S(1)}, u32[]{:S(2)}, u32[]{:S(2)}) async-start(f32[4,4,16,128]{3,2,1,0:T(8,128)} %get-tuple-element.83), calls=%async_computation.1 | async-start | bytes 262144 | tf_op jit(solution)/shard_map/all_to_all | solution.py:894
  106.0 1.1 %copy-start.3 = (f32[24,4,16,128]{3,2,1,0:T(8,128)S(1)}, f32[24,4,16,128]{3,2,1,0:T(8,128)}, u32[]{:S(2)}) copy-start(f32[24,4,16,128]{3,2,1,0:T(8,128)} %copy-done.2) | copy-start | bytes 2359300

commit v4 on v2

--- a/solution.py
+++ b/solution.py
@@ -406,9 +406,10 @@
     )
 
 
-def velocity_kernel(local_ref, faces_ref, received_ref, east_ref, north_ref):
+def velocity_kernel(local_ref, faces_ref, received_ref, east_ref, north_ref, token_ref):
     blocks = received_ref.shape[0]
     _, tile_rows, levels, cols = local_ref.shape
+    token_ref[...] = jnp.zeros_like(token_ref)
     group = lax.axis_index("comp")
     level = (group * levels + subs_of((levels, cols))).astype(jnp.float32)
     for f, out_ref in enumerate((east_ref, north_ref)):
@@ -433,8 +434,8 @@
             whole(faces.shape),
             pl.BlockSpec((blocks, 2, levels, cols), lambda i: (0, ENTRIES // 2 - 1, 0, 0)),
         ],
-        out_specs=[whole(out.shape)] * 2,
-        out_shape=[out] * 2,
+        out_specs=[whole(out.shape)] * 2 + [whole((SUB, cols))],
+        out_shape=[out] * 2 + [shaped(SUB, cols)],
         compiler_params=params(),
     )(local, faces, received)
 
@@ -817,7 +818,7 @@
     q = dissolved_species.reshape(tracer_count, level_count, sub_rows, 1, tile_cols)
     parts = levels // SUB
     every = parts * blocks
-    sizes = [every - 5 * every // 8, every // 4, every // 4, every // 8]
+    sizes = [every - 5 * every // 8, 3 * every // 8, every // 4]
     cuts = [(sum(sizes[:i]), size) for i, size in enumerate(sizes)]
     scalars_of_uptake = (
         peak_intake_speed,
@@ -833,7 +834,7 @@
 
     packed, edges, ocean_rows = pack_ocean(flat, sea, levels)
     ranges = [(first * SUB, size * SUB) for first, size in cuts]
-    chunks = [rims(cut_rows(q, ranges[:1], [packed]))]
+    chunks = [rims(cut_rows(q, ranges[:1], []))]
     later = cut_rows(q, ranges[1:], chunks[0][0][:1])
     up, down, packed = ocean_sides(packed, *from_sides(packed), edges)
     after, before = from_after(up, "gx"), from_before(down, "gx")
@@ -841,7 +842,7 @@
         blocks, levels, ocean_rows, sea, packed, after, before, later[:1]
     )
     received = lax.all_to_all(send, "comp", split_axis=0, concat_axis=0, tiled=True)
-    east_new, north_new = velocities(local, faces, received)
+    east_new, north_new, finished = velocities(local, faces, received)
     matrix = call_once(
         spread_kernel,
         [stoichiometry_matrix],
@@ -867,7 +868,7 @@
             near,
             carry,
             heat,
-            [] if i == 0 else [token],
+            [] if i == 0 else [token, finished],
         )
         if i > 0 and i + 1 < len(cuts):
             near = sides(pack_tracers(*chunks[i + 1], [carry]))

time: 117 us -> 110 us (0.940); the launches traced: 116 us -> 107 us
  starting transfers between devices: 43 us -> 34.9 us
  Pallas kernels: 44.7 us -> 42.1 us
  waiting for transfers between devices: 19.5 us -> 21.1 us
    ppermute x1, waiting for transfers between devices: 7.67 us -> 2.79 us  [from_after(): lax.ppermute(x, axis, [(i + 1, i) for i in range(lax.axis_size(axis) - 1)])]
    ppermute x4 -> x3, starting transfers between devices: 20.2 us -> 15.8 us  [from_block_before(): return lax.ppermute(x, ('comp', 'gx'), row_pairs())]
    ppermute x4 -> x3, waiting for transfers between devices: 1.9 us -> 6.05 us  [from_block_before(): return lax.ppermute(x, ('comp', 'gx'), row_pairs())]
    all_to_all x1, waiting for transfers between devices: 3.77 us -> 7.75 us  [on_device(): lax.all_to_all(send, 'comp', split_axis=0, concat_axis=0, tiled=True)]
    all_to_all x1, starting transfers between devices: 6.34 us -> 4.01 us  [on_device(): heat = lax.all_to_all(heat, 'comp', split_axis=0, concat_axis=0, tiled=True)]
    pallas_call x4 -> x3, Pallas kernels: 17.2 us -> 15.2 us  [advection(): pl.pallas_call(functools.partial(advection_kernel, first_part, parts, lev...]
    ppermute x5 -> x4, waiting for transfers between devices: 3.79 us -> 2 us  [from_sides(): other = lax.ppermute(x, 'gy', [(0, 1), (1, 0)])]
    ppermute x4 -> x3, starting transfers between devices: 5.13 us -> 3.85 us  [from_block_after(): lax.ppermute(x, ('comp', 'gx'), [(later, own) for own, later in row_pairs...]
  transfers between devices with their start and end apart: 17 -> 14, of which waited for: 7 -> 6; matrix products, arithmetic and copies ran while one was open for 0% -> 0% of each run, Pallas kernels for 32% -> 32%
where the time goes in v4:
time: 110 us; the launch traced here: 107 us
  Pallas kernels  42.1 us (38%)
  starting transfers between devices  34.9 us (32%)
  waiting for transfers between devices  21.1 us (19%)
  local copies, waits for them, and re-layouts  8.36 us (8%)
    ppermute x3, starting transfers between devices, from_block_before(): return lax.ppermute(x, ('comp', 'gx'), row_pairs())  15.8 us
    pallas_call x3, Pallas kernels, advection(): pl.pallas_call(functools.partial(advection_kernel, first_part, parts, lev...  15.2 us
    pallas_call x3, Pallas kernels, uptake(): pl.pallas_call(functools.partial(uptake_kernel, first_part * SUB), grid=(...  9.04 us
    unnamed x38, local copies, waits for them, and re-layouts  8.36 us
    all_to_all x1, waiting for transfers between devices, on_device(): lax.all_to_all(send, 'comp', split_axis=0, concat_axis=0, tiled=True)  7.75 us
    pallas_call x3, Pallas kernels, pack_tracers(): pl.pallas_call(functools.partial(ignoring, len(after), pack_tracers_kerne...  7.66 us
    pallas_call x5, Pallas kernels, call_once(): pl.pallas_call(functools.partial(ignoring, len(after), kernel), grid=(1,)...  6.75 us
    ppermute x1, starting transfers between devices, from_before(): lax.ppermute(x, axis, [(i, i + 1) for i in range(lax.axis_size(axis) - 1)])  6.24 us
  transfers between devices with their start and end apart: 14, of which 6 were waited for; matrix products, arithmetic and copies ran while one was open for 0% of the time, Pallas kernels for 32%

profile of v4, /device:TPU:0, one launch (start us, length us, event | category | flops | bytes accessed | tf_op | source)
XLA Modules:
  0.0 107.4 jit_solution(9475390614263269182)
XLA Ops:
  0.6 0.0 copy-start
  0.6 1.9 %copy-done = f32[24,64,1,1,4,128]{5,4,3,2,1,0:T(4,128)S(1)} copy-done((f32[24,64,1,1,4,128]{5,4,3,2,1,0:T(4,128)S(1)}, f32[24,64,1,1,4,128]{5,4,3,2,1,0:T(4,128)}, u32[]{:S(2)}) %copy-start) | copy-done | bytes 3145752
  2.5 1.2 %shard_map.172 = (f32[24,2,24,1,128]{4,3,2,1,0:T(1,128)S(1)}, f32[24,2,24,1,128]{4,3,2,1,0:T(1,128)}) custom-call(f32[24,64,4,1,128]{4,3,2,1,0:T(1,128)S(1)} %bitcast.20), custom_call_target="tpu_custom_call" | custom-call | tf_op jit(solution)/shard_map/pallas_call | solution.py:96
  3.8 5.7 %collective-permute-start.4 = (f32[24,2,24,128]{3,2,1,0:T(8,128)}, f32[24,2,24,128]{3,2,1,0:T(8,128)}, u32[]{:S(2)}, u32[]{:S(2)}) collective-permute-start(f32[24,2,24,128]{3,2,1,0:T(8,128)} %bitcast.12.refs_2_.refs_6_), channel_id=1, source_target_pairs={{0,8},{8,16},{16,24},{24,2},{2,10},{10,18},{18,26},{26,4},{4,12},{... | collective-permute-start | bytes 1769480 | tf_op jit(solution)/shard_map/ppermute | solution.py:782
  9.5 1.3 %collective-permute-start.3 = (f32[24,2,24,128]{3,2,1,0:T(8,128)S(1)}, f32[24,2,24,128]{3,2,1,0:T(8,128)}, u32[]{:S(2)}, u32[]{:S(2)}) collective-permute-start(f32[24,2,24,128]{3,2,1,0:T(8,128)S(1)} %bitcast.24), channel_id=1, source_target_pairs={{8,0},{16,8},{24,16},{2,24},{10,2},{18,10},{26,18},{4,26},{12,4},{... | collective-permute-start | bytes 1769480 | tf_op jit(solution)/shard_map/ppermute | solution.py:786
  10.8 2.1 %shard_map.174 = (f32[5,16,128]{2,1,0:T(8,128)}, f32[2,9,16,128]{3,2,1,0:T(8,128)}, f32[4,16,16,128]{3,2,1,0:T(8,128)}) custom-call(f32[256,128]{1,0:T(8,128)} %bitcast.35, f32[256,128]{1,0:T(8,128)} %bitcast.36, f32[256,128]{1,0:T(8,128)} %bitcast.37, f32[256,128]{1,0:T(8,128)} %bitcast.38, s32[16,128]{1,0:T(8,128)} %refs_0_.12, s32[16,128]{1,0:T(8,128)} %refs_1_.8), custom_call_target="tpu_custom_call" | custom-call | tf_op jit(solution)/shard_map/pallas_call | solution.py:159
  12.9 1.4 %collective-permute-done.refs_1_.refs_2_ = f32[5,16,128]{2,1,0:T(8,128)S(1)} collective-permute-done((f32[5,16,128]{2,1,0:T(8,128)}, f32[5,16,128]{2,1,0:T(8,128)S(1)}, u32[]{:S(2)}, u32[]{:S(2)}) %collective-permute-start) | collective-permute-done | bytes 40992 | tf_op jit(solution)/shard_map/ppermute | solution.py:791
  14.3 0.9 copy-done.9
  15.2 0.8 copy-done.12
  16.0 1.3 %collective-permute-start.1 = (f32[14,16,128]{2,1,0:T(8,128)S(1)}, f32[14,16,128]{2,1,0:T(8,128)S(1)}, u32[]{:S(2)}, u32[]{:S(2)}) collective-permute-start(f32[14,16,128]{2,1,0:T(8,128)S(1)} %get-tuple-element.55), channel_id=1, source_target_pairs={{2,0},{4,2},{6,4},{3,1},{5,3},{7,5},{10,8},{12,10},{14,12},{11,9},... | collective-permute-start | bytes 344072 | tf_op jit(solution)/shard_map/ppermute | solution.py:772
  17.3 6.2 %collective-permute-start.2 = (f32[14,16,128]{2,1,0:T(8,128)S(1)}, f32[14,16,128]{2,1,0:T(8,128)S(1)}, u32[]{:S(2)}, u32[]{:S(2)}) collective-permute-start(f32[14,16,128]{2,1,0:T(8,128)S(1)} %get-tuple-element.56), channel_id=1, source_target_pairs={{0,2},{2,4},{4,6},{1,3},{3,5},{5,7},{8,10},{10,12},{12,14},{9,11},... | collective-permute-start | bytes 344072 | tf_op jit(solution)/shard_map/ppermute | solution.py:768
  23.6 0.0 copy-start.1
  23.6 1.9 %copy-done.1 = f32[24,64,1,1,4,128]{5,4,3,2,1,0:T(4,128)S(1)} copy-done((f32[24,64,1,1,4,128]{5,4,3,2,1,0:T(4,128)S(1)}, f32[24,64,1,1,4,128]{5,4,3,2,1,0:T(4,128)}, u32[]{:S(2)}) %copy-start.1) | copy-done | bytes 3145752
  25.5 1.4 %shard_map.173 = (f32[24,2,24,1,128]{4,3,2,1,0:T(1,128)S(1)}, f32[24,2,24,1,128]{4,3,2,1,0:T(1,128)S(1)}, f32[24,2,16,1,128]{4,3,2,1,0:T(1,128)S(1)}, f32[24,2,16,1,128]{4,3,2,1,0:T(1,128)S(1)}) custom-call(f32[24,64,4,1,128]{4,3,2,1,0:T(1,128)S(1)} %bitcast.21, f32[24,2,24,128]{3,2,1,0:T(8,128)S(1)} %bitcast.25), custom_call_target="tpu_custom_call" | custom-call | tf_op jit(solution)/shard_map/pallas_call | solution.py:96
  26.9 2.8 %collective-permute-done.1.refs_5_ = f32[14,16,128]{2,1,0:T(8,128)S(1)} collective-permute-done((f32[14,16,128]{2,1,0:T(8,128)S(1)}, f32[14,16,128]{2,1,0:T(8,128)S(1)}, u32[]{:S(2)}, u32[]{:S(2)}) %collective-permute-start.1) | collective-permute-done | bytes 114720 | tf_op jit(solution)/shard_map/ppermute | solution.py:772
  29.7 0.0 copy-start.13
  29.7 0.0 copy-start.15
  29.8 3.2 %shard_map.176 = (f32[256,128]{1,0:T(8,128)}, f32[2,16,16,128]{3,2,1,0:T(8,128)S(1)}, f32[4,18,16,128]{3,2,1,0:T(8,128)S(1)}, f32[2,16,16,128]{3,2,1,0:T(8,128)S...) custom-call(f32[24,2,24,128]{3,2,1,0:T(8,128)S(1)} %bitcast.22, f32[4,16,16,128]{3,2,1,0:T(8,128)S(1)} %copy-done.4, ...), custom_call_target="tpu_custom_call" | custom-call | tf_op jit(solution)/shard_map/pallas_call | solution.py:159
  32.9 0.8 copy-done.3
  33.7 0.7 copy-done.5
  34.4 0.7 copy-done.7
  35.1 3.5 %all-to-all-start = ((f32[4,18,16,128]{3,2,1,0:T(8,128)}), f32[4,18,16,128]{3,2,1,0:T(8,128)S(1)}, u32[]{:S(2)}, u32[]{:S(2)}) async-start(f32[4,18,16,128]{3,2,1,0:T(8,128)} %copy-done.3), calls=%async_computation | async-start | bytes 1179648 | tf_op jit(solution)/shard_map/all_to_all | solution.py:844
  38.6 0.6 shard_map.178.refs_0_.refs_3_.refs_2_
  39.3 1.3 %collective-permute-start.8 = (f32[24,2,24,128]{3,2,1,0:T(8,128)S(1)}, f32[24,2,24,128]{3,2,1,0:T(8,128)}, u32[]{:S(2)}, u32[]{:S(2)}) collective-permute-start(f32[24,2,24,128]{3,2,1,0:T(8,128)S(1)} %get-tuple-element.72.refs_1_.refs_5_), channel_id=1, source_target_pairs={{8,0},{16,8},{24,16},{2,24},{10,2},{18,10},{26,18},{4,26},{12,4},{... | collective-permute-start | bytes 1769480 | tf_op jit(solution)/shard_map/ppermute | solution.py:786
  40.6 0.0 copy-start.16
  40.6 0.0 copy-start.17
  40.6 5.5 %collective-permute-start.9 = (f32[24,2,24,128]{3,2,1,0:T(8,128)S(1)}, f32[24,2,24,128]{3,2,1,0:T(8,128)}, u32[]{:S(2)}, u32[]{:S(2)}) collective-permute-start(f32[24,2,24,128]{3,2,1,0:T(8,128)S(1)} %get-tuple-element.73.refs_2_.refs_6_), channel_id=1, source_target_pairs={{0,8},{8,16},{16,24},{24,2},{2,10},{10,18},{18,26},{26,4},{4,12},{... | collective-permute-start | bytes 1769480 | tf_op jit(solution)/shard_map/ppermute | solution.py:782
  46.1 3.7 %shard_map.179.refs_9_ = f32[12,24,128]{2,1,0:T(8,128)} custom-call(f32[192,192]{1,0:T(8,128)S(1)} %shard_map.178.refs_0_.refs_3_.refs_2_, f32[24,2,24,128]{3,2,1,0:T(8,128)S(1)} %bitcast.26, f32[24,2,24,128]{3,2,1,0:T(8,128)} %bitcast.12.refs_2_.refs_6_, f32[24,2,24,128]{3,2,1,0:T(8,128)} %collective-permute-done.3.refs_3_.refs_7_, ...), custom_call_target="tpu_custom_call" | custom-call | tf_op jit(solution)/shard_map/pallas_call | solution.py:144
  49.9 7.7 %all-to-all-done.received_ref.refs_3_.refs_4_ = f32[4,18,16,128]{3,2,1,0:T(8,128)S(1)} async-done(((f32[4,18,16,128]{3,2,1,0:T(8,128)}), f32[4,18,16,128]{3,2,1,0:T(8,128)S(1)}, u32[]{:S(2)}, u32[]{:S(2)}) %all-to-all-start) | async-done | bytes 589856 | tf_op jit(solution)/shard_map/all_to_all | solution.py:844
  57.6 5.6 %shard_map.180 = (f32[24,4,24,128]{3,2,1,0:T(8,128)S(1)}, f32[4,24,128]{2,1,0:T(8,128)S(1)}, f32[4,4,16,128]{3,2,1,0:T(8,128)S(1)}, f32[4,8,128]{2,1,0:T(8,128)S(1)}) custom-call(f32[24]{0:T(128)S(1)} %copy-done.15, f32[4,128]{1,0:T(4,128)S(1)} %bitcast.31, f32[4,32,128]{2,1,0:T(8,128)S(1)} %get-tuple-element.62.refs_0_.refs_2_.refs_4_, ...), custom_call_target="tpu_custom_call" | custom-call | tf_op jit(solution)/shard_map/pallas_call | solution.py:641
  63.2 3.3 %shard_map.181 = (f32[24,256,128]{2,1,0:T(8,128)}, f32[8,128]{1,0:T(8,128)S(1)}) custom-call(f32[24]{0:T(128)S(1)} %copy-done.16, f32[24]{0:T(128)S(1)} %copy-done.17, f32[24]{0:T(128)S(1)} %copy-done.18, f32[192,192]{1,0:T(8,128)S(1)} %shard_map.178.refs_0_.refs_3_.refs_2_, f32[4,32,128]{2,1,0:T(8,128)S(1)} %get-tuple-element.62.refs_0_.refs_2_.refs_4_, ...), custom_call_target="tpu_custom_call" | custom-call | tf_op jit(solution)/shard_map/pallas_call | solution.py:732
  66.5 1.3 %collective-permute-start.6 = (f32[24,2,16,128]{3,2,1,0:T(8,128)S(1)}, f32[24,2,16,128]{3,2,1,0:T(8,128)S(1)}, u32[]{:S(2)}, u32[]{:S(2)}) collective-permute-start(f32[24,2,16,128]{3,2,1,0:T(8,128)S(1)} %get-tuple-element.69.refs_1_.refs_5_), channel_id=1, source_target_pairs={{8,0},{16,8},{24,16},{2,24},{10,2},{18,10},{26,18},{4,26},{12,4},{... | collective-permute-start | bytes 1179656 | tf_op jit(solution)/shard_map/ppermute | solution.py:786
  67.8 4.6 %collective-permute-start.7 = (f32[24,2,16,128]{3,2,1,0:T(8,128)S(1)}, f32[24,2,16,128]{3,2,1,0:T(8,128)S(1)}, u32[]{:S(2)}, u32[]{:S(2)}) collective-permute-start(f32[24,2,16,128]{3,2,1,0:T(8,128)S(1)} %get-tuple-element.70.refs_2_.refs_6_), channel_id=1, source_target_pairs={{0,8},{8,16},{16,24},{24,2},{2,10},{10,18},{18,26},{26,4},{4,12},{... | collective-permute-start | bytes 1179656 | tf_op jit(solution)/shard_map/ppermute | solution.py:782
  72.4 6.0 %collective-permute-done.9.refs_4_.refs_8_ = f32[24,2,24,128]{3,2,1,0:T(8,128)} collective-permute-done((f32[24,2,24,128]{3,2,1,0:T(8,128)S(1)}, f32[24,2,24,128]{3,2,1,0:T(8,128)}, u32[]{:S(2)}, u32[]{:S(2)}) %collective-permute-start.9) | collective-permute-done | bytes 589856 | tf_op jit(solution)/shard_map/ppermute | solution.py:782
  78.4 2.9 %shard_map.184.refs_9_ = f32[12,24,128]{2,1,0:T(8,128)S(1)} custom-call(f32[8,128]{1,0:T(8,128)S(1)} %get-tuple-element.68.refs_2_.refs_0_.refs_14_, f32[24,2,24,128]{3,2,1,0:T(8,128)S(1)} %get-tuple-element.72.refs_1_.refs_5_, f32[24,2,24,128]{3,2,1,0:T(8,128)S(1)} %get-tuple-element.73.refs_2_.refs_6_, ...), custom_call_target="tpu_custom_call" | custom-call | tf_op jit(solution)/shard_map/pallas_call | solution.py:144
  81.4 0.1 collective-permute-start.10
  81.5 0.8 shard_map.177
  82.2 0.6 collective-permute-done.10.refs_10_.refs_11_
  82.8 5.4 %shard_map.185 = (f32[24,4,24,128]{3,2,1,0:T(8,128)S(1)}, f32[4,24,128]{2,1,0:T(8,128)S(1)}, f32[4,4,16,128]{3,2,1,0:T(8,128)S(1)}, f32[4,8,128]{2,1,0:T(8,128)S(1)}) custom-call(f32[24]{0:T(128)S(1)} %copy-done.15, f32[4,128]{1,0:T(4,128)S(1)} %bitcast.32, ...), custom_call_target="tpu_custom_call", output_to_operand_aliasing={{2}: (13, {})} | custom-call | tf_op jit(solution)/shard_map/pallas_call | solution.py:641
  88.3 1.0 shard_map.186.refs_9_
  89.3 0.2 collective-permute-start.11
  89.5 3.2 %shard_map.187 = (f32[24,256,128]{2,1,0:T(8,128)}, f32[8,128]{1,0:T(8,128)S(1)}) custom-call(f32[24]{0:T(128)S(1)} %copy-done.16, f32[24]{0:T(128)S(1)} %copy-done.17, f32[24]{0:T(128)S(1)} %copy-done.18, f32[192,192]{1,0:T(8,128)S(1)} %shard_map.178.refs_0_.refs_3_.refs_2_, ...), custom_call_target="tpu_custom_call", output_to_operand_aliasing={{0}: (7, {})} | custom-call | tf_op jit(solution)/shard_map/pallas_call | solution.py:732
  92.7 4.1 %shard_map.188 = (f32[24,4,16,128]{3,2,1,0:T(8,128)S(1)}, f32[4,16,128]{2,1,0:T(8,128)S(1)}, f32[4,4,16,128]{3,2,1,0:T(8,128)S(1)}, f32[4,8,128]{2,1,0:T(8,128)}) custom-call(f32[24]{0:T(128)S(1)} %copy-done.15, f32[4,128]{1,0:T(4,128)S(1)} %bitcast.33, ...), custom_call_target="tpu_custom_call", output_to_operand_aliasing={{2}: (13, {})} | custom-call | tf_op jit(solution)/shard_map/pallas_call | solution.py:641
  96.9 0.7 copy-done.2
  97.5 4.0 %all-to-all-start.1 = ((f32[4,4,16,128]{3,2,1,0:T(8,128)}), f32[4,4,16,128]{3,2,1,0:T(8,128)S(1)}, u32[]{:S(2)}, u32[]{:S(2)}) async-start(f32[4,4,16,128]{3,2,1,0:T(8,128)} %copy-done.2), calls=%async_computation.1 | async-start | bytes 262144 | tf_op jit(solution)/shard_map/all_to_all | solution.py:890
  101.5 2.5 %shard_map.190 = (f32[24,256,128]{2,1,0:T(8,128)}, f32[8,128]{1,0:T(8,128)}) custom-call(f32[24]{0:T(128)S(1)} %copy-done.16, f32[24]{0:T(128)S(1)} %copy-done.17, f32[24]{0:T(128)S(1)} %copy-done.18, f32[192,192]{1,0:T(8,128)S(1)} %shard_map.178.refs_0_.refs_3_.refs_2_, ...), custom_call_target="tpu_custom_call", output_to_operand_aliasing={{0}: (7, {})} | custom-call | tf_op jit(solution)/shard_map/pallas_call | solution.py:732
  104.1 2.5 %all-to-all-done.1.refs_2_ = f32[4,4,16,128]{3,2,1,0:T(8,128)S(1)} async-done(((f32[4,4,16,128]{3,2,1,0:T(8,128)}), f32[4,4,16,128]{3,2,1,0:T(8,128)S(1)}, u32[]{:S(2)}, u32[]{:S(2)}) %all-to-all-start.1) | async-done | bytes 131104 | tf_op jit(solution)/shard_map/all_to_all | solution.py:890
  106.6 0.8 shard_map.189
  (37 shorter events, 0.1 us)
Async XLA Ops:
  0.6 1.9 %copy-start = (f32[24,64,1,1,4,128]{5,4,3,2,1,0:T(4,128)S(1)}, f32[24,64,1,1,4,128]{5,4,3,2,1,0:T(4,128)}, u32[]{:S(2)}) copy-start(f32[24,64,1,1,4,128]{5,4,3,2,1,0:T(4,128)} %param.19) | copy-start | bytes 9437188
  2.5 27.2 %copy-start.10 = (s32[16,128]{1,0:T(8,128)S(1)}, s32[16,128]{1,0:T(8,128)}, u32[]{:S(2)}) copy-start(s32[16,128]{1,0:T(8,128)} %refs_0_.12) | copy-start | bytes 24580
  2.5 27.2 %copy-start.11 = (s32[16,128]{1,0:T(8,128)S(1)}, s32[16,128]{1,0:T(8,128)}, u32[]{:S(2)}) copy-start(s32[16,128]{1,0:T(8,128)} %refs_1_.8) | copy-start | bytes 24580
  3.8 42.3 %collective-permute-start.4 = (f32[24,2,24,128]{3,2,1,0:T(8,128)}, f32[24,2,24,128]{3,2,1,0:T(8,128)}, u32[]{:S(2)}, u32[]{:S(2)}) collective-permute-start(f32[24,2,24,128]{3,2,1,0:T(8,128)} %bitcast.12.refs_2_.refs_6_), channel_id=1, source_target_pairs={{0,8},{8,16},{16,24},{24,2},{2,10},{10,18},{18,26},{26,4},{4,12},{... | collective-permute-start | bytes 1769480 | tf_op jit(solution)/shard_map/ppermute | solution.py:782
  9.5 36.7 %collective-permute-start.3 = (f32[24,2,24,128]{3,2,1,0:T(8,128)S(1)}, f32[24,2,24,128]{3,2,1,0:T(8,128)}, u32[]{:S(2)}, u32[]{:S(2)}) collective-permute-start(f32[24,2,24,128]{3,2,1,0:T(8,128)S(1)} %bitcast.24), channel_id=1, source_target_pairs={{8,0},{16,8},{24,16},{2,24},{10,2},{18,10},{26,18},{4,26},{12,4},{... | collective-permute-start | bytes 1769480 | tf_op jit(solution)/shard_map/ppermute | solution.py:786
  12.9 1.4 %collective-permute-start = (f32[5,16,128]{2,1,0:T(8,128)}, f32[5,16,128]{2,1,0:T(8,128)S(1)}, u32[]{:S(2)}, u32[]{:S(2)}) collective-permute-start(f32[5,16,128]{2,1,0:T(8,128)} %get-tuple-element.52.refs_0_), channel_id=1, source_target_pairs={{0,1},{1,0},{2,3},{3,2},{4,5},{5,4},{6,7},{7,6},{8,9},{9,8},{10,11... | collective-permute-start | bytes 122888 | tf_op jit(solution)/shard_map/ppermute | solution.py:791
  14.3 0.9 copy-start.9
  15.2 0.8 copy-start.12
  16.0 13.7 %collective-permute-start.1 = (f32[14,16,128]{2,1,0:T(8,128)S(1)}, f32[14,16,128]{2,1,0:T(8,128)S(1)}, u32[]{:S(2)}, u32[]{:S(2)}) collective-permute-start(f32[14,16,128]{2,1,0:T(8,128)S(1)} %get-tuple-element.55), channel_id=1, source_target_pairs={{2,0},{4,2},{6,4},{3,1},{5,3},{7,5},{10,8},{12,10},{14,12},{11,9},... | collective-permute-start | bytes 344072 | tf_op jit(solution)/shard_map/ppermute | solution.py:772
  17.3 12.4 %collective-permute-start.2 = (f32[14,16,128]{2,1,0:T(8,128)S(1)}, f32[14,16,128]{2,1,0:T(8,128)S(1)}, u32[]{:S(2)}, u32[]{:S(2)}) collective-permute-start(f32[14,16,128]{2,1,0:T(8,128)S(1)} %get-tuple-element.56), channel_id=1, source_target_pairs={{0,2},{2,4},{4,6},{1,3},{3,5},{5,7},{8,10},{10,12},{12,14},{9,11},... | collective-permute-start | bytes 344072 | tf_op jit(solution)/shard_map/ppermute | solution.py:768
  23.6 1.9 %copy-start.1 = (f32[24,64,1,1,4,128]{5,4,3,2,1,0:T(4,128)S(1)}, f32[24,64,1,1,4,128]{5,4,3,2,1,0:T(4,128)}, u32[]{:S(2)}) copy-start(f32[24,64,1,1,4,128]{5,4,3,2,1,0:T(4,128)} %param.19) | copy-start | bytes 9437188
  25.5 4.3 %copy-start.4 = (f32[4,16,16,128]{3,2,1,0:T(8,128)S(1)}, f32[4,16,16,128]{3,2,1,0:T(8,128)}, u32[]{:S(2)}) copy-start(f32[4,16,16,128]{3,2,1,0:T(8,128)} %get-tuple-element.51.refs_1_) | copy-start | bytes 1572868
  25.5 13.1 %copy-start.14 = (f32[24,24]{1,0:T(8,128)S(1)}, f32[24,24]{1,0:T(8,128)}, u32[]{:S(2)}) copy-start(f32[24,24]{1,0:T(8,128)} %refs_1_.5) | copy-start | bytes 6916
  29.7 27.9 %copy-start.13 = (f32[1,1,4,128]{3,2,1,0:T(4,128)S(1)}, f32[1,1,4,128]{3,2,1,0:T(4,128)}, u32[]{:S(2)}) copy-start(f32[1,1,4,128]{3,2,1,0:T(4,128)} %param.20) | copy-start | bytes 6148
  29.7 27.9 %copy-start.15 = (f32[24]{0:T(128)S(1)}, f32[24]{0:T(128)}, u32[]{:S(2)}) copy-start(f32[24]{0:T(128)} %refs_0_.11) | copy-start | bytes 292
  32.9 0.8 copy-start.3
  33.7 0.7 copy-start.5
  34.4 0.7 copy-start.7
  35.1 22.5 %all-to-all-start = ((f32[4,18,16,128]{3,2,1,0:T(8,128)}), f32[4,18,16,128]{3,2,1,0:T(8,128)S(1)}, u32[]{:S(2)}, u32[]{:S(2)}) async-start(f32[4,18,16,128]{3,2,1,0:T(8,128)} %copy-done.3), calls=%async_computation | async-start | bytes 1179648 | tf_op jit(solution)/shard_map/all_to_all | solution.py:844
  39.3 33.1 %collective-permute-start.8 = (f32[24,2,24,128]{3,2,1,0:T(8,128)S(1)}, f32[24,2,24,128]{3,2,1,0:T(8,128)}, u32[]{:S(2)}, u32[]{:S(2)}) collective-permute-start(f32[24,2,24,128]{3,2,1,0:T(8,128)S(1)} %get-tuple-element.72.refs_1_.refs_5_), channel_id=1, source_target_pairs={{8,0},{16,8},{24,16},{2,24},{10,2},{18,10},{26,18},{4,26},{12,4},{... | collective-permute-start | bytes 1769480 | tf_op jit(solution)/shard_map/ppermute | solution.py:786
  40.6 22.6 %copy-start.16 = (f32[24]{0:T(128)S(1)}, f32[24]{0:T(128)}, u32[]{:S(2)}) copy-start(f32[24]{0:T(128)} %refs_0_.13) | copy-start | bytes 292
  40.6 22.6 %copy-start.17 = (f32[24]{0:T(128)S(1)}, f32[24]{0:T(128)}, u32[]{:S(2)}) copy-start(f32[24]{0:T(128)} %refs_1_.9) | copy-start | bytes 292
  40.6 22.6 %copy-start.18 = (f32[24]{0:T(128)S(1)}, f32[24]{0:T(128)}, u32[]{:S(2)}) copy-start(f32[24]{0:T(128)} %refs_2_.7) | copy-start | bytes 292
  40.6 37.8 %collective-permute-start.9 = (f32[24,2,24,128]{3,2,1,0:T(8,128)S(1)}, f32[24,2,24,128]{3,2,1,0:T(8,128)}, u32[]{:S(2)}, u32[]{:S(2)}) collective-permute-start(f32[24,2,24,128]{3,2,1,0:T(8,128)S(1)} %get-tuple-element.73.refs_2_.refs_6_), channel_id=1, source_target_pairs={{0,8},{8,16},{16,24},{24,2},{2,10},{10,18},{18,26},{26,4},{4,12},{... | collective-permute-start | bytes 1769480 | tf_op jit(solution)/shard_map/ppermute | solution.py:782
  49.9 7.8 %collective-permute-start.5 = (f32[12,24,128]{2,1,0:T(8,128)}, f32[12,24,128]{2,1,0:T(8,128)}, u32[]{:S(2)}, u32[]{:S(2)}) collective-permute-start(f32[12,24,128]{2,1,0:T(8,128)} %shard_map.179.refs_9_), channel_id=1, source_target_pairs={{0,1},{1,0},{2,3},{3,2},{4,5},{5,4},{6,7},{7,6},{8,9},{9,8},{10,11... | collective-permute-start | bytes 442376 | tf_op jit(solution)/shard_map/ppermute | solution.py:791
  63.2 18.3 %copy-start.8 = (f32[2,16,16,128]{3,2,1,0:T(8,128)S(1)}, f32[2,16,16,128]{3,2,1,0:T(8,128)}, u32[]{:S(2)}) copy-start(f32[2,16,16,128]{3,2,1,0:T(8,128)} %copy-done.7) | copy-start | bytes 786436
  66.5 21.8 %collective-permute-start.6 = (f32[24,2,16,128]{3,2,1,0:T(8,128)S(1)}, f32[24,2,16,128]{3,2,1,0:T(8,128)S(1)}, u32[]{:S(2)}, u32[]{:S(2)}) collective-permute-start(f32[24,2,16,128]{3,2,1,0:T(8,128)S(1)} %get-tuple-element.69.refs_1_.refs_5_), channel_id=1, source_target_pairs={{8,0},{16,8},{24,16},{2,24},{10,2},{18,10},{26,18},{4,26},{12,4},{... | collective-permute-start | bytes 1179656 | tf_op jit(solution)/shard_map/ppermute | solution.py:786
  67.8 20.5 %collective-permute-start.7 = (f32[24,2,16,128]{3,2,1,0:T(8,128)S(1)}, f32[24,2,16,128]{3,2,1,0:T(8,128)S(1)}, u32[]{:S(2)}, u32[]{:S(2)}) collective-permute-start(f32[24,2,16,128]{3,2,1,0:T(8,128)S(1)} %get-tuple-element.70.refs_2_.refs_6_), channel_id=1, source_target_pairs={{0,8},{8,16},{16,24},{24,2},{2,10},{10,18},{18,26},{26,4},{4,12},{... | collective-permute-start | bytes 1179656 | tf_op jit(solution)/shard_map/ppermute | solution.py:782
  81.4 1.4 %collective-permute-start.10 = (f32[12,24,128]{2,1,0:T(8,128)S(1)}, f32[12,24,128]{2,1,0:T(8,128)S(1)}, u32[]{:S(2)}, u32[]{:S(2)}) collective-permute-start(f32[12,24,128]{2,1,0:T(8,128)S(1)} %shard_map.184.refs_9_), channel_id=1, source_target_pairs={{0,1},{1,0},{2,3},{3,2},{4,5},{5,4},{6,7},{7,6},{8,9},{9,8},{10,11... | collective-permute-start | bytes 442376 | tf_op jit(solution)/shard_map/ppermute | solution.py:791
  89.3 3.5 %collective-permute-start.11 = (f32[12,16,128]{2,1,0:T(8,128)S(1)}, f32[12,16,128]{2,1,0:T(8,128)S(1)}, u32[]{:S(2)}, u32[]{:S(2)}) collective-permute-start(f32[12,16,128]{2,1,0:T(8,128)S(1)} %shard_map.186.refs_9_), channel_id=1, source_target_pairs={{0,1},{1,0},{2,3},{3,2},{4,5},{5,4},{6,7},{7,6},{8,9},{9,8},{10,11... | collective-permute-start | bytes 294920 | tf_op jit(solution)/shard_map/ppermute | solution.py:791
  92.7 13.8 %copy-start.6 = (f32[2,16,16,128]{3,2,1,0:T(8,128)S(1)}, f32[2,16,16,128]{3,2,1,0:T(8,128)}, u32[]{:S(2)}) copy-start(f32[2,16,16,128]{3,2,1,0:T(8,128)} %copy-done.5) | copy-start | bytes 786436
  96.9 0.7 copy-start.2
  97.5 9.0 %all-to-all-start.1 = ((f32[4,4,16,128]{3,2,1,0:T(8,128)}), f32[4,4,16,128]{3,2,1,0:T(8,128)S(1)}, u32[]{:S(2)}, u32[]{:S(2)}) async-start(f32[4,4,16,128]{3,2,1,0:T(8,128)} %copy-done.2), calls=%async_computation.1 | async-start | bytes 262144 | tf_op jit(solution)/shard_map/all_to_all | solution.py:890

commit v5 on v4

--- a/solution.py
+++ b/solution.py
@@ -834,10 +834,10 @@
 
     packed, edges, ocean_rows = pack_ocean(flat, sea, levels)
     ranges = [(first * SUB, size * SUB) for first, size in cuts]
-    chunks = [rims(cut_rows(q, ranges[:1], []))]
-    later = cut_rows(q, ranges[1:], chunks[0][0][:1])
     up, down, packed = ocean_sides(packed, *from_sides(packed), edges)
     after, before = from_after(up, "gx"), from_before(down, "gx")
+    chunks = [rims(cut_rows(q, ranges[:1], [up]))]
+    later = cut_rows(q, ranges[1:], chunks[0][0][:1])
     smix, mixed, send, local, faces, depths = ocean_phase(
         blocks, levels, ocean_rows, sea, packed, after, before, later[:1]
     )

time: 110 us -> 113 us (1.027); the launches traced: 107 us -> 113 us
  waiting for transfers between devices: 21.1 us -> 25 us
  Pallas kernels: 42.1 us -> 43.3 us
    ppermute x1, waiting for transfers between devices: 2.79 us -> 10.9 us  [from_after(): lax.ppermute(x, axis, [(i + 1, i) for i in range(lax.axis_size(axis) - 1)])]
    ppermute x3, waiting for transfers between devices: 6.05 us -> 1.7 us  [from_block_before(): return lax.ppermute(x, ('comp', 'gx'), row_pairs())]
    pallas_call x3, Pallas kernels: 15.2 us -> 16.3 us  [advection(): pl.pallas_call(functools.partial(advection_kernel, first_part, parts, lev...]
    unnamed x38 -> x54, local copies, waits for them, and re-layouts: 8.36 us -> 7.85 us
  transfers between devices with their start and end apart: 14 -> 14, of which waited for: 6 -> 7; matrix products, arithmetic and copies ran while one was open for 0% -> 0% of each run, Pallas kernels for 32% -> 30%
where the time goes in v5:
time: 113 us
  Pallas kernels  43.3 us (38%)
  starting transfers between devices  35.5 us (31%)
  waiting for transfers between devices  25 us (22%)
  local copies, waits for them, and re-layouts  7.85 us (7%)
    pallas_call x3, Pallas kernels, advection(): pl.pallas_call(functools.partial(advection_kernel, first_part, parts, lev...  16.3 us
    ppermute x3, starting transfers between devices, from_block_before(): return lax.ppermute(x, ('comp', 'gx'), row_pairs())  15.6 us
    ppermute x1, waiting for transfers between devices, from_after(): lax.ppermute(x, axis, [(i + 1, i) for i in range(lax.axis_size(axis) - 1)])  10.9 us
    pallas_call x3, Pallas kernels, uptake(): pl.pallas_call(functools.partial(uptake_kernel, first_part * SUB), grid=(...  9.11 us
    all_to_all x1, waiting for transfers between devices, on_device(): lax.all_to_all(send, 'comp', split_axis=0, concat_axis=0, tiled=True)  8.28 us
    unnamed x54, local copies, waits for them, and re-layouts  7.85 us
    pallas_call x3, Pallas kernels, pack_tracers(): pl.pallas_call(functools.partial(ignoring, len(after), pack_tracers_kerne...  7.66 us
    pallas_call x5, Pallas kernels, call_once(): pl.pallas_call(functools.partial(ignoring, len(after), kernel), grid=(1,)...  6.74 us
  transfers between devices with their start and end apart: 14, of which 7 were waited for; matrix products, arithmetic and copies ran while one was open for 0% of the time, Pallas kernels for 30%

profile of v5, /device:TPU:0, one launch (start us, length us, event | category | flops | bytes accessed | tf_op | source)
XLA Modules:
  0.0 112.5 jit_solution(1543726216631831994)
XLA Ops:
  0.6 2.1 %shard_map.172 = (f32[5,16,128]{2,1,0:T(8,128)}, f32[2,9,16,128]{3,2,1,0:T(8,128)}, f32[4,16,16,128]{3,2,1,0:T(8,128)}) custom-call(f32[256,128]{1,0:T(8,128)} %bitcast.35, f32[256,128]{1,0:T(8,128)} %bitcast.36, f32[256,128]{1,0:T(8,128)} %bitcast.37, f32[256,128]{1,0:T(8,128)} %bitcast.38, s32[16,128]{1,0:T(8,128)} %refs_0_.12, s32[16,128]{1,0:T(8,128)} %refs_1_.8), custom_call_target="tpu_custom_call" | custom-call | tf_op jit(solution)/shard_map/pallas_call | solution.py:159
  2.7 0.5 collective-permute-start
  3.2 1.1 collective-permute-done.refs_1_.refs_2_
  4.3 0.9 copy-done.8
  5.2 0.8 copy-done.13
  6.0 1.9 %copy-done = f32[24,64,1,1,4,128]{5,4,3,2,1,0:T(4,128)S(1)} copy-done((f32[24,64,1,1,4,128]{5,4,3,2,1,0:T(4,128)S(1)}, f32[24,64,1,1,4,128]{5,4,3,2,1,0:T(4,128)}, u32[]{:S(2)}) %copy-start) | copy-done | bytes 3145752
  7.9 1.3 %shard_map.174 = (f32[24,2,24,1,128]{4,3,2,1,0:T(1,128)S(1)}, f32[24,2,24,1,128]{4,3,2,1,0:T(1,128)}) custom-call(f32[24,64,4,1,128]{4,3,2,1,0:T(1,128)S(1)} %bitcast.20, f32[14,16,128]{2,1,0:T(8,128)S(1)} %get-tuple-element.51.refs_0_), custom_call_target="tpu_custom_call" | custom-call | tf_op jit(solution)/shard_map/pallas_call | solution.py:96
  9.2 5.7 %collective-permute-start.4 = (f32[24,2,24,128]{3,2,1,0:T(8,128)}, f32[24,2,24,128]{3,2,1,0:T(8,128)}, u32[]{:S(2)}, u32[]{:S(2)}) collective-permute-start(f32[24,2,24,128]{3,2,1,0:T(8,128)} %bitcast.12.refs_2_.refs_6_), channel_id=1, source_target_pairs={{0,8},{8,16},{16,24},{24,2},{2,10},{10,18},{18,26},{26,4},{4,12},{... | collective-permute-start | bytes 1769480 | tf_op jit(solution)/shard_map/ppermute | solution.py:782
  14.9 1.3 %collective-permute-start.3 = (f32[24,2,24,128]{3,2,1,0:T(8,128)S(1)}, f32[24,2,24,128]{3,2,1,0:T(8,128)}, u32[]{:S(2)}, u32[]{:S(2)}) collective-permute-start(f32[24,2,24,128]{3,2,1,0:T(8,128)S(1)} %bitcast.24), channel_id=1, source_target_pairs={{8,0},{16,8},{24,16},{2,24},{10,2},{18,10},{26,18},{4,26},{12,4},{... | collective-permute-start | bytes 1769480 | tf_op jit(solution)/shard_map/ppermute | solution.py:786
  16.1 0.0 copy-start.18
  16.2 5.6 %collective-permute-start.2 = (f32[14,16,128]{2,1,0:T(8,128)S(1)}, f32[14,16,128]{2,1,0:T(8,128)S(1)}, u32[]{:S(2)}, u32[]{:S(2)}) collective-permute-start(f32[14,16,128]{2,1,0:T(8,128)S(1)} %get-tuple-element.56), channel_id=1, source_target_pairs={{0,2},{2,4},{4,6},{1,3},{3,5},{5,7},{8,10},{10,12},{12,14},{9,11},... | collective-permute-start | bytes 344072 | tf_op jit(solution)/shard_map/ppermute | solution.py:768
  21.8 1.3 %collective-permute-start.1 = (f32[14,16,128]{2,1,0:T(8,128)S(1)}, f32[14,16,128]{2,1,0:T(8,128)S(1)}, u32[]{:S(2)}, u32[]{:S(2)}) collective-permute-start(f32[14,16,128]{2,1,0:T(8,128)S(1)} %get-tuple-element.51.refs_0_), channel_id=1, source_target_pairs={{2,0},{4,2},{6,4},{3,1},{5,3},{7,5},{10,8},{12,10},{14,12},{11,9},... | collective-permute-start | bytes 344072 | tf_op jit(solution)/shard_map/ppermute | solution.py:772
  23.1 1.4 %shard_map.175 = (f32[24,2,24,1,128]{4,3,2,1,0:T(1,128)S(1)}, f32[24,2,24,1,128]{4,3,2,1,0:T(1,128)S(1)}, f32[24,2,16,1,128]{4,3,2,1,0:T(1,128)S(1)}, f32[24,2,16,1,128]{4,3,2,1,0:T(1,128)S(1)}) custom-call(f32[24,64,4,1,128]{4,3,2,1,0:T(1,128)S(1)} %bitcast.21, f32[24,2,24,128]{3,2,1,0:T(8,128)S(1)} %bitcast.25), custom_call_target="tpu_custom_call" | custom-call | tf_op jit(solution)/shard_map/pallas_call | solution.py:96
  24.6 10.9 %collective-permute-done.1.refs_5_ = f32[14,16,128]{2,1,0:T(8,128)S(1)} collective-permute-done((f32[14,16,128]{2,1,0:T(8,128)S(1)}, f32[14,16,128]{2,1,0:T(8,128)S(1)}, u32[]{:S(2)}, u32[]{:S(2)}) %collective-permute-start.1) | collective-permute-done | bytes 114720 | tf_op jit(solution)/shard_map/ppermute | solution.py:772
  35.4 3.2 %shard_map.176 = (f32[256,128]{1,0:T(8,128)}, f32[2,16,16,128]{3,2,1,0:T(8,128)S(1)}, f32[4,18,16,128]{3,2,1,0:T(8,128)S(1)}, f32[2,16,16,128]{3,2,1,0:T(8,128)S...) custom-call(f32[24,2,24,128]{3,2,1,0:T(8,128)S(1)} %bitcast.22, f32[4,16,16,128]{3,2,1,0:T(8,128)S(1)} %copy-done.3, ...), custom_call_target="tpu_custom_call" | custom-call | tf_op jit(solution)/shard_map/pallas_call | solution.py:159
  38.6 0.8 copy-done.2
  39.5 0.7 copy-done.4
  40.2 0.7 copy-done.6
  40.9 0.6 copy-done.16
  41.5 3.5 %all-to-all-start = ((f32[4,18,16,128]{3,2,1,0:T(8,128)}), f32[4,18,16,128]{3,2,1,0:T(8,128)S(1)}, u32[]{:S(2)}, u32[]{:S(2)}) async-start(f32[4,18,16,128]{3,2,1,0:T(8,128)} %copy-done.2), calls=%async_computation | async-start | bytes 1179648 | tf_op jit(solution)/shard_map/all_to_all | solution.py:844
  45.0 0.6 shard_map.178.refs_0_.refs_3_.refs_2_
  45.6 1.3 %collective-permute-start.8 = (f32[24,2,24,128]{3,2,1,0:T(8,128)S(1)}, f32[24,2,24,128]{3,2,1,0:T(8,128)}, u32[]{:S(2)}, u32[]{:S(2)}) collective-permute-start(f32[24,2,24,128]{3,2,1,0:T(8,128)S(1)} %get-tuple-element.72.refs_1_.refs_5_), channel_id=1, source_target_pairs={{8,0},{16,8},{24,16},{2,24},{10,2},{18,10},{26,18},{4,26},{12,4},{... | collective-permute-start | bytes 1769480 | tf_op jit(solution)/shard_map/ppermute | solution.py:786
  46.9 5.4 %collective-permute-start.9 = (f32[24,2,24,128]{3,2,1,0:T(8,128)S(1)}, f32[24,2,24,128]{3,2,1,0:T(8,128)}, u32[]{:S(2)}, u32[]{:S(2)}) collective-permute-start(f32[24,2,24,128]{3,2,1,0:T(8,128)S(1)} %get-tuple-element.73.refs_2_.refs_6_), channel_id=1, source_target_pairs={{0,8},{8,16},{16,24},{24,2},{2,10},{10,18},{18,26},{26,4},{4,12},{... | collective-permute-start | bytes 1769480 | tf_op jit(solution)/shard_map/ppermute | solution.py:782
  52.3 3.7 %shard_map.179.refs_9_ = f32[12,24,128]{2,1,0:T(8,128)} custom-call(f32[192,192]{1,0:T(8,128)S(1)} %shard_map.178.refs_0_.refs_3_.refs_2_, f32[24,2,24,128]{3,2,1,0:T(8,128)S(1)} %bitcast.26, f32[24,2,24,128]{3,2,1,0:T(8,128)} %bitcast.12.refs_2_.refs_6_, f32[24,2,24,128]{3,2,1,0:T(8,128)} %collective-permute-done.3.refs_3_.refs_7_, ...), custom_call_target="tpu_custom_call" | custom-call | tf_op jit(solution)/shard_map/pallas_call | solution.py:144
  56.0 8.3 %all-to-all-done.received_ref.refs_3_.refs_4_ = f32[4,18,16,128]{3,2,1,0:T(8,128)S(1)} async-done(((f32[4,18,16,128]{3,2,1,0:T(8,128)}), f32[4,18,16,128]{3,2,1,0:T(8,128)S(1)}, u32[]{:S(2)}, u32[]{:S(2)}) %all-to-all-start) | async-done | bytes 589856 | tf_op jit(solution)/shard_map/all_to_all | solution.py:844
  64.3 0.0 copy-start.14
  64.3 0.7 copy-done.14
  65.0 0.7 copy-done.19
  65.7 6.1 %shard_map.180 = (f32[24,4,24,128]{3,2,1,0:T(8,128)S(1)}, f32[4,24,128]{2,1,0:T(8,128)S(1)}, f32[4,4,16,128]{3,2,1,0:T(8,128)}, f32[4,8,128]{2,1,0:T(8,128)S(1)}) custom-call(f32[24]{0:T(128)S(1)} %copy-done.19, f32[4,128]{1,0:T(4,128)S(1)} %bitcast.31, f32[4,32,128]{2,1,0:T(8,128)S(1)} %get-tuple-element.62.refs_0_.refs_2_.refs_4_, ...), custom_call_target="tpu_custom_call" | custom-call | tf_op jit(solution)/shard_map/pallas_call | solution.py:641
  71.8 0.0 copy-start.20
  71.8 3.3 %shard_map.181 = (f32[24,256,128]{2,1,0:T(8,128)}, f32[8,128]{1,0:T(8,128)S(1)}) custom-call(f32[24]{0:T(128)S(1)} %copy-done.21, f32[24]{0:T(128)S(1)} %copy-done.23, f32[24]{0:T(128)S(1)} %copy-done.25, f32[192,192]{1,0:T(8,128)S(1)} %shard_map.178.refs_0_.refs_3_.refs_2_, f32[4,32,128]{2,1,0:T(8,128)S(1)} %get-tuple-element.62.refs_0_.refs_2_.refs_4_, ...), custom_call_target="tpu_custom_call" | custom-call | tf_op jit(solution)/shard_map/pallas_call | solution.py:732
  75.1 1.3 %collective-permute-start.6 = (f32[24,2,16,128]{3,2,1,0:T(8,128)S(1)}, f32[24,2,16,128]{3,2,1,0:T(8,128)S(1)}, u32[]{:S(2)}, u32[]{:S(2)}) collective-permute-start(f32[24,2,16,128]{3,2,1,0:T(8,128)S(1)} %get-tuple-element.69.refs_1_.refs_5_), channel_id=1, source_target_pairs={{8,0},{16,8},{24,16},{2,24},{10,2},{18,10},{26,18},{4,26},{12,4},{... | collective-permute-start | bytes 1179656 | tf_op jit(solution)/shard_map/ppermute | solution.py:786
  76.4 4.6 %collective-permute-start.7 = (f32[24,2,16,128]{3,2,1,0:T(8,128)S(1)}, f32[24,2,16,128]{3,2,1,0:T(8,128)S(1)}, u32[]{:S(2)}, u32[]{:S(2)}) collective-permute-start(f32[24,2,16,128]{3,2,1,0:T(8,128)S(1)} %get-tuple-element.70.refs_2_.refs_6_), channel_id=1, source_target_pairs={{0,8},{8,16},{16,24},{24,2},{2,10},{10,18},{18,26},{26,4},{4,12},{... | collective-permute-start | bytes 1179656 | tf_op jit(solution)/shard_map/ppermute | solution.py:782
  81.0 0.1 collective-permute-done.9.refs_4_.refs_8_
  81.1 2.9 %shard_map.184.refs_9_ = f32[12,24,128]{2,1,0:T(8,128)S(1)} custom-call(f32[8,128]{1,0:T(8,128)S(1)} %get-tuple-element.68.refs_2_.refs_0_.refs_14_, f32[24,2,24,128]{3,2,1,0:T(8,128)S(1)} %get-tuple-element.72.refs_1_.refs_5_, f32[24,2,24,128]{3,2,1,0:T(8,128)S(1)} %get-tuple-element.73.refs_2_.refs_6_, ...), custom_call_target="tpu_custom_call" | custom-call | tf_op jit(solution)/shard_map/pallas_call | solution.py:144
  84.0 0.1 collective-permute-start.10
  84.1 0.8 shard_map.177
  84.9 0.6 collective-permute-done.10.refs_10_.refs_11_
  85.4 6.1 %shard_map.185 = (f32[24,4,24,128]{3,2,1,0:T(8,128)S(1)}, f32[4,24,128]{2,1,0:T(8,128)S(1)}, f32[4,4,16,128]{3,2,1,0:T(8,128)}, f32[4,8,128]{2,1,0:T(8,128)S(1)}) custom-call(f32[24]{0:T(128)S(1)} %copy-done.20, f32[4,128]{1,0:T(4,128)S(1)} %bitcast.32, ...), custom_call_target="tpu_custom_call", output_to_operand_aliasing={{2}: (13, {})} | custom-call | tf_op jit(solution)/shard_map/pallas_call | solution.py:641
  91.5 1.6 %collective-permute-done.7.refs_4_.refs_8_ = f32[24,2,16,128]{3,2,1,0:T(8,128)S(1)} collective-permute-done((f32[24,2,16,128]{3,2,1,0:T(8,128)S(1)}, f32[24,2,16,128]{3,2,1,0:T(8,128)S(1)}, u32[]{:S(2)}, u32[]{:S(2)}) %collective-permute-start.7) | collective-permute-done | bytes 393248 | tf_op jit(solution)/shard_map/ppermute | solution.py:782
  93.1 1.0 shard_map.186.refs_9_
  94.1 0.1 collective-permute-start.11
  94.2 3.3 %shard_map.187 = (f32[24,256,128]{2,1,0:T(8,128)}, f32[8,128]{1,0:T(8,128)S(1)}) custom-call(f32[24]{0:T(128)S(1)} %copy-done.21, f32[24]{0:T(128)S(1)} %copy-done.23, f32[24]{0:T(128)S(1)} %copy-done.25, f32[192,192]{1,0:T(8,128)S(1)} %shard_map.178.refs_0_.refs_3_.refs_2_, ...), custom_call_target="tpu_custom_call", output_to_operand_aliasing={{0}: (7, {})} | custom-call | tf_op jit(solution)/shard_map/pallas_call | solution.py:732
  97.5 4.2 %shard_map.188 = (f32[24,4,16,128]{3,2,1,0:T(8,128)S(1)}, f32[4,16,128]{2,1,0:T(8,128)S(1)}, f32[4,4,16,128]{3,2,1,0:T(8,128)}, f32[4,8,128]{2,1,0:T(8,128)}) custom-call(f32[24]{0:T(128)S(1)} %copy-done.20, f32[4,128]{1,0:T(4,128)S(1)} %bitcast.33, f32[4,32,128]{2,1,0:T(8,128)S(1)} %get-tuple-element.62.refs_0_.refs_2_.refs_4_, ...), custom_call_target="tpu_custom_call", output_to_operand_aliasing={{2}: (13, {})} | custom-call | tf_op jit(solution)/shard_map/pallas_call | solution.py:641
  101.7 5.0 %all-to-all-start.1 = ((f32[4,4,16,128]{3,2,1,0:T(8,128)}), f32[4,4,16,128]{3,2,1,0:T(8,128)S(1)}, u32[]{:S(2)}, u32[]{:S(2)}) async-start(f32[4,4,16,128]{3,2,1,0:T(8,128)} %get-tuple-element.83), calls=%async_computation.1 | async-start | bytes 262144 | tf_op jit(solution)/shard_map/all_to_all | solution.py:890
  106.7 2.6 %shard_map.190 = (f32[24,256,128]{2,1,0:T(8,128)}, f32[8,128]{1,0:T(8,128)}) custom-call(f32[24]{0:T(128)S(1)} %copy-done.22, f32[24]{0:T(128)S(1)} %copy-done.24, f32[24]{0:T(128)S(1)} %copy-done.26, f32[192,192]{1,0:T(8,128)S(1)} %shard_map.178.refs_0_.refs_3_.refs_2_, ...), custom_call_target="tpu_custom_call", output_to_operand_aliasing={{0}: (7, {})} | custom-call | tf_op jit(solution)/shard_map/pallas_call | solution.py:732
  109.2 2.5 %all-to-all-done.1.refs_2_ = f32[4,4,16,128]{3,2,1,0:T(8,128)S(1)} async-done(((f32[4,4,16,128]{3,2,1,0:T(8,128)}), f32[4,4,16,128]{3,2,1,0:T(8,128)S(1)}, u32[]{:S(2)}, u32[]{:S(2)}) %all-to-all-start.1) | async-done | bytes 131104 | tf_op jit(solution)/shard_map/all_to_all | solution.py:890
  111.7 0.8 shard_map.189
  (53 shorter events, 0.1 us)
Async XLA Ops:
  2.7 1.5 %collective-permute-start = (f32[5,16,128]{2,1,0:T(8,128)}, f32[5,16,128]{2,1,0:T(8,128)S(1)}, u32[]{:S(2)}, u32[]{:S(2)}) collective-permute-start(f32[5,16,128]{2,1,0:T(8,128)} %get-tuple-element.49.refs_0_), channel_id=1, source_target_pairs={{0,1},{1,0},{2,3},{3,2},{4,5},{5,4},{6,7},{7,6},{8,9},{9,8},{10,11... | collective-permute-start | bytes 122888 | tf_op jit(solution)/shard_map/ppermute | solution.py:791
  4.3 0.9 copy-start.8
  5.2 0.8 copy-start.13
  6.0 1.9 %copy-start = (f32[24,64,1,1,4,128]{5,4,3,2,1,0:T(4,128)S(1)}, f32[24,64,1,1,4,128]{5,4,3,2,1,0:T(4,128)}, u32[]{:S(2)}) copy-start(f32[24,64,1,1,4,128]{5,4,3,2,1,0:T(4,128)} %param.19) | copy-start | bytes 9437188
  7.9 15.2 %copy-start.1 = (f32[24,64,1,1,4,128]{5,4,3,2,1,0:T(4,128)S(1)}, f32[24,64,1,1,4,128]{5,4,3,2,1,0:T(4,128)}, u32[]{:S(2)}) copy-start(f32[24,64,1,1,4,128]{5,4,3,2,1,0:T(4,128)} %param.19) | copy-start | bytes 9437188
  7.9 27.6 %copy-start.3 = (f32[4,16,16,128]{3,2,1,0:T(8,128)S(1)}, f32[4,16,16,128]{3,2,1,0:T(8,128)}, u32[]{:S(2)}) copy-start(f32[4,16,16,128]{3,2,1,0:T(8,128)} %get-tuple-element.54.refs_1_) | copy-start | bytes 1572868
  7.9 27.6 %copy-start.9 = (s32[16,128]{1,0:T(8,128)S(1)}, s32[16,128]{1,0:T(8,128)}, u32[]{:S(2)}) copy-start(s32[16,128]{1,0:T(8,128)} %refs_0_.12) | copy-start | bytes 24580
  7.9 27.6 %copy-start.11 = (s32[16,128]{1,0:T(8,128)S(1)}, s32[16,128]{1,0:T(8,128)}, u32[]{:S(2)}) copy-start(s32[16,128]{1,0:T(8,128)} %refs_1_.8) | copy-start | bytes 24580
  9.2 43.1 %collective-permute-start.4 = (f32[24,2,24,128]{3,2,1,0:T(8,128)}, f32[24,2,24,128]{3,2,1,0:T(8,128)}, u32[]{:S(2)}, u32[]{:S(2)}) collective-permute-start(f32[24,2,24,128]{3,2,1,0:T(8,128)} %bitcast.12.refs_2_.refs_6_), channel_id=1, source_target_pairs={{0,8},{8,16},{16,24},{24,2},{2,10},{10,18},{18,26},{26,4},{4,12},{... | collective-permute-start | bytes 1769480 | tf_op jit(solution)/shard_map/ppermute | solution.py:782
  14.9 37.4 %collective-permute-start.3 = (f32[24,2,24,128]{3,2,1,0:T(8,128)S(1)}, f32[24,2,24,128]{3,2,1,0:T(8,128)}, u32[]{:S(2)}, u32[]{:S(2)}) collective-permute-start(f32[24,2,24,128]{3,2,1,0:T(8,128)S(1)} %bitcast.24), channel_id=1, source_target_pairs={{8,0},{16,8},{24,16},{2,24},{10,2},{18,10},{26,18},{4,26},{12,4},{... | collective-permute-start | bytes 1769480 | tf_op jit(solution)/shard_map/ppermute | solution.py:786
  16.1 28.8 %copy-start.18 = (f32[24,24]{1,0:T(8,128)S(1)}, f32[24,24]{1,0:T(8,128)}, u32[]{:S(2)}) copy-start(f32[24,24]{1,0:T(8,128)} %refs_1_.5) | copy-start | bytes 6916
  16.2 8.4 %collective-permute-start.2 = (f32[14,16,128]{2,1,0:T(8,128)S(1)}, f32[14,16,128]{2,1,0:T(8,128)S(1)}, u32[]{:S(2)}, u32[]{:S(2)}) collective-permute-start(f32[14,16,128]{2,1,0:T(8,128)S(1)} %get-tuple-element.56), channel_id=1, source_target_pairs={{0,2},{2,4},{4,6},{1,3},{3,5},{5,7},{8,10},{10,12},{12,14},{9,11},... | collective-permute-start | bytes 344072 | tf_op jit(solution)/shard_map/ppermute | solution.py:768
  21.8 13.6 %collective-permute-start.1 = (f32[14,16,128]{2,1,0:T(8,128)S(1)}, f32[14,16,128]{2,1,0:T(8,128)S(1)}, u32[]{:S(2)}, u32[]{:S(2)}) collective-permute-start(f32[14,16,128]{2,1,0:T(8,128)S(1)} %get-tuple-element.51.refs_0_), channel_id=1, source_target_pairs={{2,0},{4,2},{6,4},{3,1},{5,3},{7,5},{10,8},{12,10},{14,12},{11,9},... | collective-permute-start | bytes 344072 | tf_op jit(solution)/shard_map/ppermute | solution.py:772
  38.6 0.8 copy-start.2
  39.5 0.7 copy-start.4
  40.2 0.7 copy-start.6
  40.9 0.6 copy-start.16
  41.5 22.9 %all-to-all-start = ((f32[4,18,16,128]{3,2,1,0:T(8,128)}), f32[4,18,16,128]{3,2,1,0:T(8,128)S(1)}, u32[]{:S(2)}, u32[]{:S(2)}) async-start(f32[4,18,16,128]{3,2,1,0:T(8,128)} %copy-done.2), calls=%async_computation | async-start | bytes 1179648 | tf_op jit(solution)/shard_map/all_to_all | solution.py:844
  45.6 35.4 %collective-permute-start.8 = (f32[24,2,24,128]{3,2,1,0:T(8,128)S(1)}, f32[24,2,24,128]{3,2,1,0:T(8,128)}, u32[]{:S(2)}, u32[]{:S(2)}) collective-permute-start(f32[24,2,24,128]{3,2,1,0:T(8,128)S(1)} %get-tuple-element.72.refs_1_.refs_5_), channel_id=1, source_target_pairs={{8,0},{16,8},{24,16},{2,24},{10,2},{18,10},{26,18},{4,26},{12,4},{... | collective-permute-start | bytes 1769480 | tf_op jit(solution)/shard_map/ppermute | solution.py:786
  46.9 34.2 %collective-permute-start.9 = (f32[24,2,24,128]{3,2,1,0:T(8,128)S(1)}, f32[24,2,24,128]{3,2,1,0:T(8,128)}, u32[]{:S(2)}, u32[]{:S(2)}) collective-permute-start(f32[24,2,24,128]{3,2,1,0:T(8,128)S(1)} %get-tuple-element.73.refs_2_.refs_6_), channel_id=1, source_target_pairs={{0,8},{8,16},{16,24},{24,2},{2,10},{10,18},{18,26},{26,4},{4,12},{... | collective-permute-start | bytes 1769480 | tf_op jit(solution)/shard_map/ppermute | solution.py:782
  56.0 8.3 %collective-permute-start.5 = (f32[12,24,128]{2,1,0:T(8,128)}, f32[12,24,128]{2,1,0:T(8,128)S(1)}, u32[]{:S(2)}, u32[]{:S(2)}) collective-permute-start(f32[12,24,128]{2,1,0:T(8,128)} %shard_map.179.refs_9_), channel_id=1, source_target_pairs={{0,1},{1,0},{2,3},{3,2},{4,5},{5,4},{6,7},{7,6},{8,9},{9,8},{10,11... | collective-permute-start | bytes 442376 | tf_op jit(solution)/shard_map/ppermute | solution.py:791
  64.3 7.5 %copy-start.21 = (f32[24]{0:T(128)S(1)}, f32[24]{0:T(128)}, u32[]{:S(2)}) copy-start(f32[24]{0:T(128)} %refs_0_.13) | copy-start | bytes 292
  64.3 7.5 %copy-start.23 = (f32[24]{0:T(128)S(1)}, f32[24]{0:T(128)}, u32[]{:S(2)}) copy-start(f32[24]{0:T(128)} %refs_1_.9) | copy-start | bytes 292
  64.3 7.5 %copy-start.25 = (f32[24]{0:T(128)S(1)}, f32[24]{0:T(128)}, u32[]{:S(2)}) copy-start(f32[24]{0:T(128)} %refs_2_.7) | copy-start | bytes 292
  64.3 0.7 copy-start.14
  65.0 0.7 copy-start.19
  71.8 12.3 %copy-start.7 = (f32[2,16,16,128]{3,2,1,0:T(8,128)S(1)}, f32[2,16,16,128]{3,2,1,0:T(8,128)}, u32[]{:S(2)}) copy-start(f32[2,16,16,128]{3,2,1,0:T(8,128)} %copy-done.6) | copy-start | bytes 786436
  71.8 12.3 %copy-start.17 = (f32[2,16,128]{2,1,0:T(8,128)S(1)}, f32[2,16,128]{2,1,0:T(8,128)}, u32[]{:S(2)}) copy-start(f32[2,16,128]{2,1,0:T(8,128)} %copy-done.16) | copy-start | bytes 49156
  71.8 13.7 %copy-start.15 = (f32[1,1,4,128]{3,2,1,0:T(4,128)S(1)}, f32[1,1,4,128]{3,2,1,0:T(4,128)}, u32[]{:S(2)}) copy-start(f32[1,1,4,128]{3,2,1,0:T(4,128)} %param.20) | copy-start | bytes 6148
  71.8 13.6 %copy-start.20 = (f32[24]{0:T(128)S(1)}, f32[24]{0:T(128)}, u32[]{:S(2)}) copy-start(f32[24]{0:T(128)} %refs_0_.11) | copy-start | bytes 292
  75.1 16.4 %collective-permute-start.6 = (f32[24,2,16,128]{3,2,1,0:T(8,128)S(1)}, f32[24,2,16,128]{3,2,1,0:T(8,128)S(1)}, u32[]{:S(2)}, u32[]{:S(2)}) collective-permute-start(f32[24,2,16,128]{3,2,1,0:T(8,128)S(1)} %get-tuple-element.69.refs_1_.refs_5_), channel_id=1, source_target_pairs={{8,0},{16,8},{24,16},{2,24},{10,2},{18,10},{26,18},{4,26},{12,4},{... | collective-permute-start | bytes 1179656 | tf_op jit(solution)/shard_map/ppermute | solution.py:786
  76.4 16.7 %collective-permute-start.7 = (f32[24,2,16,128]{3,2,1,0:T(8,128)S(1)}, f32[24,2,16,128]{3,2,1,0:T(8,128)S(1)}, u32[]{:S(2)}, u32[]{:S(2)}) collective-permute-start(f32[24,2,16,128]{3,2,1,0:T(8,128)S(1)} %get-tuple-element.70.refs_2_.refs_6_), channel_id=1, source_target_pairs={{0,8},{8,16},{16,24},{24,2},{2,10},{10,18},{18,26},{26,4},{4,12},{... | collective-permute-start | bytes 1179656 | tf_op jit(solution)/shard_map/ppermute | solution.py:782
  84.0 1.4 %collective-permute-start.10 = (f32[12,24,128]{2,1,0:T(8,128)S(1)}, f32[12,24,128]{2,1,0:T(8,128)S(1)}, u32[]{:S(2)}, u32[]{:S(2)}) collective-permute-start(f32[12,24,128]{2,1,0:T(8,128)S(1)} %shard_map.184.refs_9_), channel_id=1, source_target_pairs={{0,1},{1,0},{2,3},{3,2},{4,5},{5,4},{6,7},{7,6},{8,9},{9,8},{10,11... | collective-permute-start | bytes 442376 | tf_op jit(solution)/shard_map/ppermute | solution.py:791
  94.1 3.4 %collective-permute-start.11 = (f32[12,16,128]{2,1,0:T(8,128)S(1)}, f32[12,16,128]{2,1,0:T(8,128)S(1)}, u32[]{:S(2)}, u32[]{:S(2)}) collective-permute-start(f32[12,16,128]{2,1,0:T(8,128)S(1)} %shard_map.186.refs_9_), channel_id=1, source_target_pairs={{0,1},{1,0},{2,3},{3,2},{4,5},{5,4},{6,7},{7,6},{8,9},{9,8},{10,11... | collective-permute-start | bytes 294920 | tf_op jit(solution)/shard_map/ppermute | solution.py:791
  94.2 12.5 %copy-start.22 = (f32[24]{0:T(128)S(1)}, f32[24]{0:T(128)}, u32[]{:S(2)}) copy-start(f32[24]{0:T(128)} %refs_0_.13) | copy-start | bytes 292
  94.2 12.5 %copy-start.24 = (f32[24]{0:T(128)S(1)}, f32[24]{0:T(128)}, u32[]{:S(2)}) copy-start(f32[24]{0:T(128)} %refs_1_.9) | copy-start | bytes 292
  94.2 12.5 %copy-start.26 = (f32[24]{0:T(128)S(1)}, f32[24]{0:T(128)}, u32[]{:S(2)}) copy-start(f32[24]{0:T(128)} %refs_2_.7) | copy-start | bytes 292
  97.5 14.2 %copy-start.5 = (f32[2,16,16,128]{3,2,1,0:T(8,128)S(1)}, f32[2,16,16,128]{3,2,1,0:T(8,128)}, u32[]{:S(2)}) copy-start(f32[2,16,16,128]{3,2,1,0:T(8,128)} %copy-done.4) | copy-start | bytes 786436
  97.5 14.2 %copy-start.10 = (s32[16,128]{1,0:T(8,128)S(1)}, s32[16,128]{1,0:T(8,128)}, u32[]{:S(2)}) copy-start(s32[16,128]{1,0:T(8,128)} %refs_0_.12) | copy-start | bytes 24580
  97.5 14.2 %copy-start.12 = (s32[16,128]{1,0:T(8,128)S(1)}, s32[16,128]{1,0:T(8,128)}, u32[]{:S(2)}) copy-start(s32[16,128]{1,0:T(8,128)} %refs_1_.8) | copy-start | bytes 24580
  101.7 10.0 %all-to-all-start.1 = ((f32[4,4,16,128]{3,2,1,0:T(8,128)}), f32[4,4,16,128]{3,2,1,0:T(8,128)S(1)}, u32[]{:S(2)}, u32[]{:S(2)}) async-start(f32[4,4,16,128]{3,2,1,0:T(8,128)} %get-tuple-element.83), calls=%async_computation.1 | async-start | bytes 262144 | tf_op jit(solution)/shard_map/all_to_all | solution.py:890
